TPU v7x, 32 devices: a whole 2x2x4 slice. The times are simulated.
32 devices in a mesh: groups: 2 (over x), dp: 16 (over z, y, core).
Axes of the slice: x: 2, y: 2, z: 4, core: 2. Of those that a mesh axis runs over, the one named last changes fastest.
Arguments:
- tokens: bfloat16 [32, 320, 1280], P(('groups', 'dp')), parts along dimension 0, may hold values from -6 to 6
- route: int32 [32, 320, 1], P(('groups', 'dp')), parts along dimension 0, may hold values from 0 to 3; in each aligned block of 320 rows (0 to 319, 320 to 639, ..., all dimensions but the last counted through in order) at most 124 rows name the same one
- labels: int32 [32], P(('groups', 'dp')), parts along dimension 0, may hold values from 0 to 15, each once
- moe_gain: float32 [1280], replicated, may hold values from 0.1 to 1.9
- router: bfloat16 [1280, 4], replicated, may hold values from -0.15625 to 0.15625
- w_in: bfloat16 [16, 1280, 1280], P('dp'), may hold values from -0.15625 to 0.15625
- w_out: bfloat16 [16, 1280, 1280], P('dp'), may hold values from -0.078125 to 0.078125
- out_gain: float32 [1280], replicated, may hold values from 0.1 to 1.9
- pool_query: float32 [2, 16, 80], replicated
- proj: bfloat16 [1280, 1280], replicated, may hold values from -0.15625 to 0.15625
- logit_scale: float32 [1], replicated
Outputs:
- mixed: bfloat16 [32, 320, 1280], P(('groups', 'dp')), parts along dimension 0
- d_pooled: float32 [32, 2, 1280], P(('groups', 'dp')), parts along dimension 0
- grad_proj: float32 [2560, 1280], P('groups'), parts along dimension 0
- loss: float32 [2], P('groups'), parts along dimension 0
There are 2 independent parts, one for each index of `groups`. A program takes and returns all parts, laid end to end along the dimension named above; an argument that names none is the same for every part. Nothing has to cross between parts.
Inputs may be any that keep to these rules, and one draw needn't show every extreme that they name: `route`: within the rows of one device no expert is named more than 124 times, and in some device one expert is named exactly 124 times. `labels`: A permutation of the pairs.
All inputs are finite; a program needn't handle non-finite values.
Results may differ from a plain program's by a relative error of at most 0.017.
The roundings to bfloat16 on the way count: a program that leaves them out, or rounds other values in their place, can miss the bound.
Values may be sent and summed in bfloat16 or wider, within the bound.
No kernel may reach another device: no remote copies, remote signals or barrier semaphores. Data moves between devices by JAX's collectives and lax.ppermute only.
A program may use at most 128 MiB of HBM per device.

v0:
```python
import math

import jax
import jax.numpy as jnp
from jax import lax
from jax.sharding import PartitionSpec as P

HEADS = 16
IMG_TOK = 256
SPLIT = 4
HEAD_DIM = 80


def layer_norm(values, gain):
    mean = jnp.mean(values, axis=-1, keepdims=True)
    centered = values - mean
    var = jnp.mean(centered * centered, axis=-1, keepdims=True)
    return centered * lax.rsqrt(var + 1e-06) * gain


def pool(mixed, out_gain, pool_query):
    z_all = layer_norm(mixed.astype(jnp.float32), out_gain)
    count, length, width = z_all.shape
    z_all = z_all.reshape(count, length, HEADS, HEAD_DIM)
    result = []
    for modal, (lower, upper) in enumerate(((0, IMG_TOK), (IMG_TOK, length))):
        piece = z_all[:, lower:upper]
        scores = jnp.einsum(
            "pthd,hd->pht", piece, pool_query[modal], precision=lax.Precision.HIGHEST
        ) / math.sqrt(HEAD_DIM)
        scores = scores - jnp.max(scores, axis=-1, keepdims=True)
        weights = jnp.exp(scores)
        weights = weights / jnp.sum(weights, axis=-1, keepdims=True)
        summed = jnp.einsum("pht,pthd->phd", weights, piece, precision=lax.Precision.HIGHEST)
        result.append(summed.reshape(count, width))
    return jnp.stack(result, axis=1).astype(jnp.bfloat16)


def contrast(emb, labels, logit_scale):
    count = emb.shape[0]
    norm = jnp.sqrt(jnp.sum(emb * emb, axis=-1) + 1e-06)
    unit = emb / norm[..., None]
    logits = logit_scale[0] * jnp.dot(unit[:, 0], unit[:, 1].T, precision=lax.Precision.HIGHEST)
    target = (labels[:, None] == jnp.arange(count, dtype=jnp.int32)[None, :]).astype(jnp.float32)
    row_top = jnp.max(logits, axis=1, keepdims=True)
    row_exp = jnp.exp(logits - row_top)
    row_total = jnp.sum(row_exp, axis=1, keepdims=True)
    row_lse = jnp.log(row_total) + row_top
    col_top = jnp.max(logits, axis=0, keepdims=True)
    col_exp = jnp.exp(logits - col_top)
    col_total = jnp.sum(col_exp, axis=0, keepdims=True)
    col_lse = jnp.log(col_total) + col_top
    matched = jnp.sum(logits * target)
    loss = (jnp.sum(row_lse) + jnp.sum(col_lse) - 2.0 * matched) / (2.0 * count)
    grad = (
        logit_scale[0] * (row_exp / row_total + col_exp / col_total - 2.0 * target) / (2.0 * count)
    )
    d_image = jnp.dot(grad, unit[:, 1], precision=lax.Precision.HIGHEST)
    d_text = jnp.dot(grad.T, unit[:, 0], precision=lax.Precision.HIGHEST)
    d_unit = jnp.stack([d_image, d_text], axis=1)
    d_emb = (d_unit - unit * jnp.sum(unit * d_unit, axis=-1, keepdims=True)) / norm[..., None]
    return (loss.reshape(1), d_emb)


def on_device(
    tokens, route, labels, moe_gain, router, w_in, w_out, out_gain, pool_query, proj, logit_scale
):
    count, length, width = tokens.shape
    rows = count * length
    devices = lax.axis_size("dp")
    experts = devices // SPLIT
    capacity = SPLIT * (3 * rows // (8 * experts) + 1)
    normed = (
        layer_norm(tokens.astype(jnp.float32), moe_gain).astype(jnp.bfloat16).reshape(rows, width)
    )
    ids = route.reshape(rows)
    onehot = (ids[:, None] == jnp.arange(experts, dtype=jnp.int32)[None, :]).astype(jnp.int32)
    slot = jnp.sum((jnp.cumsum(onehot, axis=0) - 1) * onehot, axis=1)
    place = ids * capacity + slot
    select = (place[:, None] == jnp.arange(experts * capacity, dtype=jnp.int32)[None, :]).astype(
        jnp.bfloat16
    )
    buffer = jnp.einsum("tc,td->cd", select, normed, preferred_element_type=jnp.float32).astype(
        jnp.bfloat16
    )
    copies = jnp.broadcast_to(
        buffer.reshape(experts, 1, capacity, width), (experts, SPLIT, capacity, width)
    )
    sending = copies.reshape(devices, capacity, width)
    hidden = jax.nn.gelu(
        jnp.dot(
            lax.all_to_all(sending, "dp", split_axis=0, concat_axis=0, tiled=True),
            w_in[0],
            preferred_element_type=jnp.float32,
        )
    ).astype(jnp.bfloat16)
    partial_value = jnp.dot(hidden, w_out[0], preferred_element_type=jnp.float32).astype(
        jnp.bfloat16
    )
    back = lax.all_to_all(partial_value, "dp", split_axis=0, concat_axis=0, tiled=True)
    sums = jnp.sum(back.reshape(experts, SPLIT, capacity, width).astype(jnp.float32), axis=1)
    summed = sums.reshape(experts * capacity, width)
    expert_out = jnp.take(summed, place, axis=0)
    router_logits = jnp.dot(normed, router, preferred_element_type=jnp.float32)
    gate = jax.nn.sigmoid(jnp.sum(router_logits * onehot.astype(jnp.float32), axis=-1))
    mixed = (
        tokens.astype(jnp.float32) + (gate[:, None] * expert_out).reshape(count, length, width)
    ).astype(jnp.bfloat16)
    pooled = pool(mixed, out_gain, pool_query)
    start = lax.axis_index("dp") * count
    emb = jnp.dot(pooled.reshape(-1, width), proj, preferred_element_type=jnp.float32).reshape(
        count, 2, width
    )
    emb_all, labels_all = (
        lax.all_gather(emb, "dp", axis=0, tiled=True),
        lax.all_gather(labels, "dp", axis=0, tiled=True),
    )
    loss, d_emb_all = contrast(emb_all, labels_all, logit_scale)
    d_emb = lax.dynamic_slice_in_dim(d_emb_all, start, count, 0)
    local_grad = jnp.dot(
        pooled.reshape(-1, width).astype(jnp.float32).T,
        d_emb.reshape(-1, width),
        precision=lax.Precision.HIGHEST,
    )
    grad_proj = lax.psum(local_grad, "dp")
    d_pooled = jnp.dot(
        d_emb.reshape(-1, width), proj.astype(jnp.float32).T, precision=lax.Precision.HIGHEST
    ).reshape(count, 2, width)
    return (mixed, d_pooled, grad_proj, loss)


def solution(mesh):
    placed = (
        P(("groups", "dp"), None, None),
        P(("groups", "dp"), None, None),
        P(("groups", "dp")),
        P(),
        P(),
        P("dp", None, None),
        P("dp", None, None),
        P(),
        P(),
        P(),
        P(),
    )
    return jax.shard_map(
        on_device,
        mesh=mesh,
        in_specs=placed,
        out_specs=(
            P(("groups", "dp"), None, None),
            P(("groups", "dp"), None, None),
            P("groups", None),
            P("groups"),
        ),
        check_vma=False,
    )
```

profile of v0, /device:TPU:0, one launch (start us, length us, event | category | flops | bytes accessed | tf_op | source)
XLA Modules:
  0.0 499.9 jit_solution(1429135940510245432)
XLA Ops:
  7.2 0.0 copy-start
  7.2 0.9 reduce.14
  8.0 1.5 convert_reduce_fusion.1
  9.5 1.5 fusion.14
  11.1 1.2 reduce-window.6
  12.3 0.2 slice_reduce_fusion
  12.5 0.2 reduce-window.9
  12.7 0.1 add_bitcast_fusion
  12.8 3.2 convolution_convert_fusion.1
  16.1 2.3 broadcast_in_dim.15
  18.3 1.9 broadcast_in_dim.16
  20.2 122.0 %all_to_all.10 = bf16[16,124,1280]{2,1,0:T(8,128)(2,1)} all-to-all(bf16[16,124,1280]{2,1,0:T(8,128)(2,1)S(1)} %bitcast.114), channel_id=1, replica_groups=mesh['groups'=2,'dp'=16] {'dp'}, dimensions={0} | all-to-all | bytes 10158080 | tf_op jit(solution)/shard_map/all_to_all | solution.py:92
  142.2 0.0 copy-done
  142.2 18.5 %convolution_convert_fusion = bf16[16,124,1280]{2,1,0:T(8,128)(2,1)} fusion(bf16[1,1280,1280]{2,1,0:T(8,128)(2,1)S(1)} %copy-done, bf16[16,124,1280]{2,1,0:T(8,128)(2,1)} %all_to_all.10, bf16[1,1280,1280]{2,1,0:T(8,128)(2,1)} %param.16), kind=kOutput, calls=%fused_computation.11 | convolution fusion | flops 13027737600 | bytes 16711680 | tf_op jit(solution)/shard_map/dot_general | solution.py:97
  160.7 0.0 copy-start.6
  160.7 0.0 copy-start.2
  160.8 5.6 %all-to-all-start.1 = ((bf16[16,124,1280]{2,1,0:T(8,128)(2,1)}), bf16[16,124,1280]{2,1,0:T(8,128)(2,1)}, u32[]{:S(2)}, u32[]{:S(2)}) async-start(bf16[16,124,1280]{2,1,0:T(8,128)(2,1)} %convolution_convert_fusion), calls=%async_computation.1 | async-start | bytes 10485760 | tf_op jit(solution)/shard_map/all_to_all | solution.py:100
  166.3 0.0 all-reduce.4.cloned.1.call-start
  167.0 0.0 copy-done.7
  167.0 0.6 dynamic-slice
  167.6 0.8 dynamic-update-slice
  168.4 114.6 %all-reduce.1 = s32[16]{0:T(128)S(1)} all-reduce(s32[16]{0:T(128)S(1)} %dynamic-update-slice), channel_id=1, replica_groups=mesh['groups'=2,'dp'=16] {'dp'}, use_global_device_ids=true, to_apply=%add.1 | all-reduce | flops 16 | bytes 128
  283.7 1.6 fusion.25
  285.3 0.0 all-to-all-done.1
  285.3 5.0 %convert_reduce_fusion = f32[4,124,1280]{2,1,0:T(8,128)} fusion(bf16[16,124,1280]{2,1,0:T(8,128)(2,1)} %all-to-all-done.1), kind=kLoop, calls=%fused_computation.10 | loop fusion | flops 4444160 | bytes 7618560 | tf_op jit(solution)/shard_map/reduce_sum | solution.py:101
  290.4 2.9 reshape.280
  293.3 5.4 %gather_fusion = f32[320,1280]{1,0:T(8,128)} fusion(f32[496,1280]{1,0:T(8,128)} %reshape.280, s32[1024]{0:T(1024)S(1)} %pad_clamp_fusion), kind=kCustom, calls=%fused_computation | custom fusion | bytes 3278080 | tf_op jit(solution)/shard_map/jit(_take)/gather | solution.py:103
  298.7 2.1 convert_reduce_fusion.2
  300.8 0.0 copy-start.1
  300.9 0.4 fusion.17
  301.2 0.5 copy-done.1
  301.7 1.5 fusion.18
  303.2 2.8 copy.29
  306.0 1.7 fusion.28
  307.7 0.1 multiply_reduce_fusion.1
  307.9 0.2 fusion.46
  308.1 0.1 fusion.45
  308.1 2.2 fusion.27
  310.4 0.1 stack.17
  310.5 2.1 fusion.22
  312.6 0.1 fusion.34
  312.7 0.2 fusion.33
  312.9 0.1 divide_bitcast_fusion
  313.0 2.5 fusion.21
  315.5 0.1 stack.16
  315.6 2.5 convolution_bitcast_fusion.3
  318.0 19.8 %all-gather.1 = f32[16,2,1280]{2,1,0:T(2,128)S(1)} all-gather(f32[1,2,1280]{2,1,0:T(2,128)S(1)} %convolution_bitcast_fusion.3), channel_id=2, replica_groups=mesh['groups'=2,'dp'=16] {'dp'}, dimensions={0}, use_global_device_ids=true | all-gather | bytes 174080 | tf_op jit(solution)/shard_map/all_gather | solution.py:115
  337.8 0.1 multiply_reduce_fusion
  338.0 0.1 copy.30
  338.1 0.1 copy_divide_fusion
  338.2 0.1 constant_dynamic-slice_fusion
  338.3 0.3 fusion.56
  338.6 0.7 select_reduce_fusion
  339.3 0.4 convolution_bitcast_fusion
  339.6 0.3 convolution_bitcast_fusion.1
  339.9 0.2 fusion.31
  340.1 0.1 constant_dynamic-slice_fusion.1
  340.2 0.1 fusion.40
  340.3 4.7 fusion.37
  345.0 0.0 all-reduce.4.cloned.1.call-update
  345.7 0.6 add_reduce_fusion
  347.6 5.5 %convolution_bitcast_fusion.2 = f32[1,2,1280]{2,1,0:T(2,128)} fusion(bf16[1280,1280]{1,0:T(8,128)(2,1)} %param.20, f32[1,2,1280]{2,0,1:T(1,128)S(1)} %fusion.40), kind=kOutput, calls=%fused_computation.20 | convolution fusion | flops 39321600 | bytes 3297280 | tf_op jit(solution)/shard_map/dot_general | solution.py:126
  353.1 132.8 %all-reduce.4.cloned.1.call-done = f32[1280,1280]{1,0:T(8,128)} async-done(((f32[1280,1280]{1,0:T(8,128)}), f32[1280,1280]{1,0:T(8,128)}) %all-reduce.4.cloned.1.call-update) | async-done | bytes 6553616 | tf_op jit(solution)/shard_map/psum | solution.py:125
  485.9 6.1 %copy.68 = f32[1280,1280]{1,0:T(8,128)} copy(f32[1280,1280]{1,0:T(8,128)} %all-reduce.4.cloned.1.call-done) | data formatting | bytes 13107200
  (27 shorter events, 0.2 us)
Async XLA Ops:
  7.2 135.0 %copy-start = (bf16[1,1280,1280]{2,1,0:T(8,128)(2,1)S(1)}, bf16[1,1280,1280]{2,1,0:T(8,128)(2,1)}, u32[]{:S(2)}) copy-start(bf16[1,1280,1280]{2,1,0:T(8,128)(2,1)} %param.17) | copy-start | bytes 9830404
  160.7 6.3 %copy-start.7 = (u32[32]{0:T(128)S(1)}, u32[32]{0:T(128)}, u32[]{:S(2)}) copy-start(u32[32]{0:T(128)} %constant.80) | copy-start | bytes 388
  160.7 122.9 %copy-start.4 = (s32[1,320,1]{1,2,0:T(1,128)S(1)}, s32[1,320,1]{1,2,0:T(1,128)}, u32[]{:S(2)}) copy-start(s32[1,320,1]{1,2,0:T(1,128)} %param.12) | copy-start | bytes 3844
  160.7 123.0 %copy-start.5 = (bf16[1280,4]{0,1:T(4,128)(2,1)S(1)}, bf16[1280,4]{0,1:T(4,128)(2,1)}, u32[]{:S(2)}) copy-start(bf16[1280,4]{0,1:T(4,128)(2,1)} %param.15) | copy-start | bytes 30724
  160.7 123.0 %copy-start.6 = (f32[1280]{0:T(1024)S(1)}, f32[1280]{0:T(1024)}, u32[]{:S(2)}) copy-start(f32[1280]{0:T(1024)} %param.14) | copy-start | bytes 15364
  160.7 124.6 %copy-start.2 = (f32[2,16,80]{2,1,0:T(8,128)S(1)}, f32[2,16,80]{2,1,0:T(8,128)}, u32[]{:S(2)}) copy-start(f32[2,16,80]{2,1,0:T(8,128)} %param.19) | copy-start | bytes 30724
  160.8 124.6 %all-to-all-start.1 = ((bf16[16,124,1280]{2,1,0:T(8,128)(2,1)}), bf16[16,124,1280]{2,1,0:T(8,128)(2,1)}, u32[]{:S(2)}, u32[]{:S(2)}) async-start(bf16[16,124,1280]{2,1,0:T(8,128)(2,1)} %convolution_convert_fusion), calls=%async_computation.1 | async-start | bytes 10485760 | tf_op jit(solution)/shard_map/all_to_all | solution.py:100
  166.3 319.5 %all-reduce.4.cloned.1.call-start = ((), (), s32[]{:S(2)}) async-start(), calls=%async_computation.2 | async-start | bytes 13107200 | tf_op jit(solution)/shard_map/psum | solution.py:125
  298.7 3.0 copy-start.3
  300.8 0.9 copy-start.1
Sparse Core Ops, SparseCore 0:
  345.1 140.6 all-reduce.3
where the time goes:
time: 501 us; the launch traced here: 500 us
  blocking collectives  256 us (51%)
  waiting for transfers between devices  133 us (27%)
  matrix products  45.6 us (9%)
  local copies, waits for them, and re-layouts  23.8 us (5%)
  between operations  18.7 us (4%)
  other arithmetic  17 us (3%)
  starting transfers between devices  5.61 us (1%)
    psum x1, waiting for transfers between devices, on_device(): grad_proj = lax.psum(local_grad, 'dp')  133 us
    all_to_all x1, blocking collectives, on_device(): lax.all_to_all(sending, 'dp', split_axis=0, concat_axis=0, tiled=True)  122 us
    unnamed x1, blocking collectives  115 us
    all_gather x1, blocking collectives, on_device(): lax.all_gather(emb, 'dp', axis=0, tiled=True)  19.8 us
    dot_general x1, matrix products, on_device(): jnp.dot(hidden, w_out[0], preferred_element_type=jnp.float32)  18.5 us
  transfers between devices with their start and end apart: 2, of which 1 were waited for; matrix products, arithmetic and copies ran while one was open for 2% of the time, Pallas kernels for 0%

commit v1 on v0

v1 whole, which is shorter than its diff:
```python
import functools
import math

import jax
import jax.numpy as jnp
from jax import lax
from jax.experimental import pallas as pl
from jax.experimental.pallas import tpu as pltpu
from jax.sharding import PartitionSpec as P

HEADS = 16
IMG_TOK = 256
SPLIT = 4
HEAD_DIM = 80
F32 = jnp.float32
BF16 = jnp.bfloat16
VMEM = pl.BlockSpec(memory_space=pltpu.VMEM)
SMEM = pl.BlockSpec(memory_space=pltpu.SMEM)


def iota(shape, dim):
    return lax.broadcasted_iota(jnp.int32, shape, dim)


def dot(a, b, contract=((1,), (0,)), precision=None):
    return lax.dot_general(
        a, b, (contract, ((), ())), precision=precision, preferred_element_type=F32
    )


def split3(values):
    high = values.astype(BF16)
    rest = values - high.astype(F32)
    middle = rest.astype(BF16)
    low = (rest - middle.astype(F32)).astype(BF16)
    return high, middle, low


def layer_norm(values, gain):
    mean = jnp.mean(values, axis=-1, keepdims=True)
    centered = values - mean
    var = jnp.mean(centered * centered, axis=-1, keepdims=True)
    return centered * lax.rsqrt(var + 1e-06) * gain


def dispatch_kernel(experts, cap, mine_ref, ids_ref, tokens_ref, *outs):
    chunks, place_ref = outs[:experts], outs[experts]
    rows = tokens_ref.shape[0]
    ids = ids_ref[...]
    onehot = (iota((experts, rows), 0) == ids).astype(F32)
    earlier = (iota((rows, rows), 0) <= iota((rows, rows), 1)).astype(F32).astype(BF16)
    count = dot(onehot.astype(BF16), earlier)
    slot = jnp.sum((count - 1.0) * onehot, axis=0, keepdims=True).astype(jnp.int32)
    place = (ids ^ mine_ref[0]) * cap + slot
    place_ref[...] = place
    select = (iota((experts * cap, rows), 0) == place).astype(F32).astype(BF16)
    buffer = dot(select, tokens_ref[...]).astype(BF16)
    for k in range(experts):
        chunks[k][...] = buffer[k * cap : (k + 1) * cap]


def ffn_kernel(mine_ref, own_ref, other_ref, gain_ref, router_ref, in_a, out_a, in_b, out_b, *outs):
    kept_ref, gate_ref, sent_ref, x_ref, hidden_ref = outs
    cap = own_ref.shape[0]
    block = 256
    gain = gain_ref[...]
    own = layer_norm(own_ref[...].astype(F32), gain).astype(BF16)
    x_ref[:cap] = own
    x_ref[cap:] = layer_norm(other_ref[...].astype(F32), gain).astype(BF16)
    ff, width = out_a.shape
    for index, w_in in enumerate((in_a, in_b)):
        for at in range(0, ff, block):
            pre = dot(x_ref[...], w_in[:, at : at + block])
            hidden_ref[index, :, at : at + block] = jax.nn.gelu(pre, approximate=True).astype(BF16)
    router = router_ref[...].astype(F32)
    column = jnp.where(iota(router.shape, 0) == mine_ref[0], router, 0.0)
    column = jnp.sum(column, axis=0, keepdims=True)
    gate_ref[...] = jax.nn.sigmoid(jnp.sum(own.astype(F32) * column, axis=1, keepdims=True))
    for at in range(0, width, block):
        total = None
        for index, w_out in enumerate((out_a, out_b)):
            part = dot(hidden_ref[index], w_out[:, at : at + block]).astype(BF16).astype(F32)
            total = part if total is None else total + part
        kept_ref[:, at : at + block] = total[:cap]
        sent_ref[:, at : at + block] = total[cap:].astype(BF16)


def finish_kernel(tokens_ref, gate_ref, kept_ref, got_ref, mixed_ref):
    total = kept_ref[...] + got_ref[...].astype(F32)
    mixed_ref[...] = (tokens_ref[...].astype(F32) + gate_ref[...] * total).astype(BF16)


def combine_kernel(experts, *refs):
    label_ref, parts, rest = refs[0], refs[1 : 1 + experts], refs[1 + experts :]
    place_ref, gain_ref, query_ref, mixed_ref, pooled_ref, buffer = rest
    cap = parts[0].shape[0]
    rows, width = mixed_ref.shape
    for k, part in enumerate(parts):
        buffer[k * cap : (k + 1) * cap] = part[...]
    select = (iota((experts * cap, rows), 0) == place_ref[...]).astype(F32).astype(BF16)
    mixed = dot(select, buffer[...], ((0,), (0,)))
    mixed_ref[...] = mixed.astype(BF16)
    z = layer_norm(mixed, gain_ref[...])
    head, feature = iota((width, HEADS), 1), iota((width, HEADS), 0)
    member = (feature >= head * HEAD_DIM) & (feature < (head + 1) * HEAD_DIM)
    member = member.astype(F32).astype(BF16)
    head, feature = iota((HEADS, width), 0), iota((HEADS, width), 1)
    spread = (feature >= head * HEAD_DIM) & (feature < (head + 1) * HEAD_DIM)
    spread = spread.astype(F32).astype(BF16)
    for modal, (lower, upper) in enumerate(((0, IMG_TOK), (IMG_TOK, rows))):
        piece = z[lower:upper]
        scores = sum(dot(term, member) for term in split3(piece * query_ref[modal : modal + 1]))
        scores = scores / math.sqrt(HEAD_DIM)
        weights = jnp.exp(scores - jnp.max(scores, axis=0, keepdims=True))
        weights = weights / jnp.sum(weights, axis=0, keepdims=True)
        wide = sum(dot(term, spread) for term in split3(weights))
        pooled_ref[modal : modal + 1] = jnp.sum(wide * piece, axis=0, keepdims=True).astype(BF16)
    pooled_ref[2:4] = jnp.full((2, width), label_ref[0], jnp.int32).astype(F32).astype(BF16)


def tail_kernel(pairs, mine_ref, scale_ref, all_ref, proj_ref, grad_ref, d_pooled_ref, loss_ref):
    exact = lax.Precision.HIGHEST
    me, scale = mine_ref[0], scale_ref[0]
    source = all_ref[...]
    row, col = iota((2 * pairs, 4 * pairs), 0), iota((2 * pairs, 4 * pairs), 1)
    wanted = jnp.where(row < pairs, (row ^ me) * 4, ((row - pairs) ^ me) * 4 + 1)
    pooled = dot((col == wanted).astype(F32).astype(BF16), source).astype(BF16)
    row, col = iota((pairs, 4 * pairs), 0), iota((pairs, 4 * pairs), 1)
    labels = dot((col == (row ^ me) * 4 + 2).astype(F32).astype(BF16), source[:, :128])[:, :1]
    emb = dot(pooled, proj_ref[...])
    norm = jnp.sqrt(jnp.sum(emb * emb, axis=-1, keepdims=True) + 1e-06)
    unit = emb / norm
    image, text = unit[:pairs], unit[pairs:]
    logits = scale * dot(image, text, ((1,), (1,)), exact)
    target = (labels == iota((pairs, pairs), 1).astype(F32)).astype(F32)
    row_top = jnp.max(logits, axis=1, keepdims=True)
    row_exp = jnp.exp(logits - row_top)
    row_total = jnp.sum(row_exp, axis=1, keepdims=True)
    row_lse = jnp.log(row_total) + row_top
    col_top = jnp.max(logits, axis=0, keepdims=True)
    col_exp = jnp.exp(logits - col_top)
    col_total = jnp.sum(col_exp, axis=0, keepdims=True)
    col_lse = jnp.log(col_total) + col_top
    matched = jnp.sum(jnp.sum(logits * target, axis=1, keepdims=True), axis=0, keepdims=True)
    total = jnp.sum(row_lse, axis=0, keepdims=True) + jnp.sum(col_lse, axis=1, keepdims=True)
    loss_ref[...] = (total - 2.0 * matched) / (2.0 * pairs)
    grad = scale * (row_exp / row_total + col_exp / col_total - 2.0 * target) / (2.0 * pairs)
    d_image = dot(grad, text, precision=exact)
    d_text = dot(grad, image, ((0,), (0,)), exact)
    d_unit = jnp.concatenate([d_image, d_text], axis=0)
    d_emb = (d_unit - unit * jnp.sum(unit * d_unit, axis=-1, keepdims=True)) / norm
    row = iota(d_emb.shape, 0)
    for modal in range(2):
        own = jnp.sum(jnp.where(row == me + modal * pairs, d_emb, 0.0), axis=0, keepdims=True)
        back = sum(dot(term, proj_ref[...], ((1,), (1,))) for term in split3(own))
        d_pooled_ref[modal : modal + 1] = back
    terms = jnp.concatenate(split3(d_emb), axis=0)
    thrice = jnp.concatenate([pooled] * 3, axis=0)
    block = 256
    for at in range(0, pooled.shape[1], block):
        grad_ref[at : at + block] = dot(thrice[:, at : at + block], terms, ((0,), (0,)))


def call(kernel, name, outs, specs, limit, scratch=()):
    return pl.pallas_call(
        kernel,
        out_shape=[jax.ShapeDtypeStruct(*o) for o in outs],
        in_specs=specs,
        out_specs=[VMEM] * len(outs),
        scratch_shapes=list(scratch),
        compiler_params=pltpu.CompilerParams(vmem_limit_bytes=limit * 1024 * 1024),
        cost_estimate=pl.CostEstimate(flops=0, bytes_accessed=0, transcendentals=0),
        name=name,
    )


def after(values, *others):
    return lax.optimization_barrier((values,) + others)[0]


def on_device(
    tokens, route, labels, moe_gain, router, w_in, w_out, out_gain, pool_query, proj, logit_scale
):
    count, length, width = tokens.shape
    rows = count * length
    devices = lax.axis_size("dp")
    experts = devices // SPLIT
    capacity = SPLIT * (3 * rows // (8 * experts) + 1)
    cap = -(-capacity // 16) * 16
    ff = w_in.shape[2]
    me = lax.axis_index("dp").astype(jnp.int32)
    mine = (me // SPLIT).reshape(1)

    def swap(values, bits):
        return lax.ppermute(values, "dp", [(i, i ^ bits) for i in range(devices)])

    weights = [w_in[0], w_out[0]]
    weights = weights + [swap(w, 1) for w in weights]
    *chunks, place = call(
        functools.partial(dispatch_kernel, experts, cap),
        "dispatch",
        [((cap, width), BF16)] * experts + [((1, rows), jnp.int32)],
        [SMEM] + [VMEM] * 2,
        8,
    )(mine, route.reshape(1, rows), tokens.reshape(rows, width))
    held = {k: swap(chunks[k], SPLIT * k) for k in range(1, min(experts, 3))}
    held[0] = chunks[0]
    parts = []
    for k in range(experts):
        if k > 2:
            held[k] = swap(after(chunks[k], held[k - 1], parts[0][2]), SPLIT * k)
        partner = swap(after(held[k], parts[(k - 1) // 2][2]) if k % 2 else held[k], 2)
        parts.append(
            call(
                ffn_kernel,
                "ffn",
                [((cap, width), F32), ((cap, 1), F32), ((cap, width), BF16)],
                [SMEM] + [VMEM] * 8,
                20,
                [pltpu.VMEM((2 * cap, width), BF16), pltpu.VMEM((2, 2 * cap, ff), BF16)],
            )(
                mine,
                held[k],
                after(partner, parts[-1][2]) if k else partner,
                moe_gain.reshape(1, width),
                router.T,
                *weights,
            )
        )
    ready, result = {}, parts[-1][2]
    for k in list(range(1, experts)) + [0]:
        kept, gate, leave = parts[k]
        got = swap(leave if k else after(leave, parts[-1][2]), 2)
        (result,) = call(finish_kernel, "finish", [((cap, width), BF16)], [VMEM] * 4, 4)(
            held[k], gate, after(kept, result), got
        )
        ready[k] = swap(result, SPLIT * k) if k else result
    mixed, pooled = call(
        functools.partial(combine_kernel, experts),
        "combine",
        [((rows, width), BF16), ((4, width), BF16)],
        [SMEM] + [VMEM] * (3 + experts),
        20,
        [pltpu.VMEM((experts * cap, width), BF16)],
    )(
        labels,
        *[ready[k] for k in range(experts)],
        place,
        out_gain.reshape(1, width),
        pool_query.reshape(2, width),
    )
    bits = 1
    while bits < devices:
        pooled = jnp.concatenate([pooled, swap(pooled, bits)], axis=0)
        bits = bits * 2
    grad_proj, d_pooled, loss = call(
        functools.partial(tail_kernel, devices),
        "contrast",
        [((width, width), F32), ((2, width), F32), ((1, 1), F32)],
        [SMEM] * 2 + [VMEM] * 2,
        24,
    )(me.reshape(1), logit_scale, pooled, proj)
    return (
        mixed.reshape(count, length, width),
        d_pooled.reshape(count, 2, width),
        grad_proj,
        loss.reshape(1),
    )


def solution(mesh):
    placed = (
        P(("groups", "dp"), None, None),
        P(("groups", "dp"), None, None),
        P(("groups", "dp")),
        P(),
        P(),
        P("dp", None, None),
        P("dp", None, None),
        P(),
        P(),
        P(),
        P(),
    )
    return jax.shard_map(
        on_device,
        mesh=mesh,
        in_specs=placed,
        out_specs=(
            P(("groups", "dp"), None, None),
            P(("groups", "dp"), None, None),
            P("groups", None),
            P("groups"),
        ),
        check_vma=False,
    )
```

time: 501 us -> 127 us (0.25)
  blocking collectives: 256 us -> 0 us
  waiting for transfers between devices: 133 us -> 31.6 us
  matrix products: 45.6 us -> 0 us
  Pallas kernels: 0 us -> 45 us
  starting transfers between devices: 5.61 us -> 37.1 us
  other arithmetic: 17 us -> 0.06 us
  between operations: 18.7 us -> 2.09 us
  local copies, waits for them, and re-layouts: 23.8 us -> 11 us
    psum x1 -> x0, waiting for transfers between devices: 133 us -> none  [on_device(): grad_proj = lax.psum(local_grad, 'dp')]
    all_to_all x1 -> x0, blocking collectives: 122 us -> none  [on_device(): lax.all_to_all(sending, 'dp', split_axis=0, concat_axis=0, tiled=True)]
    unnamed x1 -> x0, blocking collectives: 115 us -> none
    dot_general x13 -> x0, matrix products: 45.6 us -> none  [the longest x1 18.5 us: on_device(): jnp.dot(hidden, w_out[0], preferred_element_type=jnp.float32)]
    pallas_call x0 -> x11, Pallas kernels: none -> 45 us  [the longest x4 25.3 us: on_device(): call(ffn_kernel, 'ffn', [((cap, width), F32), ((cap, 1), F32), ((cap, wid...]
    ppermute x0 -> x20, starting transfers between devices: none -> 37.1 us  [swap(): return lax.ppermute(values, 'dp', [(i, i ^ bits) for i in range(devices)])]
    ppermute x0 -> x20, waiting for transfers between devices: none -> 31.6 us  [swap(): return lax.ppermute(values, 'dp', [(i, i ^ bits) for i in range(devices)])]
    all_gather x1 -> x0, blocking collectives: 19.8 us -> none  [on_device(): lax.all_gather(emb, 'dp', axis=0, tiled=True)]
  transfers between devices with their start and end apart: 2 -> 20, of which waited for: 1 -> 10; matrix products, arithmetic and copies ran while one was open for 2% -> 1% of each run, Pallas kernels for 0% -> 24%
where the time goes in v1:
time: 127 us
  Pallas kernels  45 us (35%)
  starting transfers between devices  37.1 us (29%)
  waiting for transfers between devices  31.6 us (25%)
  local copies, waits for them, and re-layouts  11 us (9%)
  between operations  2.09 us (2%)
    ppermute x20, starting transfers between devices, swap(): return lax.ppermute(values, 'dp', [(i, i ^ bits) for i in range(devices)])  37.1 us
    ppermute x20, waiting for transfers between devices, swap(): return lax.ppermute(values, 'dp', [(i, i ^ bits) for i in range(devices)])  31.6 us
    pallas_call x4, Pallas kernels, on_device(): call(ffn_kernel, 'ffn', [((cap, width), F32), ((cap, 1), F32), ((cap, wid...  25.3 us
    pallas_call x1, Pallas kernels, on_device(): call(functools.partial(tail_kernel, devices), 'contrast', [((width, width...  10.7 us
    unnamed x28, local copies, waits for them, and re-layouts  9.3 us
    pallas_call x1, Pallas kernels, on_device(): call(functools.partial(combine_kernel, experts), 'combine', [((rows, widt...  4.29 us
    pallas_call x4, Pallas kernels, on_device(): call(finish_kernel, 'finish', [((cap, width), BF16)], [VMEM] * 4, 4)  3.78 us
  transfers between devices with their start and end apart: 20, of which 10 were waited for; matrix products, arithmetic and copies ran while one was open for 1% of the time, Pallas kernels for 24%

profile of v1, /device:TPU:0, one launch (start us, length us, event | category | flops | bytes accessed | tf_op | source)
XLA Modules:
  0.0 126.8 jit_solution(5108436122012766679)
XLA Ops:
  0.6 0.5 collective-permute-start.1
  1.1 0.1 collective-permute-start.2
  1.2 1.1 copy-done.7
  2.4 0.7 copy-done.11
  3.1 1.0 dispatch.1
  4.1 0.0 copy-start.5
  4.1 3.0 %collective-permute-start = (bf16[128,1280]{1,0:T(8,128)(2,1)S(1)}, bf16[128,1280]{1,0:T(8,128)(2,1)S(1)}, u32[]{:S(2)}, u32[]{:S(2)}) collective-permute-start(bf16[128,1280]{1,0:T(8,128)(2,1)S(1)} %get-tuple-element.37.own_ref.tokens_ref), channel_id=1, source_target_pairs={{0,2},{1,3},{2,0},{3,1},{4,6},{5,7},{6,4},{7,5},{8,10},{9,11},{10,... | collective-permute-start | bytes 983048 | tf_op jit(solution)/shard_map/ppermute | solution.py:195
  7.1 1.6 %collective-permute-start.5 = (bf16[128,1280]{1,0:T(8,128)(2,1)S(1)}, bf16[128,1280]{1,0:T(8,128)(2,1)S(1)}, u32[]{:S(2)}, u32[]{:S(2)}) collective-permute-start(bf16[128,1280]{1,0:T(8,128)(2,1)S(1)} %get-tuple-element.44), channel_id=1, source_target_pairs={{0,4},{1,5},{2,6},{3,7},{4,0},{5,1},{6,2},{7,3},{8,12},{9,13},{10,... | collective-permute-start | bytes 983048 | tf_op jit(solution)/shard_map/ppermute | solution.py:195
  8.6 2.6 %collective-permute-start.3 = (bf16[128,1280]{1,0:T(8,128)(2,1)S(1)}, bf16[128,1280]{1,0:T(8,128)(2,1)S(1)}, u32[]{:S(2)}, u32[]{:S(2)}) collective-permute-start(bf16[128,1280]{1,0:T(8,128)(2,1)S(1)} %get-tuple-element.41), channel_id=1, source_target_pairs={{0,8},{1,9},{2,10},{3,11},{4,12},{5,13},{6,14},{7,15},{8,0},{9,1},... | collective-permute-start | bytes 983048 | tf_op jit(solution)/shard_map/ppermute | solution.py:195
  11.2 0.7 reshape.44.gain_ref
  11.9 3.1 %collective-permute-done.other_ref = bf16[128,1280]{1,0:T(8,128)(2,1)S(1)} collective-permute-done((bf16[128,1280]{1,0:T(8,128)(2,1)S(1)}, bf16[128,1280]{1,0:T(8,128)(2,1)S(1)}, u32[]{:S(2)}, u32[]{:S(2)}) %collective-permute-start) | collective-permute-done | bytes 327712 | tf_op jit(solution)/shard_map/ppermute | solution.py:195
  15.0 0.0 collective-permute-done.1.in_b
  15.0 0.0 collective-permute-done.2.out_b
  15.0 1.9 %copy-done = bf16[1,1280,1280]{2,1,0:T(8,128)(2,1)S(1)} copy-done((bf16[1,1280,1280]{2,1,0:T(8,128)(2,1)S(1)}, bf16[1,1280,1280]{2,1,0:T(8,128)(2,1)}, u32[]{:S(2)}) %copy-start) | copy-done | bytes 3276824
  17.0 1.9 %copy-done.2 = bf16[1,1280,1280]{2,1,0:T(8,128)(2,1)S(1)} copy-done((bf16[1,1280,1280]{2,1,0:T(8,128)(2,1)S(1)}, bf16[1,1280,1280]{2,1,0:T(8,128)(2,1)}, u32[]{:S(2)}) %copy-start.2) | copy-done | bytes 3276824
  18.9 0.7 copy-done.10
  19.6 6.9 %ffn.4 = (f32[128,1280]{1,0:T(8,128)S(1)}, f32[128,1]{1,0:T(8,128)S(1)}, bf16[128,1280]{1,0:T(8,128)(2,1)}) custom-call(s32[1]{0:T(128)} %bitcast.mine_ref, bf16[128,1280]{1,0:T(8,128)(2,1)S(1)} %get-tuple-element.37.own_ref.tokens_ref, bf16[128,1280]{1,0:T(8,128)(2,1)S(1)} %collective-permute-done.other_ref, f32[1,1280]{1,0:T(1,128)S(1)} %reshape.44.gain_ref, ...), custom_call_target="tpu_custom_call" | custom-call | tf_op jit(solution)/shard_map/ffn/pallas_call | solution.py:214
  26.5 0.8 copy-done.8
  27.4 0.0 collective-permute-done.5.own_ref.tokens_ref
  27.4 1.7 %collective-permute-start.6 = (bf16[128,1280]{1,0:T(8,128)(2,1)S(1)}, bf16[128,1280]{1,0:T(8,128)(2,1)S(1)}, u32[]{:S(2)}, u32[]{:S(2)}) collective-permute-start(bf16[128,1280]{1,0:T(8,128)(2,1)S(1)} %collective-permute-done.5.own_ref.tokens_ref), channel_id=1, source_target_pairs={{0,2},{1,3},{2,0},{3,1},{4,6},{5,7},{6,4},{7,5},{8,10},{9,11},{10,... | collective-permute-start | bytes 983048 | tf_op jit(solution)/shard_map/ppermute | solution.py:195
  29.1 0.0 collective-permute-done.3.own_ref.tokens_ref
  29.1 3.6 %collective-permute-start.4 = (bf16[128,1280]{1,0:T(8,128)(2,1)S(1)}, bf16[128,1280]{1,0:T(8,128)(2,1)S(1)}, u32[]{:S(2)}, u32[]{:S(2)}) collective-permute-start(bf16[128,1280]{1,0:T(8,128)(2,1)S(1)} %get-tuple-element.43), channel_id=1, source_target_pairs={{0,12},{1,13},{2,14},{3,15},{4,8},{5,9},{6,10},{7,11},{8,4},{9,5},... | collective-permute-start | bytes 983048 | tf_op jit(solution)/shard_map/ppermute | solution.py:195
  32.7 0.5 collective-permute-start.8
  33.2 4.8 %collective-permute-done.6.other_ref = bf16[128,1280]{1,0:T(8,128)(2,1)S(1)} collective-permute-done((bf16[128,1280]{1,0:T(8,128)(2,1)S(1)}, bf16[128,1280]{1,0:T(8,128)(2,1)S(1)}, u32[]{:S(2)}, u32[]{:S(2)}) %collective-permute-start.6) | collective-permute-done | bytes 327712 | tf_op jit(solution)/shard_map/ppermute | solution.py:195
  38.0 6.1 %ffn.5 = (f32[128,1280]{1,0:T(8,128)S(1)}, f32[128,1]{1,0:T(8,128)S(1)}, bf16[128,1280]{1,0:T(8,128)(2,1)S(1)}) custom-call(s32[1]{0:T(128)} %bitcast.mine_ref, bf16[128,1280]{1,0:T(8,128)(2,1)S(1)} %collective-permute-done.5.own_ref.tokens_ref, bf16[128,1280]{1,0:T(8,128)(2,1)S(1)} %collective-permute-done.6.other_ref, f32[1,1280]{1,0:T(1,128)S(1)} %reshape.44.gain_ref, ...), custom_call_target="tpu_custom_call" | custom-call | tf_op jit(solution)/shard_map/ffn/pallas_call | solution.py:214
  44.1 0.0 collective-permute-done.4.own_ref.tokens_ref
  44.1 1.8 %collective-permute-start.7 = (bf16[128,1280]{1,0:T(8,128)(2,1)S(1)}, bf16[128,1280]{1,0:T(8,128)(2,1)S(1)}, u32[]{:S(2)}, u32[]{:S(2)}) collective-permute-start(bf16[128,1280]{1,0:T(8,128)(2,1)S(1)} %collective-permute-done.4.own_ref.tokens_ref), channel_id=1, source_target_pairs={{0,2},{1,3},{2,0},{3,1},{4,6},{5,7},{6,4},{7,5},{8,10},{9,11},{10,... | collective-permute-start | bytes 983048 | tf_op jit(solution)/shard_map/ppermute | solution.py:195
  45.9 0.3 collective-permute-start.9
  46.2 0.0 collective-permute-done.8.other_ref
  46.2 6.0 %ffn.6 = (f32[128,1280]{1,0:T(8,128)S(1)}, f32[128,1]{1,0:T(8,128)S(1)}, bf16[128,1280]{1,0:T(8,128)(2,1)S(1)}) custom-call(s32[1]{0:T(128)} %bitcast.mine_ref, bf16[128,1280]{1,0:T(8,128)(2,1)S(1)} %collective-permute-done.3.own_ref.tokens_ref, bf16[128,1280]{1,0:T(8,128)(2,1)S(1)} %collective-permute-done.8.other_ref, f32[1,1280]{1,0:T(1,128)S(1)} %reshape.44.gain_ref, ...), custom_call_target="tpu_custom_call" | custom-call | tf_op jit(solution)/shard_map/ffn/pallas_call | solution.py:214
  52.2 1.8 %collective-permute-start.10 = (bf16[128,1280]{1,0:T(8,128)(2,1)S(1)}, bf16[128,1280]{1,0:T(8,128)(2,1)S(1)}, u32[]{:S(2)}, u32[]{:S(2)}) collective-permute-start(bf16[128,1280]{1,0:T(8,128)(2,1)S(1)} %get-tuple-element.50), channel_id=1, source_target_pairs={{0,2},{1,3},{2,0},{3,1},{4,6},{5,7},{6,4},{7,5},{8,10},{9,11},{10,... | collective-permute-start | bytes 983048 | tf_op jit(solution)/shard_map/ppermute | solution.py:195
  54.0 0.7 collective-permute-done.7.other_ref
  54.8 6.2 %ffn.7 = (f32[128,1280]{1,0:T(8,128)S(1)}, f32[128,1]{1,0:T(8,128)S(1)}, bf16[128,1280]{1,0:T(8,128)(2,1)S(1)}) custom-call(s32[1]{0:T(128)} %bitcast.mine_ref, bf16[128,1280]{1,0:T(8,128)(2,1)S(1)} %collective-permute-done.4.own_ref.tokens_ref, bf16[128,1280]{1,0:T(8,128)(2,1)S(1)} %collective-permute-done.7.other_ref, f32[1,1280]{1,0:T(1,128)S(1)} %reshape.44.gain_ref, ...), custom_call_target="tpu_custom_call" | custom-call | tf_op jit(solution)/shard_map/ffn/pallas_call | solution.py:214
  61.0 0.0 copy-start.12
  61.1 0.0 copy-start.13
  61.1 1.8 %collective-permute-start.11 = (bf16[128,1280]{1,0:T(8,128)(2,1)S(1)}, bf16[128,1280]{1,0:T(8,128)(2,1)S(1)}, u32[]{:S(2)}, u32[]{:S(2)}) collective-permute-start(bf16[128,1280]{1,0:T(8,128)(2,1)S(1)} %get-tuple-element.58), channel_id=1, source_target_pairs={{0,2},{1,3},{2,0},{3,1},{4,6},{5,7},{6,4},{7,5},{8,10},{9,11},{10,... | collective-permute-start | bytes 983048 | tf_op jit(solution)/shard_map/ppermute | solution.py:195
  62.9 0.3 collective-permute-start.12
  63.2 0.0 collective-permute-done.9.got_ref
  63.2 0.9 finish.4
  64.1 2.1 %collective-permute-start.13 = (bf16[128,1280]{1,0:T(8,128)(2,1)}, bf16[128,1280]{1,0:T(8,128)(2,1)}, u32[]{:S(2)}, u32[]{:S(2)}) collective-permute-start(bf16[128,1280]{1,0:T(8,128)(2,1)} %finish.4), channel_id=1, source_target_pairs={{0,4},{1,5},{2,6},{3,7},{4,0},{5,1},{6,2},{7,3},{8,12},{9,13},{10,... | collective-permute-start | bytes 983048 | tf_op jit(solution)/shard_map/ppermute | solution.py:195
  66.2 2.6 %collective-permute-done.10.got_ref = bf16[128,1280]{1,0:T(8,128)(2,1)S(1)} collective-permute-done((bf16[128,1280]{1,0:T(8,128)(2,1)S(1)}, bf16[128,1280]{1,0:T(8,128)(2,1)S(1)}, u32[]{:S(2)}, u32[]{:S(2)}) %collective-permute-start.10) | collective-permute-done | bytes 327712 | tf_op jit(solution)/shard_map/ppermute | solution.py:195
  68.8 0.9 finish.5
  69.7 3.1 %collective-permute-start.14 = (bf16[128,1280]{1,0:T(8,128)(2,1)}, bf16[128,1280]{1,0:T(8,128)(2,1)}, u32[]{:S(2)}, u32[]{:S(2)}) collective-permute-start(bf16[128,1280]{1,0:T(8,128)(2,1)} %finish.5), channel_id=1, source_target_pairs={{0,8},{1,9},{2,10},{3,11},{4,12},{5,13},{6,14},{7,15},{8,0},{9,1},... | collective-permute-start | bytes 983048 | tf_op jit(solution)/shard_map/ppermute | solution.py:195
  72.9 2.6 %collective-permute-done.11.got_ref = bf16[128,1280]{1,0:T(8,128)(2,1)S(1)} collective-permute-done((bf16[128,1280]{1,0:T(8,128)(2,1)S(1)}, bf16[128,1280]{1,0:T(8,128)(2,1)S(1)}, u32[]{:S(2)}, u32[]{:S(2)}) %collective-permute-start.11) | collective-permute-done | bytes 327712 | tf_op jit(solution)/shard_map/ppermute | solution.py:195
  75.5 0.9 finish.6
  76.4 3.2 %collective-permute-start.15 = (bf16[128,1280]{1,0:T(8,128)(2,1)}, bf16[128,1280]{1,0:T(8,128)(2,1)}, u32[]{:S(2)}, u32[]{:S(2)}) collective-permute-start(bf16[128,1280]{1,0:T(8,128)(2,1)} %finish.6), channel_id=1, source_target_pairs={{0,12},{1,13},{2,14},{3,15},{4,8},{5,9},{6,10},{7,11},{8,4},{9,5},... | collective-permute-start | bytes 983048 | tf_op jit(solution)/shard_map/ppermute | solution.py:195
  79.6 0.1 reshape.46.refs_7_
  80.3 0.0 collective-permute-done.12.got_ref
  80.3 0.0 copy-start.6
  80.3 1.0 copy-done.6
  81.3 1.1 copy-done.9
  82.4 1.1 finish.7.refs_1_
  83.5 9.5 %collective-permute-done.14.refs_3_ = bf16[128,1280]{1,0:T(8,128)(2,1)} collective-permute-done((bf16[128,1280]{1,0:T(8,128)(2,1)}, bf16[128,1280]{1,0:T(8,128)(2,1)}, u32[]{:S(2)}, u32[]{:S(2)}) %collective-permute-start.14) | collective-permute-done | bytes 327712 | tf_op jit(solution)/shard_map/ppermute | solution.py:195
  93.1 4.3 %combine.1 = (bf16[320,1280]{1,0:T(8,128)(2,1)}, bf16[4,1280]{1,0:T(4,128)(2,1)S(1)}) custom-call(s32[1]{0:T(128)S(6)} %copy.15.refs_0_, bf16[128,1280]{1,0:T(8,128)(2,1)S(1)} %finish.7.refs_1_, bf16[128,1280]{1,0:T(8,128)(2,1)} %collective-permute-done.13.refs_2_, bf16[128,1280]{1,0:T(8,128)(2,1)} %collective-permute-done.14.refs_3_, ...), custom_call_target="tpu_custom_call" | custom-call | tf_op jit(solution)/shard_map/combine/pallas_call | solution.py:238
  97.3 0.1 collective-permute-start.16
  97.4 1.2 collective-permute-done.16
  98.6 1.0 collective-permute-start.17
  99.6 2.9 %collective-permute-done.17 = bf16[8,1280]{1,0:T(8,128)(2,1)S(1)} collective-permute-done((bf16[8,1280]{1,0:T(8,128)(2,1)S(1)}, bf16[8,1280]{1,0:T(8,128)(2,1)S(1)}, u32[]{:S(2)}, u32[]{:S(2)}) %collective-permute-start.17) | collective-permute-done | bytes 20512 | tf_op jit(solution)/shard_map/ppermute | solution.py:195
  102.5 5.2 %collective-permute-start.18 = (bf16[16,1280]{1,0:T(8,128)(2,1)S(1)}, bf16[16,1280]{1,0:T(8,128)(2,1)S(1)}, u32[]{:S(2)}, u32[]{:S(2)}) collective-permute-start(bf16[16,1280]{1,0:T(8,128)(2,1)S(1)} %pad_maximum_fusion.1), channel_id=1, source_target_pairs={{0,4},{1,5},{2,6},{3,7},{4,0},{5,1},{6,2},{7,3},{8,12},{9,13},{10,... | collective-permute-start | bytes 122888 | tf_op jit(solution)/shard_map/ppermute | solution.py:195
  107.7 2.0 %collective-permute-done.18 = bf16[16,1280]{1,0:T(8,128)(2,1)S(1)} collective-permute-done((bf16[16,1280]{1,0:T(8,128)(2,1)S(1)}, bf16[16,1280]{1,0:T(8,128)(2,1)S(1)}, u32[]{:S(2)}, u32[]{:S(2)}) %collective-permute-start.18) | collective-permute-done | bytes 40992 | tf_op jit(solution)/shard_map/ppermute | solution.py:195
  109.7 2.7 %collective-permute-start.19 = (bf16[32,1280]{1,0:T(8,128)(2,1)S(1)}, bf16[32,1280]{1,0:T(8,128)(2,1)}, u32[]{:S(2)}, u32[]{:S(2)}) collective-permute-start(bf16[32,1280]{1,0:T(8,128)(2,1)S(1)} %pad_maximum_fusion), channel_id=1, source_target_pairs={{0,8},{1,9},{2,10},{3,11},{4,12},{5,13},{6,14},{7,15},{8,0},{9,1},... | collective-permute-start | bytes 245768 | tf_op jit(solution)/shard_map/ppermute | solution.py:195
  113.1 2.1 %collective-permute-done.19 = bf16[32,1280]{1,0:T(8,128)(2,1)} collective-permute-done((bf16[32,1280]{1,0:T(8,128)(2,1)S(1)}, bf16[32,1280]{1,0:T(8,128)(2,1)}, u32[]{:S(2)}, u32[]{:S(2)}) %collective-permute-start.19) | collective-permute-done | bytes 81952 | tf_op jit(solution)/shard_map/ppermute | solution.py:195
  115.2 0.9 concatenate.18.all_ref
  116.1 10.7 %contrast.1 = (f32[1280,1280]{1,0:T(8,128)}, f32[2,1280]{1,0:T(2,128)}, f32[1,1]{1,0:T(1,128)}) custom-call(s32[1]{0:T(128)} %bitcast.7.mine_ref, f32[1]{0:T(128)S(6)} %copy.16.scale_ref, bf16[64,1280]{1,0:T(8,128)(2,1)S(1)} %concatenate.18.all_ref, bf16[1280,1280]{1,0:T(8,128)(2,1)S(1)} %copy-done.4), custom_call_target="tpu_custom_call" | custom-call | tf_op jit(solution)/shard_map/contrast/pallas_call | solution.py:256
  (22 shorter events, 0.1 us)
Async XLA Ops:
  0.6 14.4 %collective-permute-start.1 = (bf16[1280,1280]{1,0:T(8,128)(2,1)}, bf16[1280,1280]{1,0:T(8,128)(2,1)S(1)}, u32[]{:S(2)}, u32[]{:S(2)}) collective-permute-start(bf16[1280,1280]{1,0:T(8,128)(2,1)} %bitcast.10), channel_id=1, source_target_pairs={{0,1},{1,0},{2,3},{3,2},{4,5},{5,4},{6,7},{7,6},{8,9},{9,8},{10,11... | collective-permute-start | bytes 9830408 | tf_op jit(solution)/shard_map/ppermute | solution.py:195
  1.1 13.9 %collective-permute-start.2 = (bf16[1280,1280]{1,0:T(8,128)(2,1)}, bf16[1280,1280]{1,0:T(8,128)(2,1)}, u32[]{:S(2)}, u32[]{:S(2)}) collective-permute-start(bf16[1280,1280]{1,0:T(8,128)(2,1)} %bitcast.15), channel_id=1, source_target_pairs={{0,1},{1,0},{2,3},{3,2},{4,5},{5,4},{6,7},{7,6},{8,9},{9,8},{10,11... | collective-permute-start | bytes 9830408 | tf_op jit(solution)/shard_map/ppermute | solution.py:195
  1.2 1.1 copy-start.7
  2.4 0.7 copy-start.11
  4.1 22.5 %copy-start.5 = (bf16[128,1280]{1,0:T(8,128)(2,1)}, bf16[128,1280]{1,0:T(8,128)(2,1)S(1)}, u32[]{:S(2)}) copy-start(bf16[128,1280]{1,0:T(8,128)(2,1)S(1)} %get-tuple-element.37.own_ref.tokens_ref) | copy-start | bytes 983044
  4.1 11.0 %collective-permute-start = (bf16[128,1280]{1,0:T(8,128)(2,1)S(1)}, bf16[128,1280]{1,0:T(8,128)(2,1)S(1)}, u32[]{:S(2)}, u32[]{:S(2)}) collective-permute-start(bf16[128,1280]{1,0:T(8,128)(2,1)S(1)} %get-tuple-element.37.own_ref.tokens_ref), channel_id=1, source_target_pairs={{0,2},{1,3},{2,0},{3,1},{4,6},{5,7},{6,4},{7,5},{8,10},{9,11},{10,... | collective-permute-start | bytes 983048 | tf_op jit(solution)/shard_map/ppermute | solution.py:195
  7.1 20.3 %collective-permute-start.5 = (bf16[128,1280]{1,0:T(8,128)(2,1)S(1)}, bf16[128,1280]{1,0:T(8,128)(2,1)S(1)}, u32[]{:S(2)}, u32[]{:S(2)}) collective-permute-start(bf16[128,1280]{1,0:T(8,128)(2,1)S(1)} %get-tuple-element.44), channel_id=1, source_target_pairs={{0,4},{1,5},{2,6},{3,7},{4,0},{5,1},{6,2},{7,3},{8,12},{9,13},{10,... | collective-permute-start | bytes 983048 | tf_op jit(solution)/shard_map/ppermute | solution.py:195
  8.6 20.5 %collective-permute-start.3 = (bf16[128,1280]{1,0:T(8,128)(2,1)S(1)}, bf16[128,1280]{1,0:T(8,128)(2,1)S(1)}, u32[]{:S(2)}, u32[]{:S(2)}) collective-permute-start(bf16[128,1280]{1,0:T(8,128)(2,1)S(1)} %get-tuple-element.41), channel_id=1, source_target_pairs={{0,8},{1,9},{2,10},{3,11},{4,12},{5,13},{6,14},{7,15},{8,0},{9,1},... | collective-permute-start | bytes 983048 | tf_op jit(solution)/shard_map/ppermute | solution.py:195
  15.0 1.9 %copy-start = (bf16[1,1280,1280]{2,1,0:T(8,128)(2,1)S(1)}, bf16[1,1280,1280]{2,1,0:T(8,128)(2,1)}, u32[]{:S(2)}) copy-start(bf16[1,1280,1280]{2,1,0:T(8,128)(2,1)} %param.16) | copy-start | bytes 9830404
  17.0 1.9 %copy-start.2 = (bf16[1,1280,1280]{2,1,0:T(8,128)(2,1)S(1)}, bf16[1,1280,1280]{2,1,0:T(8,128)(2,1)}, u32[]{:S(2)}) copy-start(bf16[1,1280,1280]{2,1,0:T(8,128)(2,1)} %param.17) | copy-start | bytes 9830404
  18.9 0.7 copy-start.10
  19.6 18.4 %copy-start.1 = (bf16[1,1280,1280]{2,1,0:T(8,128)(2,1)S(1)}, bf16[1,1280,1280]{2,1,0:T(8,128)(2,1)}, u32[]{:S(2)}) copy-start(bf16[1,1280,1280]{2,1,0:T(8,128)(2,1)} %param.16) | copy-start | bytes 9830404
  19.6 18.4 %copy-start.3 = (bf16[1,1280,1280]{2,1,0:T(8,128)(2,1)S(1)}, bf16[1,1280,1280]{2,1,0:T(8,128)(2,1)}, u32[]{:S(2)}) copy-start(bf16[1,1280,1280]{2,1,0:T(8,128)(2,1)} %param.17) | copy-start | bytes 9830404
  26.5 0.8 copy-start.8
  27.4 10.6 %collective-permute-start.6 = (bf16[128,1280]{1,0:T(8,128)(2,1)S(1)}, bf16[128,1280]{1,0:T(8,128)(2,1)S(1)}, u32[]{:S(2)}, u32[]{:S(2)}) collective-permute-start(bf16[128,1280]{1,0:T(8,128)(2,1)S(1)} %collective-permute-done.5.own_ref.tokens_ref), channel_id=1, source_target_pairs={{0,2},{1,3},{2,0},{3,1},{4,6},{5,7},{6,4},{7,5},{8,10},{9,11},{10,... | collective-permute-start | bytes 983048 | tf_op jit(solution)/shard_map/ppermute | solution.py:195
  29.1 15.0 %collective-permute-start.4 = (bf16[128,1280]{1,0:T(8,128)(2,1)S(1)}, bf16[128,1280]{1,0:T(8,128)(2,1)S(1)}, u32[]{:S(2)}, u32[]{:S(2)}) collective-permute-start(bf16[128,1280]{1,0:T(8,128)(2,1)S(1)} %get-tuple-element.43), channel_id=1, source_target_pairs={{0,12},{1,13},{2,14},{3,15},{4,8},{5,9},{6,10},{7,11},{8,4},{9,5},... | collective-permute-start | bytes 983048 | tf_op jit(solution)/shard_map/ppermute | solution.py:195
  32.7 13.5 %collective-permute-start.8 = (bf16[128,1280]{1,0:T(8,128)(2,1)S(1)}, bf16[128,1280]{1,0:T(8,128)(2,1)S(1)}, u32[]{:S(2)}, u32[]{:S(2)}) collective-permute-start(bf16[128,1280]{1,0:T(8,128)(2,1)S(1)} %collective-permute-done.3.own_ref.tokens_ref), channel_id=1, source_target_pairs={{0,2},{1,3},{2,0},{3,1},{4,6},{5,7},{6,4},{7,5},{8,10},{9,11},{10,... | collective-permute-start | bytes 983048 | tf_op jit(solution)/shard_map/ppermute | solution.py:195
  44.1 10.7 %collective-permute-start.7 = (bf16[128,1280]{1,0:T(8,128)(2,1)S(1)}, bf16[128,1280]{1,0:T(8,128)(2,1)S(1)}, u32[]{:S(2)}, u32[]{:S(2)}) collective-permute-start(bf16[128,1280]{1,0:T(8,128)(2,1)S(1)} %collective-permute-done.4.own_ref.tokens_ref), channel_id=1, source_target_pairs={{0,2},{1,3},{2,0},{3,1},{4,6},{5,7},{6,4},{7,5},{8,10},{9,11},{10,... | collective-permute-start | bytes 983048 | tf_op jit(solution)/shard_map/ppermute | solution.py:195
  45.9 17.3 %collective-permute-start.9 = (bf16[128,1280]{1,0:T(8,128)(2,1)S(1)}, bf16[128,1280]{1,0:T(8,128)(2,1)S(1)}, u32[]{:S(2)}, u32[]{:S(2)}) collective-permute-start(bf16[128,1280]{1,0:T(8,128)(2,1)S(1)} %get-tuple-element.47), channel_id=1, source_target_pairs={{0,2},{1,3},{2,0},{3,1},{4,6},{5,7},{6,4},{7,5},{8,10},{9,11},{10,... | collective-permute-start | bytes 983048 | tf_op jit(solution)/shard_map/ppermute | solution.py:195
  52.2 16.6 %collective-permute-start.10 = (bf16[128,1280]{1,0:T(8,128)(2,1)S(1)}, bf16[128,1280]{1,0:T(8,128)(2,1)S(1)}, u32[]{:S(2)}, u32[]{:S(2)}) collective-permute-start(bf16[128,1280]{1,0:T(8,128)(2,1)S(1)} %get-tuple-element.50), channel_id=1, source_target_pairs={{0,2},{1,3},{2,0},{3,1},{4,6},{5,7},{6,4},{7,5},{8,10},{9,11},{10,... | collective-permute-start | bytes 983048 | tf_op jit(solution)/shard_map/ppermute | solution.py:195
  61.0 18.5 %copy-start.12 = (f32[2,16,80]{2,1,0:T(8,128)S(1)}, f32[2,16,80]{2,1,0:T(8,128)}, u32[]{:S(2)}) copy-start(f32[2,16,80]{2,1,0:T(8,128)} %param.19) | copy-start | bytes 30724
  61.1 18.6 %copy-start.13 = (f32[1280]{0:T(1024)S(1)}, f32[1280]{0:T(1024)}, u32[]{:S(2)}) copy-start(f32[1280]{0:T(1024)} %param.18) | copy-start | bytes 15364
  61.1 14.4 %collective-permute-start.11 = (bf16[128,1280]{1,0:T(8,128)(2,1)S(1)}, bf16[128,1280]{1,0:T(8,128)(2,1)S(1)}, u32[]{:S(2)}, u32[]{:S(2)}) collective-permute-start(bf16[128,1280]{1,0:T(8,128)(2,1)S(1)} %get-tuple-element.58), channel_id=1, source_target_pairs={{0,2},{1,3},{2,0},{3,1},{4,6},{5,7},{6,4},{7,5},{8,10},{9,11},{10,... | collective-permute-start | bytes 983048 | tf_op jit(solution)/shard_map/ppermute | solution.py:195
  62.9 17.4 %collective-permute-start.12 = (bf16[128,1280]{1,0:T(8,128)(2,1)}, bf16[128,1280]{1,0:T(8,128)(2,1)}, u32[]{:S(2)}, u32[]{:S(2)}) collective-permute-start(bf16[128,1280]{1,0:T(8,128)(2,1)} %get-tuple-element.63), channel_id=1, source_target_pairs={{0,2},{1,3},{2,0},{3,1},{4,6},{5,7},{6,4},{7,5},{8,10},{9,11},{10,... | collective-permute-start | bytes 983048 | tf_op jit(solution)/shard_map/ppermute | solution.py:195
  64.1 29.0 %collective-permute-start.13 = (bf16[128,1280]{1,0:T(8,128)(2,1)}, bf16[128,1280]{1,0:T(8,128)(2,1)}, u32[]{:S(2)}, u32[]{:S(2)}) collective-permute-start(bf16[128,1280]{1,0:T(8,128)(2,1)} %finish.4), channel_id=1, source_target_pairs={{0,4},{1,5},{2,6},{3,7},{4,0},{5,1},{6,2},{7,3},{8,12},{9,13},{10,... | collective-permute-start | bytes 983048 | tf_op jit(solution)/shard_map/ppermute | solution.py:195
  68.8 47.3 %copy-start.4 = (bf16[1280,1280]{1,0:T(8,128)(2,1)S(1)}, bf16[1280,1280]{1,0:T(8,128)(2,1)}, u32[]{:S(2)}) copy-start(bf16[1280,1280]{1,0:T(8,128)(2,1)} %proj_ref.1) | copy-start | bytes 9830404
  69.7 23.3 %collective-permute-start.14 = (bf16[128,1280]{1,0:T(8,128)(2,1)}, bf16[128,1280]{1,0:T(8,128)(2,1)}, u32[]{:S(2)}, u32[]{:S(2)}) collective-permute-start(bf16[128,1280]{1,0:T(8,128)(2,1)} %finish.5), channel_id=1, source_target_pairs={{0,8},{1,9},{2,10},{3,11},{4,12},{5,13},{6,14},{7,15},{8,0},{9,1},... | collective-permute-start | bytes 983048 | tf_op jit(solution)/shard_map/ppermute | solution.py:195
  76.4 16.7 %collective-permute-start.15 = (bf16[128,1280]{1,0:T(8,128)(2,1)}, bf16[128,1280]{1,0:T(8,128)(2,1)}, u32[]{:S(2)}, u32[]{:S(2)}) collective-permute-start(bf16[128,1280]{1,0:T(8,128)(2,1)} %finish.6), channel_id=1, source_target_pairs={{0,12},{1,13},{2,14},{3,15},{4,8},{5,9},{6,10},{7,11},{8,4},{9,5},... | collective-permute-start | bytes 983048 | tf_op jit(solution)/shard_map/ppermute | solution.py:195
  80.3 1.0 copy-start.6
  81.3 1.1 copy-start.9
  97.3 1.2 collective-permute-start.16
  98.6 3.8 %collective-permute-start.17 = (bf16[8,1280]{1,0:T(8,128)(2,1)S(1)}, bf16[8,1280]{1,0:T(8,128)(2,1)S(1)}, u32[]{:S(2)}, u32[]{:S(2)}) collective-permute-start(bf16[8,1280]{1,0:T(8,128)(2,1)S(1)} %pad_maximum_fusion.2), channel_id=1, source_target_pairs={{0,2},{1,3},{2,0},{3,1},{4,6},{5,7},{6,4},{7,5},{8,10},{9,11},{10,... | collective-permute-start | bytes 61448 | tf_op jit(solution)/shard_map/ppermute | solution.py:195
  102.5 7.2 %collective-permute-start.18 = (bf16[16,1280]{1,0:T(8,128)(2,1)S(1)}, bf16[16,1280]{1,0:T(8,128)(2,1)S(1)}, u32[]{:S(2)}, u32[]{:S(2)}) collective-permute-start(bf16[16,1280]{1,0:T(8,128)(2,1)S(1)} %pad_maximum_fusion.1), channel_id=1, source_target_pairs={{0,4},{1,5},{2,6},{3,7},{4,0},{5,1},{6,2},{7,3},{8,12},{9,13},{10,... | collective-permute-start | bytes 122888 | tf_op jit(solution)/shard_map/ppermute | solution.py:195
  109.7 5.5 %collective-permute-start.19 = (bf16[32,1280]{1,0:T(8,128)(2,1)S(1)}, bf16[32,1280]{1,0:T(8,128)(2,1)}, u32[]{:S(2)}, u32[]{:S(2)}) collective-permute-start(bf16[32,1280]{1,0:T(8,128)(2,1)S(1)} %pad_maximum_fusion), channel_id=1, source_target_pairs={{0,8},{1,9},{2,10},{3,11},{4,12},{5,13},{6,14},{7,15},{8,0},{9,1},... | collective-permute-start | bytes 245768 | tf_op jit(solution)/shard_map/ppermute | solution.py:195

commit v2 on v1

--- a/solution.py
+++ b/solution.py
@@ -12,10 +12,13 @@
 IMG_TOK = 256
 SPLIT = 4
 HEAD_DIM = 80
+TILE = 256
 F32 = jnp.float32
 BF16 = jnp.bfloat16
 VMEM = pl.BlockSpec(memory_space=pltpu.VMEM)
 SMEM = pl.BlockSpec(memory_space=pltpu.SMEM)
+ANY = pl.BlockSpec(memory_space=pl.ANY)
+FIRST = 20_000_000_000
 
 
 def iota(shape, dim):
@@ -60,45 +63,62 @@
 
 
 def ffn_kernel(mine_ref, own_ref, other_ref, gain_ref, router_ref, in_a, out_a, in_b, out_b, *outs):
-    kept_ref, gate_ref, sent_ref, x_ref, hidden_ref = outs
+    kept_ref, gate_ref, *sent_refs, x_ref, hidden_ref = outs
     cap = own_ref.shape[0]
-    block = 256
     gain = gain_ref[...]
     own = layer_norm(own_ref[...].astype(F32), gain).astype(BF16)
     x_ref[:cap] = own
     x_ref[cap:] = layer_norm(other_ref[...].astype(F32), gain).astype(BF16)
     ff, width = out_a.shape
     for index, w_in in enumerate((in_a, in_b)):
-        for at in range(0, ff, block):
-            pre = dot(x_ref[...], w_in[:, at : at + block])
-            hidden_ref[index, :, at : at + block] = jax.nn.gelu(pre, approximate=True).astype(BF16)
+        for at in range(0, ff, TILE):
+            pre = dot(x_ref[...], w_in[:, at : at + TILE])
+            hidden_ref[index, :, at : at + TILE] = jax.nn.gelu(pre, approximate=True).astype(BF16)
     router = router_ref[...].astype(F32)
     column = jnp.where(iota(router.shape, 0) == mine_ref[0], router, 0.0)
     column = jnp.sum(column, axis=0, keepdims=True)
     gate_ref[...] = jax.nn.sigmoid(jnp.sum(own.astype(F32) * column, axis=1, keepdims=True))
-    for at in range(0, width, block):
+    for at in range(0, width, TILE):
         total = None
         for index, w_out in enumerate((out_a, out_b)):
-            part = dot(hidden_ref[index], w_out[:, at : at + block]).astype(BF16).astype(F32)
+            part = dot(hidden_ref[index], w_out[:, at : at + TILE]).astype(BF16).astype(F32)
             total = part if total is None else total + part
-        kept_ref[:, at : at + block] = total[:cap]
-        sent_ref[:, at : at + block] = total[cap:].astype(BF16)
-
-
-def finish_kernel(tokens_ref, gate_ref, kept_ref, got_ref, mixed_ref):
-    total = kept_ref[...] + got_ref[...].astype(F32)
+        kept_ref[:, at : at + TILE] = total[:cap]
+        for sent_ref, term in zip(sent_refs, split3(total[cap:])):
+            sent_ref[:, at : at + TILE] = term
+
+
+def finish_kernel(tokens_ref, gate_ref, kept_ref, *refs):
+    got_refs, mixed_ref = refs[:-1], refs[-1]
+    total = kept_ref[...] + sum(got_ref[...].astype(F32) for got_ref in got_refs)
     mixed_ref[...] = (tokens_ref[...].astype(F32) + gate_ref[...] * total).astype(BF16)
 
 
-def combine_kernel(experts, *refs):
-    label_ref, parts, rest = refs[0], refs[1 : 1 + experts], refs[1 + experts :]
-    place_ref, gain_ref, query_ref, mixed_ref, pooled_ref, buffer = rest
+def chosen(place, first, many):
+    return (iota((many, place.shape[1]), 0) + first == place).astype(F32).astype(BF16)
+
+
+def partial_kernel(*refs):
+    parts, (place_ref, sum_ref, buffer) = refs[:-3], refs[-3:]
     cap = parts[0].shape[0]
-    rows, width = mixed_ref.shape
     for k, part in enumerate(parts):
         buffer[k * cap : (k + 1) * cap] = part[...]
-    select = (iota((experts * cap, rows), 0) == place_ref[...]).astype(F32).astype(BF16)
-    mixed = dot(select, buffer[...], ((0,), (0,)))
+    select = chosen(place_ref[...], cap, len(parts) * cap)
+    sum_ref[...] = dot(select, buffer[...], ((0,), (0,)))
+
+
+def combine_kernel(experts, *refs):
+    label_ref, sum_ref, back_ref, tokens_ref, gate_ref, kept_ref, high_ref, low_ref = refs[:8]
+    place_ref, gain_ref, query_ref, mixed_ref, pooled_ref, buffer = refs[8:]
+    cap = back_ref.shape[0]
+    rows, width = mixed_ref.shape
+    finish_kernel(tokens_ref, gate_ref, kept_ref, high_ref, low_ref, buffer.at[:cap])
+    buffer[cap:] = back_ref[...]
+    place = place_ref[...]
+    select = jnp.concatenate(
+        [chosen(place, 0, cap), chosen(place, (experts - 1) * cap, cap)], axis=0
+    )
+    mixed = sum_ref[...] + dot(select, buffer[...], ((0,), (0,)))
     mixed_ref[...] = mixed.astype(BF16)
     z = layer_norm(mixed, gain_ref[...])
     head, feature = iota((width, HEADS), 1), iota((width, HEADS), 0)
@@ -118,7 +138,9 @@
     pooled_ref[2:4] = jnp.full((2, width), label_ref[0], jnp.int32).astype(F32).astype(BF16)
 
 
-def tail_kernel(pairs, mine_ref, scale_ref, all_ref, proj_ref, grad_ref, d_pooled_ref, loss_ref):
+def tail_kernel(
+    pairs, mine_ref, scale_ref, all_ref, proj_ref, d_pooled_ref, loss_ref, grad_ref, store, sems
+):
     exact = lax.Precision.HIGHEST
     me, scale = mine_ref[0], scale_ref[0]
     source = all_ref[...]
@@ -149,27 +171,38 @@
     d_text = dot(grad, image, ((0,), (0,)), exact)
     d_unit = jnp.concatenate([d_image, d_text], axis=0)
     d_emb = (d_unit - unit * jnp.sum(unit * d_unit, axis=-1, keepdims=True)) / norm
-    row = iota(d_emb.shape, 0)
-    for modal in range(2):
-        own = jnp.sum(jnp.where(row == me + modal * pairs, d_emb, 0.0), axis=0, keepdims=True)
-        back = sum(dot(term, proj_ref[...], ((1,), (1,))) for term in split3(own))
-        d_pooled_ref[modal : modal + 1] = back
     terms = jnp.concatenate(split3(d_emb), axis=0)
     thrice = jnp.concatenate([pooled] * 3, axis=0)
-    block = 256
-    for at in range(0, pooled.shape[1], block):
-        grad_ref[at : at + block] = dot(thrice[:, at : at + block], terms, ((0,), (0,)))
-
-
-def call(kernel, name, outs, specs, limit, scratch=()):
+    copies = []
+    for at in range(0, pooled.shape[1], TILE):
+        store[at : at + TILE] = dot(thrice[:, at : at + TILE], terms, ((0,), (0,)))
+        copies.append(
+            pltpu.make_async_copy(
+                store.at[at : at + TILE], grad_ref.at[at : at + TILE], sems.at[at // TILE]
+            )
+        )
+        copies[-1].start()
+    row = iota(d_emb.shape, 0)
+    own = [
+        jnp.sum(jnp.where(row == me + modal * pairs, d_emb, 0.0), axis=0, keepdims=True)
+        for modal in range(2)
+    ]
+    terms = jnp.concatenate(split3(jnp.concatenate(own, axis=0)), axis=0)
+    back = dot(terms, proj_ref[...], ((1,), (1,)))
+    d_pooled_ref[...] = back[0:2] + back[2:4] + back[4:6]
+    for copy in copies:
+        copy.wait()
+
+
+def call(kernel, name, outs, specs, limit, scratch=(), flops=0, in_hbm=0):
     return pl.pallas_call(
         kernel,
         out_shape=[jax.ShapeDtypeStruct(*o) for o in outs],
         in_specs=specs,
-        out_specs=[VMEM] * len(outs),
+        out_specs=[VMEM] * (len(outs) - in_hbm) + [ANY] * in_hbm,
         scratch_shapes=list(scratch),
         compiler_params=pltpu.CompilerParams(vmem_limit_bytes=limit * 1024 * 1024),
-        cost_estimate=pl.CostEstimate(flops=0, bytes_accessed=0, transcendentals=0),
+        cost_estimate=pl.CostEstimate(flops=flops, bytes_accessed=0, transcendentals=0),
         name=name,
     )
 
@@ -202,6 +235,7 @@
         [((cap, width), BF16)] * experts + [((1, rows), jnp.int32)],
         [SMEM] + [VMEM] * 2,
         8,
+        flops=FIRST,
     )(mine, route.reshape(1, rows), tokens.reshape(rows, width))
     held = {k: swap(chunks[k], SPLIT * k) for k in range(1, min(experts, 3))}
     held[0] = chunks[0]
@@ -214,7 +248,7 @@
             call(
                 ffn_kernel,
                 "ffn",
-                [((cap, width), F32), ((cap, 1), F32), ((cap, width), BF16)],
+                [((cap, width), F32), ((cap, 1), F32)] + [((cap, width), BF16)] * (1 if k else 2),
                 [SMEM] + [VMEM] * 8,
                 20,
                 [pltpu.VMEM((2 * cap, width), BF16), pltpu.VMEM((2, 2 * cap, ff), BF16)],
@@ -228,23 +262,37 @@
             )
         )
     ready, result = {}, parts[-1][2]
-    for k in list(range(1, experts)) + [0]:
+    for k in range(1, experts):
         kept, gate, leave = parts[k]
-        got = swap(leave if k else after(leave, parts[-1][2]), 2)
         (result,) = call(finish_kernel, "finish", [((cap, width), BF16)], [VMEM] * 4, 4)(
-            held[k], gate, after(kept, result), got
+            held[k], gate, after(kept, result), swap(leave, 2)
         )
-        ready[k] = swap(result, SPLIT * k) if k else result
+        ready[k] = swap(result, SPLIT * k)
+    kept, gate, *leave = parts[0]
+    got = [swap(after(term, result), 2) for term in leave]
+    (partial,) = call(
+        partial_kernel,
+        "partial",
+        [((rows, width), F32)],
+        [VMEM] * (experts - 1),
+        8,
+        [pltpu.VMEM(((experts - 2) * cap, width), BF16)],
+    )(*[ready[k] for k in range(1, experts - 1)], place)
     mixed, pooled = call(
         functools.partial(combine_kernel, experts),
         "combine",
         [((rows, width), BF16), ((4, width), BF16)],
-        [SMEM] + [VMEM] * (3 + experts),
+        [SMEM] + [VMEM] * 10,
         20,
-        [pltpu.VMEM((experts * cap, width), BF16)],
+        [pltpu.VMEM((2 * cap, width), BF16)],
     )(
         labels,
-        *[ready[k] for k in range(experts)],
+        partial,
+        ready[experts - 1],
+        held[0],
+        gate,
+        kept,
+        *got,
         place,
         out_gain.reshape(1, width),
         pool_query.reshape(2, width),
@@ -253,12 +301,14 @@
     while bits < devices:
         pooled = jnp.concatenate([pooled, swap(pooled, bits)], axis=0)
         bits = bits * 2
-    grad_proj, d_pooled, loss = call(
+    d_pooled, loss, grad_proj = call(
         functools.partial(tail_kernel, devices),
         "contrast",
-        [((width, width), F32), ((2, width), F32), ((1, 1), F32)],
+        [((2, width), F32), ((1, 1), F32), ((width, width), F32)],
         [SMEM] * 2 + [VMEM] * 2,
         24,
+        [pltpu.VMEM((width, width), F32), pltpu.SemaphoreType.DMA((-(-width // TILE),))],
+        in_hbm=1,
     )(me.reshape(1), logit_scale, pooled, proj)
     return (
         mixed.reshape(count, length, width),

time: 127 us -> 121 us (0.953)
  waiting for transfers between devices: 31.6 us -> 46.6 us
  starting transfers between devices: 37.1 us -> 25.7 us
  Pallas kernels: 45 us -> 37.8 us
  local copies, waits for them, and re-layouts: 11 us -> 8.58 us
    ppermute x20 -> x21, waiting for transfers between devices: 31.6 us -> 46.6 us  [swap(): return lax.ppermute(values, 'dp', [(i, i ^ bits) for i in range(devices)])]
    ppermute x20 -> x21, starting transfers between devices: 37.1 us -> 25.7 us  [swap(): return lax.ppermute(values, 'dp', [(i, i ^ bits) for i in range(devices)])]
    pallas_call x5 -> x6, Pallas kernels: 36 us -> 31.5 us  [the longest x4 25.2 us: on_device(): call(ffn_kernel, 'ffn', [((cap, width), F32), ((cap, 1), F32)] + [((cap,...]
    pallas_call x4 -> x3, Pallas kernels: 3.78 us -> 1.19 us  [on_device(): call(finish_kernel, 'finish', [((cap, width), BF16)], [VMEM] * 4, 4)]
    unnamed x28 -> x34, local copies, waits for them, and re-layouts: 9.3 us -> 7.57 us
  transfers between devices with their start and end apart: 20 -> 21, of which waited for: 10 -> 13; matrix products, arithmetic and copies ran while one was open for 1% -> 0% of each run, Pallas kernels for 24% -> 23%
where the time goes in v2:
time: 121 us
  waiting for transfers between devices  46.6 us (39%)
  Pallas kernels  37.8 us (31%)
  starting transfers between devices  25.7 us (21%)
  local copies, waits for them, and re-layouts  8.58 us (7%)
  between operations  2.3 us (2%)
    ppermute x21, waiting for transfers between devices, swap(): return lax.ppermute(values, 'dp', [(i, i ^ bits) for i in range(devices)])  46.6 us
    ppermute x21, starting transfers between devices, swap(): return lax.ppermute(values, 'dp', [(i, i ^ bits) for i in range(devices)])  25.7 us
    pallas_call x4, Pallas kernels, on_device(): call(ffn_kernel, 'ffn', [((cap, width), F32), ((cap, 1), F32)] + [((cap,...  25.2 us
    unnamed x34, local copies, waits for them, and re-layouts  7.57 us
    pallas_call x1, Pallas kernels, on_device(): call(functools.partial(tail_kernel, devices), 'contrast', [((2, width), F...  5.83 us
    pallas_call x1, Pallas kernels, on_device(): call(functools.partial(combine_kernel, experts), 'combine', [((rows, widt...  4.15 us
  transfers between devices with their start and end apart: 21, of which 13 were waited for; matrix products, arithmetic and copies ran while one was open for 0% of the time, Pallas kernels for 23%

profile of v2, /device:TPU:0, one launch (start us, length us, event | category | flops | bytes accessed | tf_op | source)
XLA Modules:
  0.0 121.0 jit_solution(16455289697261459261)
XLA Ops:
  0.6 0.5 collective-permute-start.2
  1.2 0.1 collective-permute-start.3
  1.2 1.1 copy-done.12
  2.4 0.7 copy-done.13
  3.1 1.0 dispatch.1
  4.1 3.0 %collective-permute-start.1 = (bf16[128,1280]{1,0:T(8,128)(2,1)S(1)}, bf16[128,1280]{1,0:T(8,128)(2,1)S(1)}, u32[]{:S(2)}, u32[]{:S(2)}) collective-permute-start(bf16[128,1280]{1,0:T(8,128)(2,1)S(1)} %get-tuple-element.39.own_ref.refs_3_), channel_id=1, source_target_pairs={{0,2},{1,3},{2,0},{3,1},{4,6},{5,7},{6,4},{7,5},{8,10},{9,11},{10,... | collective-permute-start | bytes 983048 | tf_op jit(solution)/shard_map/ppermute | solution.py:228
  7.1 1.6 %collective-permute-start = (bf16[128,1280]{1,0:T(8,128)(2,1)S(1)}, bf16[128,1280]{1,0:T(8,128)(2,1)S(1)}, u32[]{:S(2)}, u32[]{:S(2)}) collective-permute-start(bf16[128,1280]{1,0:T(8,128)(2,1)S(1)} %get-tuple-element.38), channel_id=1, source_target_pairs={{0,4},{1,5},{2,6},{3,7},{4,0},{5,1},{6,2},{7,3},{8,12},{9,13},{10,... | collective-permute-start | bytes 983048 | tf_op jit(solution)/shard_map/ppermute | solution.py:228
  8.7 2.6 %collective-permute-start.5 = (bf16[128,1280]{1,0:T(8,128)(2,1)S(1)}, bf16[128,1280]{1,0:T(8,128)(2,1)S(1)}, u32[]{:S(2)}, u32[]{:S(2)}) collective-permute-start(bf16[128,1280]{1,0:T(8,128)(2,1)S(1)} %get-tuple-element.46), channel_id=1, source_target_pairs={{0,8},{1,9},{2,10},{3,11},{4,12},{5,13},{6,14},{7,15},{8,0},{9,1},... | collective-permute-start | bytes 983048 | tf_op jit(solution)/shard_map/ppermute | solution.py:228
  11.3 3.8 %collective-permute-done.1.other_ref = bf16[128,1280]{1,0:T(8,128)(2,1)S(1)} collective-permute-done((bf16[128,1280]{1,0:T(8,128)(2,1)S(1)}, bf16[128,1280]{1,0:T(8,128)(2,1)S(1)}, u32[]{:S(2)}, u32[]{:S(2)}) %collective-permute-start.1) | collective-permute-done | bytes 327712 | tf_op jit(solution)/shard_map/ppermute | solution.py:228
  15.0 0.0 collective-permute-done.2.in_b
  15.0 0.0 collective-permute-done.3.out_b
  15.1 6.9 %ffn.4 = (f32[128,1280]{1,0:T(8,128)S(1)}, f32[128,1]{1,0:T(8,128)S(1)}, bf16[128,1280]{1,0:T(8,128)(2,1)}, bf16[128,1280]{1,0:T(8,128)(2,1)}) custom-call(s32[1]{0:T(128)} %bitcast.mine_ref, bf16[128,1280]{1,0:T(8,128)(2,1)S(1)} %get-tuple-element.39.own_ref.refs_3_, bf16[128,1280]{1,0:T(8,128)(2,1)S(1)} %collective-permute-done.1.other_ref, ...), custom_call_target="tpu_custom_call" | custom-call | tf_op jit(solution)/shard_map/ffn/pallas_call | solution.py:248
  22.0 1.4 %collective-permute-done.own_ref.tokens_ref = bf16[128,1280]{1,0:T(8,128)(2,1)S(1)} collective-permute-done((bf16[128,1280]{1,0:T(8,128)(2,1)S(1)}, bf16[128,1280]{1,0:T(8,128)(2,1)S(1)}, u32[]{:S(2)}, u32[]{:S(2)}) %collective-permute-start) | collective-permute-done | bytes 327712 | tf_op jit(solution)/shard_map/ppermute | solution.py:228
  23.4 0.4 collective-permute-start.4
  23.8 2.0 %collective-permute-done.5.own_ref.tokens_ref = bf16[128,1280]{1,0:T(8,128)(2,1)S(1)} collective-permute-done((bf16[128,1280]{1,0:T(8,128)(2,1)S(1)}, bf16[128,1280]{1,0:T(8,128)(2,1)S(1)}, u32[]{:S(2)}, u32[]{:S(2)}) %collective-permute-start.5) | collective-permute-done | bytes 327712 | tf_op jit(solution)/shard_map/ppermute | solution.py:228
  25.8 2.5 %collective-permute-start.6 = (bf16[128,1280]{1,0:T(8,128)(2,1)S(1)}, bf16[128,1280]{1,0:T(8,128)(2,1)S(1)}, u32[]{:S(2)}, u32[]{:S(2)}) collective-permute-start(bf16[128,1280]{1,0:T(8,128)(2,1)S(1)} %get-tuple-element.47), channel_id=1, source_target_pairs={{0,12},{1,13},{2,14},{3,15},{4,8},{5,9},{6,10},{7,11},{8,4},{9,5},... | collective-permute-start | bytes 983048 | tf_op jit(solution)/shard_map/ppermute | solution.py:228
  28.2 0.5 collective-permute-start.8
  28.7 5.3 %collective-permute-done.4.other_ref = bf16[128,1280]{1,0:T(8,128)(2,1)S(1)} collective-permute-done((bf16[128,1280]{1,0:T(8,128)(2,1)S(1)}, bf16[128,1280]{1,0:T(8,128)(2,1)S(1)}, u32[]{:S(2)}, u32[]{:S(2)}) %collective-permute-start.4) | collective-permute-done | bytes 327712 | tf_op jit(solution)/shard_map/ppermute | solution.py:228
  34.1 6.1 %ffn.5 = (f32[128,1280]{1,0:T(8,128)S(1)}, f32[128,1]{1,0:T(8,128)S(1)}, bf16[128,1280]{1,0:T(8,128)(2,1)S(1)}) custom-call(s32[1]{0:T(128)} %bitcast.mine_ref, bf16[128,1280]{1,0:T(8,128)(2,1)S(1)} %collective-permute-done.own_ref.tokens_ref, bf16[128,1280]{1,0:T(8,128)(2,1)S(1)} %collective-permute-done.4.other_ref, f32[1,1280]{1,0:T(1,128)S(1)} %reshape.44.gain_ref, ...), custom_call_target="tpu_custom_call" | custom-call | tf_op jit(solution)/shard_map/ffn/pallas_call | solution.py:248
  40.1 0.0 collective-permute-done.6.own_ref.tokens_ref
  40.1 0.4 collective-permute-start.7
  40.6 1.6 %collective-permute-start.9 = (bf16[128,1280]{1,0:T(8,128)(2,1)S(1)}, bf16[128,1280]{1,0:T(8,128)(2,1)S(1)}, u32[]{:S(2)}, u32[]{:S(2)}) collective-permute-start(bf16[128,1280]{1,0:T(8,128)(2,1)S(1)} %get-tuple-element.48), channel_id=1, source_target_pairs={{0,2},{1,3},{2,0},{3,1},{4,6},{5,7},{6,4},{7,5},{8,10},{9,11},{10,... | collective-permute-start | bytes 983048 | tf_op jit(solution)/shard_map/ppermute | solution.py:228
  42.2 0.0 collective-permute-done.8.other_ref
  42.2 6.1 %ffn.6 = (f32[128,1280]{1,0:T(8,128)S(1)}, f32[128,1]{1,0:T(8,128)S(1)}, bf16[128,1280]{1,0:T(8,128)(2,1)S(1)}) custom-call(s32[1]{0:T(128)} %bitcast.mine_ref, bf16[128,1280]{1,0:T(8,128)(2,1)S(1)} %collective-permute-done.5.own_ref.tokens_ref, bf16[128,1280]{1,0:T(8,128)(2,1)S(1)} %collective-permute-done.8.other_ref, f32[1,1280]{1,0:T(1,128)S(1)} %reshape.44.gain_ref, ...), custom_call_target="tpu_custom_call" | custom-call | tf_op jit(solution)/shard_map/ffn/pallas_call | solution.py:248
  48.3 0.4 collective-permute-start.11
  48.7 2.1 %collective-permute-done.7.other_ref = bf16[128,1280]{1,0:T(8,128)(2,1)S(1)} collective-permute-done((bf16[128,1280]{1,0:T(8,128)(2,1)S(1)}, bf16[128,1280]{1,0:T(8,128)(2,1)S(1)}, u32[]{:S(2)}, u32[]{:S(2)}) %collective-permute-start.7) | collective-permute-done | bytes 327712 | tf_op jit(solution)/shard_map/ppermute | solution.py:228
  50.9 6.2 %ffn.7 = (f32[128,1280]{1,0:T(8,128)S(1)}, f32[128,1]{1,0:T(8,128)S(1)}, bf16[128,1280]{1,0:T(8,128)(2,1)S(1)}) custom-call(s32[1]{0:T(128)} %bitcast.mine_ref, bf16[128,1280]{1,0:T(8,128)(2,1)S(1)} %collective-permute-done.6.own_ref.tokens_ref, bf16[128,1280]{1,0:T(8,128)(2,1)S(1)} %collective-permute-done.7.other_ref, f32[1,1280]{1,0:T(1,128)S(1)} %reshape.44.gain_ref, ...), custom_call_target="tpu_custom_call" | custom-call | tf_op jit(solution)/shard_map/ffn/pallas_call | solution.py:248
  57.1 0.0 copy-start.14
  57.1 0.0 copy-start.16
  57.1 0.5 collective-permute-start.13
  57.6 0.3 collective-permute-done.9.refs_0_
  57.9 0.2 finish.3
  58.0 1.5 %collective-permute-start.10 = (bf16[128,1280]{1,0:T(8,128)(2,1)S(1)}, bf16[128,1280]{1,0:T(8,128)(2,1)S(1)}, u32[]{:S(2)}, u32[]{:S(2)}) collective-permute-start(bf16[128,1280]{1,0:T(8,128)(2,1)S(1)} %finish.3), channel_id=1, source_target_pairs={{0,4},{1,5},{2,6},{3,7},{4,0},{5,1},{6,2},{7,3},{8,12},{9,13},{10,... | collective-permute-start | bytes 983048 | tf_op jit(solution)/shard_map/ppermute | solution.py:228
  59.6 4.0 %collective-permute-done.11.refs_0_ = bf16[128,1280]{1,0:T(8,128)(2,1)S(1)} collective-permute-done((bf16[128,1280]{1,0:T(8,128)(2,1)S(1)}, bf16[128,1280]{1,0:T(8,128)(2,1)S(1)}, u32[]{:S(2)}, u32[]{:S(2)}) %collective-permute-start.11) | collective-permute-done | bytes 327712 | tf_op jit(solution)/shard_map/ppermute | solution.py:228
  63.5 0.2 finish.4
  63.7 3.2 %collective-permute-start.12 = (bf16[128,1280]{1,0:T(8,128)(2,1)S(1)}, bf16[128,1280]{1,0:T(8,128)(2,1)S(1)}, u32[]{:S(2)}, u32[]{:S(2)}) collective-permute-start(bf16[128,1280]{1,0:T(8,128)(2,1)S(1)} %finish.4), channel_id=1, source_target_pairs={{0,8},{1,9},{2,10},{3,11},{4,12},{5,13},{6,14},{7,15},{8,0},{9,1},... | collective-permute-start | bytes 983048 | tf_op jit(solution)/shard_map/ppermute | solution.py:228
  66.9 1.1 collective-permute-done.13.refs_0_
  68.1 0.9 finish.5
  68.9 0.4 collective-permute-start.16
  69.3 1.6 %collective-permute-start.15 = (bf16[128,1280]{1,0:T(8,128)(2,1)}, bf16[128,1280]{1,0:T(8,128)(2,1)}, u32[]{:S(2)}, u32[]{:S(2)}) collective-permute-start(bf16[128,1280]{1,0:T(8,128)(2,1)} %get-tuple-element.64), channel_id=1, source_target_pairs={{0,2},{1,3},{2,0},{3,1},{4,6},{5,7},{6,4},{7,5},{8,10},{9,11},{10,... | collective-permute-start | bytes 983048 | tf_op jit(solution)/shard_map/ppermute | solution.py:228
  71.0 2.0 %collective-permute-start.14 = (bf16[128,1280]{1,0:T(8,128)(2,1)}, bf16[128,1280]{1,0:T(8,128)(2,1)}, u32[]{:S(2)}, u32[]{:S(2)}) collective-permute-start(bf16[128,1280]{1,0:T(8,128)(2,1)} %finish.5), channel_id=1, source_target_pairs={{0,12},{1,13},{2,14},{3,15},{4,8},{5,9},{6,10},{7,11},{8,4},{9,5},... | collective-permute-start | bytes 983048 | tf_op jit(solution)/shard_map/ppermute | solution.py:228
  73.0 0.1 reshape.46.refs_10_
  73.7 14.8 %collective-permute-done.12.refs_1_ = bf16[128,1280]{1,0:T(8,128)(2,1)S(1)} collective-permute-done((bf16[128,1280]{1,0:T(8,128)(2,1)S(1)}, bf16[128,1280]{1,0:T(8,128)(2,1)S(1)}, u32[]{:S(2)}, u32[]{:S(2)}) %collective-permute-start.12) | collective-permute-done | bytes 327712 | tf_op jit(solution)/shard_map/ppermute | solution.py:228
  88.5 0.8 copy-done.9
  89.3 0.0 collective-permute-done.10.refs_0_
  89.3 0.7 copy-done.7
  90.0 1.0 copy-done.8
  91.0 1.0 copy-done.10
  91.9 0.4 partial.1.refs_1_
  92.4 0.0 collective-permute-done.16.refs_7_
  92.4 0.0 collective-permute-done.15.refs_6_
  92.4 1.2 copy-done.4
  93.6 1.1 copy-done.6
  94.7 4.2 %combine.1 = (bf16[320,1280]{1,0:T(8,128)(2,1)}, bf16[4,1280]{1,0:T(4,128)(2,1)S(1)}) custom-call(s32[1]{0:T(128)S(6)} %copy.15.refs_0_, f32[320,1280]{1,0:T(8,128)S(1)} %partial.1.refs_1_, bf16[128,1280]{1,0:T(8,128)(2,1)} %collective-permute-done.14.refs_2_, bf16[128,1280]{1,0:T(8,128)(2,1)S(1)} %copy-done.4, f32[128,1]{1,0:T(8,128)S(1)} %get-tuple-element.62.refs_4_, ...), custom_call_target="tpu_custom_call" | custom-call | tf_op jit(solution)/shard_map/combine/pallas_call | solution.py:281
  98.8 0.1 collective-permute-start.17
  98.9 1.2 collective-permute-done.17
  100.1 0.3 collective-permute-start.18
  100.3 3.6 %collective-permute-done.18 = bf16[8,1280]{1,0:T(8,128)(2,1)S(1)} collective-permute-done((bf16[8,1280]{1,0:T(8,128)(2,1)S(1)}, bf16[8,1280]{1,0:T(8,128)(2,1)S(1)}, u32[]{:S(2)}, u32[]{:S(2)}) %collective-permute-start.18) | collective-permute-done | bytes 20512 | tf_op jit(solution)/shard_map/ppermute | solution.py:228
  104.0 0.2 collective-permute-start.19
  104.2 3.8 %collective-permute-done.19 = bf16[16,1280]{1,0:T(8,128)(2,1)S(1)} collective-permute-done((bf16[16,1280]{1,0:T(8,128)(2,1)S(1)}, bf16[16,1280]{1,0:T(8,128)(2,1)S(1)}, u32[]{:S(2)}, u32[]{:S(2)}) %collective-permute-start.19) | collective-permute-done | bytes 40992 | tf_op jit(solution)/shard_map/ppermute | solution.py:228
  108.0 2.2 %collective-permute-start.20 = (bf16[32,1280]{1,0:T(8,128)(2,1)S(1)}, bf16[32,1280]{1,0:T(8,128)(2,1)}, u32[]{:S(2)}, u32[]{:S(2)}) collective-permute-start(bf16[32,1280]{1,0:T(8,128)(2,1)S(1)} %pad_maximum_fusion), channel_id=1, source_target_pairs={{0,8},{1,9},{2,10},{3,11},{4,12},{5,13},{6,14},{7,15},{8,0},{9,1},... | collective-permute-start | bytes 245768 | tf_op jit(solution)/shard_map/ppermute | solution.py:228
  110.9 3.1 %collective-permute-done.20 = bf16[32,1280]{1,0:T(8,128)(2,1)} collective-permute-done((bf16[32,1280]{1,0:T(8,128)(2,1)S(1)}, bf16[32,1280]{1,0:T(8,128)(2,1)}, u32[]{:S(2)}, u32[]{:S(2)}) %collective-permute-start.20) | collective-permute-done | bytes 81952 | tf_op jit(solution)/shard_map/ppermute | solution.py:228
  114.0 0.9 concatenate.18.all_ref
  115.0 5.8 %contrast.1 = (f32[2,1280]{1,0:T(2,128)}, f32[1,1]{1,0:T(1,128)}, f32[1280,1280]{1,0:T(8,128)}) custom-call(s32[1]{0:T(128)} %bitcast.7.mine_ref, f32[1]{0:T(128)S(6)} %copy.16.scale_ref, bf16[64,1280]{1,0:T(8,128)(2,1)S(1)} %concatenate.18.all_ref, bf16[1280,1280]{1,0:T(8,128)(2,1)S(1)} %copy-done.2), custom_call_target="tpu_custom_call" | custom-call | tf_op jit(solution)/shard_map/contrast/pallas_call | solution.py:304
  (30 shorter events, 0.1 us)
Async XLA Ops:
  0.6 14.4 %collective-permute-start.2 = (bf16[1280,1280]{1,0:T(8,128)(2,1)}, bf16[1280,1280]{1,0:T(8,128)(2,1)S(1)}, u32[]{:S(2)}, u32[]{:S(2)}) collective-permute-start(bf16[1280,1280]{1,0:T(8,128)(2,1)} %bitcast.10), channel_id=1, source_target_pairs={{0,1},{1,0},{2,3},{3,2},{4,5},{5,4},{6,7},{7,6},{8,9},{9,8},{10,11... | collective-permute-start | bytes 9830408 | tf_op jit(solution)/shard_map/ppermute | solution.py:228
  1.2 13.9 %collective-permute-start.3 = (bf16[1280,1280]{1,0:T(8,128)(2,1)}, bf16[1280,1280]{1,0:T(8,128)(2,1)}, u32[]{:S(2)}, u32[]{:S(2)}) collective-permute-start(bf16[1280,1280]{1,0:T(8,128)(2,1)} %bitcast.15), channel_id=1, source_target_pairs={{0,1},{1,0},{2,3},{3,2},{4,5},{5,4},{6,7},{7,6},{8,9},{9,8},{10,11... | collective-permute-start | bytes 9830408 | tf_op jit(solution)/shard_map/ppermute | solution.py:228
  1.2 1.1 copy-start.12
  2.4 0.7 copy-start.13
  3.1 8.2 %copy-start.15 = (f32[1280]{0:T(1024)S(1)}, f32[1280]{0:T(1024)}, u32[]{:S(2)}) copy-start(f32[1280]{0:T(1024)} %param.14) | copy-start | bytes 15364
  3.1 12.0 %copy-start = (bf16[1,1280,1280]{2,1,0:T(8,128)(2,1)S(1)}, bf16[1,1280,1280]{2,1,0:T(8,128)(2,1)}, u32[]{:S(2)}) copy-start(bf16[1,1280,1280]{2,1,0:T(8,128)(2,1)} %param.16) | copy-start | bytes 9830404
  3.1 12.0 %copy-start.1 = (bf16[1,1280,1280]{2,1,0:T(8,128)(2,1)S(1)}, bf16[1,1280,1280]{2,1,0:T(8,128)(2,1)}, u32[]{:S(2)}) copy-start(bf16[1,1280,1280]{2,1,0:T(8,128)(2,1)} %param.17) | copy-start | bytes 9830404
  3.1 12.0 %copy-start.11 = (bf16[1280,4]{0,1:T(4,128)(2,1)S(1)}, bf16[1280,4]{0,1:T(4,128)(2,1)}, u32[]{:S(2)}) copy-start(bf16[1280,4]{0,1:T(4,128)(2,1)} %param.15) | copy-start | bytes 30724
  4.1 17.9 %copy-start.3 = (bf16[128,1280]{1,0:T(8,128)(2,1)}, bf16[128,1280]{1,0:T(8,128)(2,1)S(1)}, u32[]{:S(2)}) copy-start(bf16[128,1280]{1,0:T(8,128)(2,1)S(1)} %get-tuple-element.39.own_ref.refs_3_) | copy-start | bytes 983044
  4.1 11.0 %collective-permute-start.1 = (bf16[128,1280]{1,0:T(8,128)(2,1)S(1)}, bf16[128,1280]{1,0:T(8,128)(2,1)S(1)}, u32[]{:S(2)}, u32[]{:S(2)}) collective-permute-start(bf16[128,1280]{1,0:T(8,128)(2,1)S(1)} %get-tuple-element.39.own_ref.refs_3_), channel_id=1, source_target_pairs={{0,2},{1,3},{2,0},{3,1},{4,6},{5,7},{6,4},{7,5},{8,10},{9,11},{10,... | collective-permute-start | bytes 983048 | tf_op jit(solution)/shard_map/ppermute | solution.py:228
  7.1 16.3 %collective-permute-start = (bf16[128,1280]{1,0:T(8,128)(2,1)S(1)}, bf16[128,1280]{1,0:T(8,128)(2,1)S(1)}, u32[]{:S(2)}, u32[]{:S(2)}) collective-permute-start(bf16[128,1280]{1,0:T(8,128)(2,1)S(1)} %get-tuple-element.38), channel_id=1, source_target_pairs={{0,4},{1,5},{2,6},{3,7},{4,0},{5,1},{6,2},{7,3},{8,12},{9,13},{10,... | collective-permute-start | bytes 983048 | tf_op jit(solution)/shard_map/ppermute | solution.py:228
  8.7 17.1 %collective-permute-start.5 = (bf16[128,1280]{1,0:T(8,128)(2,1)S(1)}, bf16[128,1280]{1,0:T(8,128)(2,1)S(1)}, u32[]{:S(2)}, u32[]{:S(2)}) collective-permute-start(bf16[128,1280]{1,0:T(8,128)(2,1)S(1)} %get-tuple-element.46), channel_id=1, source_target_pairs={{0,8},{1,9},{2,10},{3,11},{4,12},{5,13},{6,14},{7,15},{8,0},{9,1},... | collective-permute-start | bytes 983048 | tf_op jit(solution)/shard_map/ppermute | solution.py:228
  22.0 18.1 %copy-start.5 = (f32[128,1280]{1,0:T(8,128)}, f32[128,1280]{1,0:T(8,128)S(1)}, u32[]{:S(2)}) copy-start(f32[128,1280]{1,0:T(8,128)S(1)} %get-tuple-element.63.refs_5_) | copy-start | bytes 1966084
  23.4 10.6 %collective-permute-start.4 = (bf16[128,1280]{1,0:T(8,128)(2,1)S(1)}, bf16[128,1280]{1,0:T(8,128)(2,1)S(1)}, u32[]{:S(2)}, u32[]{:S(2)}) collective-permute-start(bf16[128,1280]{1,0:T(8,128)(2,1)S(1)} %collective-permute-done.own_ref.tokens_ref), channel_id=1, source_target_pairs={{0,2},{1,3},{2,0},{3,1},{4,6},{5,7},{6,4},{7,5},{8,10},{9,11},{10,... | collective-permute-start | bytes 983048 | tf_op jit(solution)/shard_map/ppermute | solution.py:228
  25.8 14.4 %collective-permute-start.6 = (bf16[128,1280]{1,0:T(8,128)(2,1)S(1)}, bf16[128,1280]{1,0:T(8,128)(2,1)S(1)}, u32[]{:S(2)}, u32[]{:S(2)}) collective-permute-start(bf16[128,1280]{1,0:T(8,128)(2,1)S(1)} %get-tuple-element.47), channel_id=1, source_target_pairs={{0,12},{1,13},{2,14},{3,15},{4,8},{5,9},{6,10},{7,11},{8,4},{9,5},... | collective-permute-start | bytes 983048 | tf_op jit(solution)/shard_map/ppermute | solution.py:228
  28.2 14.0 %collective-permute-start.8 = (bf16[128,1280]{1,0:T(8,128)(2,1)S(1)}, bf16[128,1280]{1,0:T(8,128)(2,1)S(1)}, u32[]{:S(2)}, u32[]{:S(2)}) collective-permute-start(bf16[128,1280]{1,0:T(8,128)(2,1)S(1)} %collective-permute-done.5.own_ref.tokens_ref), channel_id=1, source_target_pairs={{0,2},{1,3},{2,0},{3,1},{4,6},{5,7},{6,4},{7,5},{8,10},{9,11},{10,... | collective-permute-start | bytes 983048 | tf_op jit(solution)/shard_map/ppermute | solution.py:228
  40.1 10.7 %collective-permute-start.7 = (bf16[128,1280]{1,0:T(8,128)(2,1)S(1)}, bf16[128,1280]{1,0:T(8,128)(2,1)S(1)}, u32[]{:S(2)}, u32[]{:S(2)}) collective-permute-start(bf16[128,1280]{1,0:T(8,128)(2,1)S(1)} %collective-permute-done.6.own_ref.tokens_ref), channel_id=1, source_target_pairs={{0,2},{1,3},{2,0},{3,1},{4,6},{5,7},{6,4},{7,5},{8,10},{9,11},{10,... | collective-permute-start | bytes 983048 | tf_op jit(solution)/shard_map/ppermute | solution.py:228
  40.6 17.3 %collective-permute-start.9 = (bf16[128,1280]{1,0:T(8,128)(2,1)S(1)}, bf16[128,1280]{1,0:T(8,128)(2,1)S(1)}, u32[]{:S(2)}, u32[]{:S(2)}) collective-permute-start(bf16[128,1280]{1,0:T(8,128)(2,1)S(1)} %get-tuple-element.48), channel_id=1, source_target_pairs={{0,2},{1,3},{2,0},{3,1},{4,6},{5,7},{6,4},{7,5},{8,10},{9,11},{10,... | collective-permute-start | bytes 983048 | tf_op jit(solution)/shard_map/ppermute | solution.py:228
  48.3 15.2 %collective-permute-start.11 = (bf16[128,1280]{1,0:T(8,128)(2,1)S(1)}, bf16[128,1280]{1,0:T(8,128)(2,1)S(1)}, u32[]{:S(2)}, u32[]{:S(2)}) collective-permute-start(bf16[128,1280]{1,0:T(8,128)(2,1)S(1)} %get-tuple-element.51), channel_id=1, source_target_pairs={{0,2},{1,3},{2,0},{3,1},{4,6},{5,7},{6,4},{7,5},{8,10},{9,11},{10,... | collective-permute-start | bytes 983048 | tf_op jit(solution)/shard_map/ppermute | solution.py:228
  57.1 15.9 %copy-start.14 = (f32[2,16,80]{2,1,0:T(8,128)S(1)}, f32[2,16,80]{2,1,0:T(8,128)}, u32[]{:S(2)}) copy-start(f32[2,16,80]{2,1,0:T(8,128)} %param.19) | copy-start | bytes 30724
  57.1 16.0 %copy-start.16 = (f32[1280]{0:T(1024)S(1)}, f32[1280]{0:T(1024)}, u32[]{:S(2)}) copy-start(f32[1280]{0:T(1024)} %param.18) | copy-start | bytes 15364
  57.1 11.0 %collective-permute-start.13 = (bf16[128,1280]{1,0:T(8,128)(2,1)S(1)}, bf16[128,1280]{1,0:T(8,128)(2,1)S(1)}, u32[]{:S(2)}, u32[]{:S(2)}) collective-permute-start(bf16[128,1280]{1,0:T(8,128)(2,1)S(1)} %get-tuple-element.53), channel_id=1, source_target_pairs={{0,2},{1,3},{2,0},{3,1},{4,6},{5,7},{6,4},{7,5},{8,10},{9,11},{10,... | collective-permute-start | bytes 983048 | tf_op jit(solution)/shard_map/ppermute | solution.py:228
  58.0 31.2 %collective-permute-start.10 = (bf16[128,1280]{1,0:T(8,128)(2,1)S(1)}, bf16[128,1280]{1,0:T(8,128)(2,1)S(1)}, u32[]{:S(2)}, u32[]{:S(2)}) collective-permute-start(bf16[128,1280]{1,0:T(8,128)(2,1)S(1)} %finish.3), channel_id=1, source_target_pairs={{0,4},{1,5},{2,6},{3,7},{4,0},{5,1},{6,2},{7,3},{8,12},{9,13},{10,... | collective-permute-start | bytes 983048 | tf_op jit(solution)/shard_map/ppermute | solution.py:228
  63.7 24.8 %collective-permute-start.12 = (bf16[128,1280]{1,0:T(8,128)(2,1)S(1)}, bf16[128,1280]{1,0:T(8,128)(2,1)S(1)}, u32[]{:S(2)}, u32[]{:S(2)}) collective-permute-start(bf16[128,1280]{1,0:T(8,128)(2,1)S(1)} %finish.4), channel_id=1, source_target_pairs={{0,8},{1,9},{2,10},{3,11},{4,12},{5,13},{6,14},{7,15},{8,0},{9,1},... | collective-permute-start | bytes 983048 | tf_op jit(solution)/shard_map/ppermute | solution.py:228
  68.9 23.4 %collective-permute-start.16 = (bf16[128,1280]{1,0:T(8,128)(2,1)}, bf16[128,1280]{1,0:T(8,128)(2,1)}, u32[]{:S(2)}, u32[]{:S(2)}) collective-permute-start(bf16[128,1280]{1,0:T(8,128)(2,1)} %get-tuple-element.66), channel_id=1, source_target_pairs={{0,2},{1,3},{2,0},{3,1},{4,6},{5,7},{6,4},{7,5},{8,10},{9,11},{10,... | collective-permute-start | bytes 983048 | tf_op jit(solution)/shard_map/ppermute | solution.py:228
  69.3 23.0 %collective-permute-start.15 = (bf16[128,1280]{1,0:T(8,128)(2,1)}, bf16[128,1280]{1,0:T(8,128)(2,1)}, u32[]{:S(2)}, u32[]{:S(2)}) collective-permute-start(bf16[128,1280]{1,0:T(8,128)(2,1)} %get-tuple-element.64), channel_id=1, source_target_pairs={{0,2},{1,3},{2,0},{3,1},{4,6},{5,7},{6,4},{7,5},{8,10},{9,11},{10,... | collective-permute-start | bytes 983048 | tf_op jit(solution)/shard_map/ppermute | solution.py:228
  71.0 21.4 %collective-permute-start.14 = (bf16[128,1280]{1,0:T(8,128)(2,1)}, bf16[128,1280]{1,0:T(8,128)(2,1)}, u32[]{:S(2)}, u32[]{:S(2)}) collective-permute-start(bf16[128,1280]{1,0:T(8,128)(2,1)} %finish.5), channel_id=1, source_target_pairs={{0,12},{1,13},{2,14},{3,15},{4,8},{5,9},{6,10},{7,11},{8,4},{9,5},... | collective-permute-start | bytes 983048 | tf_op jit(solution)/shard_map/ppermute | solution.py:228
  88.5 0.8 copy-start.9
  89.3 0.7 copy-start.7
  90.0 1.0 copy-start.8
  91.0 1.0 copy-start.10
  91.9 23.0 %copy-start.2 = (bf16[1280,1280]{1,0:T(8,128)(2,1)S(1)}, bf16[1280,1280]{1,0:T(8,128)(2,1)}, u32[]{:S(2)}) copy-start(bf16[1280,1280]{1,0:T(8,128)(2,1)} %proj_ref.1) | copy-start | bytes 9830404
  92.4 1.2 copy-start.4
  93.6 1.1 copy-start.6
  98.8 1.2 %collective-permute-start.17 = (bf16[4,1280]{1,0:T(4,128)(2,1)S(1)}, bf16[4,1280]{1,0:T(4,128)(2,1)S(1)}, u32[]{:S(2)}, u32[]{:S(2)}) collective-permute-start(bf16[4,1280]{1,0:T(4,128)(2,1)S(1)} %get-tuple-element.68), channel_id=1, source_target_pairs={{0,1},{1,0},{2,3},{3,2},{4,5},{5,4},{6,7},{7,6},{8,9},{9,8},{10,11... | collective-permute-start | bytes 30728 | tf_op jit(solution)/shard_map/ppermute | solution.py:228
  100.1 3.8 %collective-permute-start.18 = (bf16[8,1280]{1,0:T(8,128)(2,1)S(1)}, bf16[8,1280]{1,0:T(8,128)(2,1)S(1)}, u32[]{:S(2)}, u32[]{:S(2)}) collective-permute-start(bf16[8,1280]{1,0:T(8,128)(2,1)S(1)} %pad_maximum_fusion.2), channel_id=1, source_target_pairs={{0,2},{1,3},{2,0},{3,1},{4,6},{5,7},{6,4},{7,5},{8,10},{9,11},{10,... | collective-permute-start | bytes 61448 | tf_op jit(solution)/shard_map/ppermute | solution.py:228
  104.0 4.1 %collective-permute-start.19 = (bf16[16,1280]{1,0:T(8,128)(2,1)S(1)}, bf16[16,1280]{1,0:T(8,128)(2,1)S(1)}, u32[]{:S(2)}, u32[]{:S(2)}) collective-permute-start(bf16[16,1280]{1,0:T(8,128)(2,1)S(1)} %pad_maximum_fusion.1), channel_id=1, source_target_pairs={{0,4},{1,5},{2,6},{3,7},{4,0},{5,1},{6,2},{7,3},{8,12},{9,13},{10,... | collective-permute-start | bytes 122888 | tf_op jit(solution)/shard_map/ppermute | solution.py:228
  108.0 6.0 %collective-permute-start.20 = (bf16[32,1280]{1,0:T(8,128)(2,1)S(1)}, bf16[32,1280]{1,0:T(8,128)(2,1)}, u32[]{:S(2)}, u32[]{:S(2)}) collective-permute-start(bf16[32,1280]{1,0:T(8,128)(2,1)S(1)} %pad_maximum_fusion), channel_id=1, source_target_pairs={{0,8},{1,9},{2,10},{3,11},{4,12},{5,13},{6,14},{7,15},{8,0},{9,1},... | collective-permute-start | bytes 245768 | tf_op jit(solution)/shard_map/ppermute | solution.py:228

commit v3 on v2

--- a/solution.py
+++ b/solution.py
@@ -98,35 +98,47 @@
     return (iota((many, place.shape[1]), 0) + first == place).astype(F32).astype(BF16)
 
 
-def partial_kernel(*refs):
-    parts, (place_ref, sum_ref, buffer) = refs[:-3], refs[-3:]
-    cap = parts[0].shape[0]
-    for k, part in enumerate(parts):
-        buffer[k * cap : (k + 1) * cap] = part[...]
-    select = chosen(place_ref[...], cap, len(parts) * cap)
+def heads_of(shape):
+    head, feature = iota(shape, 0), iota(shape, 1)
+    return (feature >= head * HEAD_DIM) & (feature < (head + 1) * HEAD_DIM)
+
+
+def partial_kernel(early, query_ref, place_ref, *refs):
+    parts, sum_ref, rows_ref, buffer = refs[:-3], *refs[-3:]
+    cap, width = parts[0].shape
+    for at, part_ref in enumerate(parts):
+        buffer[at * cap : (at + 1) * cap] = part_ref[...]
+    place = place_ref[...]
+    select = jnp.concatenate([chosen(place, k * cap, cap) for k in early], axis=0)
     sum_ref[...] = dot(select, buffer[...], ((0,), (0,)))
-
-
-def combine_kernel(experts, *refs):
-    label_ref, sum_ref, back_ref, tokens_ref, gate_ref, kept_ref, high_ref, low_ref = refs[:8]
-    place_ref, gain_ref, query_ref, mixed_ref, pooled_ref, buffer = refs[8:]
-    cap = back_ref.shape[0]
+    feature = iota((1, width), 1)
+    inner = feature - HEAD_DIM * sum(
+        (feature >= h * HEAD_DIM).astype(jnp.int32) for h in range(1, HEADS)
+    )
+    spread = (iota((HEAD_DIM, width), 0) == inner).astype(F32).astype(BF16)
+    for modal in range(2):
+        wide = sum(dot(term, spread) for term in split3(query_ref[modal]))
+        wide = jnp.where(heads_of((HEADS, width)), wide, 0.0)
+        rows_ref[modal : modal + 1] = jnp.sum(wide, axis=0, keepdims=True)
+
+
+def combine_kernel(late, *refs):
+    label_ref, sum_ref, tokens_ref, gate_ref, kept_ref, high_ref, low_ref, place_ref = refs[:8]
+    gain_ref, query_ref, *backs, mixed_ref, pooled_ref, buffer = refs[8:]
+    cap = kept_ref.shape[0]
     rows, width = mixed_ref.shape
     finish_kernel(tokens_ref, gate_ref, kept_ref, high_ref, low_ref, buffer.at[:cap])
-    buffer[cap:] = back_ref[...]
+    for at, back_ref in enumerate(backs):
+        buffer[(at + 1) * cap : (at + 2) * cap] = back_ref[...]
     place = place_ref[...]
-    select = jnp.concatenate(
-        [chosen(place, 0, cap), chosen(place, (experts - 1) * cap, cap)], axis=0
-    )
+    select = jnp.concatenate([chosen(place, k * cap, cap) for k in [0] + late], axis=0)
     mixed = sum_ref[...] + dot(select, buffer[...], ((0,), (0,)))
     mixed_ref[...] = mixed.astype(BF16)
     z = layer_norm(mixed, gain_ref[...])
     head, feature = iota((width, HEADS), 1), iota((width, HEADS), 0)
     member = (feature >= head * HEAD_DIM) & (feature < (head + 1) * HEAD_DIM)
     member = member.astype(F32).astype(BF16)
-    head, feature = iota((HEADS, width), 0), iota((HEADS, width), 1)
-    spread = (feature >= head * HEAD_DIM) & (feature < (head + 1) * HEAD_DIM)
-    spread = spread.astype(F32).astype(BF16)
+    spread = heads_of((HEADS, width)).astype(F32).astype(BF16)
     for modal, (lower, upper) in enumerate(((0, IMG_TOK), (IMG_TOK, rows))):
         piece = z[lower:upper]
         scores = sum(dot(term, member) for term in split3(piece * query_ref[modal : modal + 1]))
@@ -139,16 +151,22 @@
 
 
 def tail_kernel(
-    pairs, mine_ref, scale_ref, all_ref, proj_ref, d_pooled_ref, loss_ref, grad_ref, store, sems
+    pairs, mine_ref, scale_ref, proj_ref, *refs
 ):
+    pieces, (d_pooled_ref, loss_ref, grad_ref, store, sems) = refs[:-5], refs[-5:]
     exact = lax.Precision.HIGHEST
     me, scale = mine_ref[0], scale_ref[0]
-    source = all_ref[...]
-    row, col = iota((2 * pairs, 4 * pairs), 0), iota((2 * pairs, 4 * pairs), 1)
-    wanted = jnp.where(row < pairs, (row ^ me) * 4, ((row - pairs) ^ me) * 4 + 1)
-    pooled = dot((col == wanted).astype(F32).astype(BF16), source).astype(BF16)
-    row, col = iota((pairs, 4 * pairs), 0), iota((pairs, 4 * pairs), 1)
-    labels = dot((col == (row ^ me) * 4 + 2).astype(F32).astype(BF16), source[:, :128])[:, :1]
+    at, pooled, labels = 0, 0.0, 0.0
+    for piece in pieces:
+        many = piece.shape[0]
+        row, col = iota((2 * pairs, many), 0), iota((2 * pairs, many), 1) + at
+        wanted = jnp.where(row < pairs, (row ^ me) * 4, ((row - pairs) ^ me) * 4 + 1)
+        pooled = pooled + dot((col == wanted).astype(F32).astype(BF16), piece[...])
+        row, col = iota((pairs, many), 0), iota((pairs, many), 1) + at
+        wanted = (col == (row ^ me) * 4 + 2).astype(F32).astype(BF16)
+        labels = labels + dot(wanted, piece[:, :128])
+        at = at + many
+    pooled, labels = pooled.astype(BF16), labels[:, :1]
     emb = dot(pooled, proj_ref[...])
     norm = jnp.sqrt(jnp.sum(emb * emb, axis=-1, keepdims=True) + 1e-06)
     unit = emb / norm
@@ -208,7 +226,7 @@
 
 
 def after(values, *others):
-    return lax.optimization_barrier((values,) + others)[0]
+    return lax.optimization_barrier((values,) + others)[0] if others else values
 
 
 def on_device(
@@ -237,79 +255,95 @@
         8,
         flops=FIRST,
     )(mine, route.reshape(1, rows), tokens.reshape(rows, width))
-    held = {k: swap(chunks[k], SPLIT * k) for k in range(1, min(experts, 3))}
-    held[0] = chunks[0]
-    parts = []
+    held = {0: chunks[0]}
+    for k in range(1, min(experts, 3)):
+        held[k] = swap(chunks[k], SPLIT * k)
+    parts, done, final = {}, [], {}
+
+    def finish(k, early=None):
+        kept, gate, leave = parts[k]
+        (final[k],) = call(finish_kernel, "finish", [((cap, width), BF16)], [VMEM] * 4, 4)(
+            held[k],
+            gate,
+            kept if early is None else after(kept, early),
+            swap(leave, 2),
+        )
+
     for k in range(experts):
+        waits = done[-1:]
         if k > 2:
-            held[k] = swap(after(chunks[k], held[k - 1], parts[0][2]), SPLIT * k)
-        partner = swap(after(held[k], parts[(k - 1) // 2][2]) if k % 2 else held[k], 2)
-        parts.append(
-            call(
-                ffn_kernel,
-                "ffn",
-                [((cap, width), F32), ((cap, 1), F32)] + [((cap, width), BF16)] * (1 if k else 2),
-                [SMEM] + [VMEM] * 8,
-                20,
-                [pltpu.VMEM((2 * cap, width), BF16), pltpu.VMEM((2, 2 * cap, ff), BF16)],
-            )(
-                mine,
-                held[k],
-                after(partner, parts[-1][2]) if k else partner,
-                moe_gain.reshape(1, width),
-                router.T,
-                *weights,
-            )
+            held[k] = swap(after(chunks[k], done[0], held[k - 1]), SPLIT * k)
+        if k < 2 and k + 1 < experts:
+            waits = waits + [held[k + 1]]
+        partner = swap(after(held[k], done[k - 1 if k > 2 else 0]) if k > 1 else held[k], 2)
+        if k == 3:
+            finish(2, early=partner)
+            waits = waits + [final[2]]
+        kept, gate, *leave = call(
+            ffn_kernel,
+            "ffn",
+            [((cap, width), F32), ((cap, 1), F32)] + [((cap, width), BF16)] * (1 if k else 2),
+            [SMEM] + [VMEM] * 8,
+            20,
+            [pltpu.VMEM((2 * cap, width), BF16), pltpu.VMEM((2, 2 * cap, ff), BF16)],
+        )(
+            mine,
+            held[k],
+            after(partner, *waits),
+            moe_gain.reshape(1, width),
+            router.T,
+            *weights,
         )
-    ready, result = {}, parts[-1][2]
-    for k in range(1, experts):
-        kept, gate, leave = parts[k]
-        (result,) = call(finish_kernel, "finish", [((cap, width), BF16)], [VMEM] * 4, 4)(
-            held[k], gate, after(kept, result), swap(leave, 2)
-        )
-        ready[k] = swap(result, SPLIT * k)
-    kept, gate, *leave = parts[0]
+        parts[k] = (kept, gate, leave[0] if k else leave)
+        done.append(leave[0])
+    finish(1)
+    early = [1, 2]
+    partial, query = call(
+        functools.partial(partial_kernel, early),
+        "partial",
+        [((rows, width), F32), ((2, width), F32)],
+        [VMEM] * 4,
+        8,
+        [pltpu.VMEM((2 * cap, width), BF16)],
+    )(pool_query, place, *[swap(final[k], SPLIT * k) for k in early])
+    for k in range(3, experts):
+        finish(k, early=partial)
+    result = final[experts - 1]
+    kept, gate, leave = parts[0]
     got = [swap(after(term, result), 2) for term in leave]
-    (partial,) = call(
-        partial_kernel,
-        "partial",
-        [((rows, width), F32)],
-        [VMEM] * (experts - 1),
-        8,
-        [pltpu.VMEM(((experts - 2) * cap, width), BF16)],
-    )(*[ready[k] for k in range(1, experts - 1)], place)
+    late = list(range(3, experts))
     mixed, pooled = call(
-        functools.partial(combine_kernel, experts),
+        functools.partial(combine_kernel, late),
         "combine",
         [((rows, width), BF16), ((4, width), BF16)],
-        [SMEM] + [VMEM] * 10,
+        [SMEM] + [VMEM] * (9 + len(late)),
         20,
-        [pltpu.VMEM((2 * cap, width), BF16)],
+        [pltpu.VMEM(((1 + len(late)) * cap, width), BF16)],
     )(
         labels,
         partial,
-        ready[experts - 1],
         held[0],
         gate,
         kept,
         *got,
         place,
         out_gain.reshape(1, width),
-        pool_query.reshape(2, width),
-    )
-    bits = 1
+        query,
+        *[swap(final[k], SPLIT * k) for k in late],
+    )
+    pieces, bits = [pooled], 1
     while bits < devices:
-        pooled = jnp.concatenate([pooled, swap(pooled, bits)], axis=0)
+        pieces.append(swap(jnp.concatenate(pieces, axis=0), bits))
         bits = bits * 2
     d_pooled, loss, grad_proj = call(
         functools.partial(tail_kernel, devices),
         "contrast",
         [((2, width), F32), ((1, 1), F32), ((width, width), F32)],
-        [SMEM] * 2 + [VMEM] * 2,
+        [SMEM] * 2 + [VMEM] * (1 + len(pieces)),
         24,
         [pltpu.VMEM((width, width), F32), pltpu.SemaphoreType.DMA((-(-width // TILE),))],
         in_hbm=1,
-    )(me.reshape(1), logit_scale, pooled, proj)
+    )(me.reshape(1), logit_scale, proj, *pieces)
     return (
         mixed.reshape(count, length, width),
         d_pooled.reshape(count, 2, width),

time: 121 us -> 118 us (0.975)
  local copies, waits for them, and re-layouts: 8.58 us -> 1.87 us
  waiting for transfers between devices: 46.6 us -> 50.2 us
  Pallas kernels: 37.8 us -> 35.2 us
  starting transfers between devices: 25.7 us -> 28 us
    unnamed x34 -> x18, local copies, waits for them, and re-layouts: 7.57 us -> 1.86 us
    ppermute x21, waiting for transfers between devices: 46.6 us -> 50.2 us  [swap(): return lax.ppermute(values, 'dp', [(i, i ^ bits) for i in range(devices)])]
    ppermute x21, starting transfers between devices: 25.7 us -> 28 us  [swap(): return lax.ppermute(values, 'dp', [(i, i ^ bits) for i in range(devices)])]
    pallas_call x5, Pallas kernels: 5.75 us -> 4.02 us  [the longest x1 2.97 us: on_device(): call(functools.partial(combine_kernel, late), 'combine', [((rows, width),...]
  transfers between devices with their start and end apart: 21 -> 21, of which waited for: 13 -> 10; matrix products, arithmetic and copies ran while one was open for 0% -> 0% of each run, Pallas kernels for 23% -> 22%
where the time goes in v3:
time: 118 us
  waiting for transfers between devices  50.2 us (43%)
  Pallas kernels  35.2 us (30%)
  starting transfers between devices  28 us (24%)
  between operations  2.29 us (2%)
  local copies, waits for them, and re-layouts  1.87 us (2%)
    ppermute x21, waiting for transfers between devices, swap(): return lax.ppermute(values, 'dp', [(i, i ^ bits) for i in range(devices)])  50.2 us
    ppermute x21, starting transfers between devices, swap(): return lax.ppermute(values, 'dp', [(i, i ^ bits) for i in range(devices)])  28 us
    pallas_call x4, Pallas kernels, on_device(): call(ffn_kernel, 'ffn', [((cap, width), F32), ((cap, 1), F32)] + [((cap,...  24.2 us
    pallas_call x1, Pallas kernels, on_device(): call(functools.partial(tail_kernel, devices), 'contrast', [((2, width), F...  5.94 us
    pallas_call x1, Pallas kernels, on_device(): call(functools.partial(combine_kernel, late), 'combine', [((rows, width),...  2.97 us
  transfers between devices with their start and end apart: 21, of which 10 were waited for; matrix products, arithmetic and copies ran while one was open for 0% of the time, Pallas kernels for 22%

profile of v3, /device:TPU:0, one launch (start us, length us, event | category | flops | bytes accessed | tf_op | source)
XLA Modules:
  0.0 117.6 jit_solution(13132518000468821428)
XLA Ops:
  0.6 0.5 collective-permute-start.3
  1.2 0.1 collective-permute-start.4
  1.2 1.1 copy-done.5
  2.4 0.7 copy-done.6
  3.1 1.0 dispatch.1
  4.1 3.1 %collective-permute-start = (bf16[128,1280]{1,0:T(8,128)(2,1)S(1)}, bf16[128,1280]{1,0:T(8,128)(2,1)S(1)}, u32[]{:S(2)}, u32[]{:S(2)}) collective-permute-start(bf16[128,1280]{1,0:T(8,128)(2,1)S(1)} %get-tuple-element.41), channel_id=1, source_target_pairs={{0,4},{1,5},{2,6},{3,7},{4,0},{5,1},{6,2},{7,3},{8,12},{9,13},{10,... | collective-permute-start | bytes 983048 | tf_op jit(solution)/shard_map/ppermute | solution.py:246
  7.1 1.5 %collective-permute-start.2 = (bf16[128,1280]{1,0:T(8,128)(2,1)S(1)}, bf16[128,1280]{1,0:T(8,128)(2,1)S(1)}, u32[]{:S(2)}, u32[]{:S(2)}) collective-permute-start(bf16[128,1280]{1,0:T(8,128)(2,1)S(1)} %get-tuple-element.42.own_ref.refs_2_), channel_id=1, source_target_pairs={{0,2},{1,3},{2,0},{3,1},{4,6},{5,7},{6,4},{7,5},{8,10},{9,11},{10,... | collective-permute-start | bytes 983048 | tf_op jit(solution)/shard_map/ppermute | solution.py:246
  8.7 2.6 %collective-permute-start.5 = (bf16[128,1280]{1,0:T(8,128)(2,1)S(1)}, bf16[128,1280]{1,0:T(8,128)(2,1)S(1)}, u32[]{:S(2)}, u32[]{:S(2)}) collective-permute-start(bf16[128,1280]{1,0:T(8,128)(2,1)S(1)} %get-tuple-element.45), channel_id=1, source_target_pairs={{0,8},{1,9},{2,10},{3,11},{4,12},{5,13},{6,14},{7,15},{8,0},{9,1},... | collective-permute-start | bytes 983048 | tf_op jit(solution)/shard_map/ppermute | solution.py:246
  11.2 0.0 copy-done.7
  11.3 9.5 %collective-permute-done.own_ref.tokens_ref = bf16[128,1280]{1,0:T(8,128)(2,1)S(1)} collective-permute-done((bf16[128,1280]{1,0:T(8,128)(2,1)S(1)}, bf16[128,1280]{1,0:T(8,128)(2,1)S(1)}, u32[]{:S(2)}, u32[]{:S(2)}) %collective-permute-start) | collective-permute-done | bytes 327712 | tf_op jit(solution)/shard_map/ppermute | solution.py:246
  20.8 0.0 collective-permute-done.2.other_ref
  20.8 2.7 %collective-permute-start.1 = (bf16[128,1280]{1,0:T(8,128)(2,1)S(1)}, bf16[128,1280]{1,0:T(8,128)(2,1)S(1)}, u32[]{:S(2)}, u32[]{:S(2)}) collective-permute-start(bf16[128,1280]{1,0:T(8,128)(2,1)S(1)} %collective-permute-done.own_ref.tokens_ref), channel_id=1, source_target_pairs={{0,2},{1,3},{2,0},{3,1},{4,6},{5,7},{6,4},{7,5},{8,10},{9,11},{10,... | collective-permute-start | bytes 983048 | tf_op jit(solution)/shard_map/ppermute | solution.py:246
  23.5 0.0 collective-permute-done.3.in_b
  23.5 0.0 collective-permute-done.4.out_b
  23.5 0.0 copy-done
  23.5 0.0 copy-done.1
  23.5 0.0 copy-done.3
  23.5 6.1 %ffn.4 = (f32[128,1280]{1,0:T(8,128)S(1)}, f32[128,1]{1,0:T(8,128)S(1)}, bf16[128,1280]{1,0:T(8,128)(2,1)S(1)}, bf16[128,1280]{1,0:T(8,128)(2,1)S(1)}) custom-call(s32[1]{0:T(128)} %bitcast.mine_ref, bf16[128,1280]{1,0:T(8,128)(2,1)S(1)} %get-tuple-element.42.own_ref.refs_2_, bf16[128,1280]{1,0:T(8,128)(2,1)S(1)} %collective-permute-done.2.other_ref, ...), custom_call_target="tpu_custom_call" | custom-call | tf_op jit(solution)/shard_map/ffn/pallas_call | solution.py:282
  29.6 0.0 collective-permute-done.5.own_ref.tokens_ref
  29.6 0.1 collective-permute-start.8
  29.7 2.5 %collective-permute-start.9 = (bf16[128,1280]{1,0:T(8,128)(2,1)S(1)}, bf16[128,1280]{1,0:T(8,128)(2,1)S(1)}, u32[]{:S(2)}, u32[]{:S(2)}) collective-permute-start(bf16[128,1280]{1,0:T(8,128)(2,1)S(1)} %get-tuple-element.55), channel_id=1, source_target_pairs={{0,12},{1,13},{2,14},{3,15},{4,8},{5,9},{6,10},{7,11},{8,4},{9,5},... | collective-permute-start | bytes 983048 | tf_op jit(solution)/shard_map/ppermute | solution.py:246
  32.2 0.0 collective-permute-done.1.other_ref
  32.2 6.1 %ffn.5 = (f32[128,1280]{1,0:T(8,128)S(1)}, f32[128,1]{1,0:T(8,128)S(1)}, bf16[128,1280]{1,0:T(8,128)(2,1)S(1)}) custom-call(s32[1]{0:T(128)} %bitcast.mine_ref, bf16[128,1280]{1,0:T(8,128)(2,1)S(1)} %collective-permute-done.own_ref.tokens_ref, bf16[128,1280]{1,0:T(8,128)(2,1)S(1)} %collective-permute-done.1.other_ref, f32[1,1280]{1,0:T(1,128)S(1)} %reshape.41.gain_ref, ...), custom_call_target="tpu_custom_call" | custom-call | tf_op jit(solution)/shard_map/ffn/pallas_call | solution.py:282
  38.2 2.0 %collective-permute-start.6 = (bf16[128,1280]{1,0:T(8,128)(2,1)S(1)}, bf16[128,1280]{1,0:T(8,128)(2,1)S(1)}, u32[]{:S(2)}, u32[]{:S(2)}) collective-permute-start(bf16[128,1280]{1,0:T(8,128)(2,1)S(1)} %get-tuple-element.49), channel_id=1, source_target_pairs={{0,2},{1,3},{2,0},{3,1},{4,6},{5,7},{6,4},{7,5},{8,10},{9,11},{10,... | collective-permute-start | bytes 983048 | tf_op jit(solution)/shard_map/ppermute | solution.py:246
  40.3 0.0 collective-permute-done.8.other_ref
  40.3 6.1 %ffn.6 = (f32[128,1280]{1,0:T(8,128)S(1)}, f32[128,1]{1,0:T(8,128)S(1)}, bf16[128,1280]{1,0:T(8,128)(2,1)S(1)}) custom-call(s32[1]{0:T(128)} %bitcast.mine_ref, bf16[128,1280]{1,0:T(8,128)(2,1)S(1)} %collective-permute-done.5.own_ref.tokens_ref, bf16[128,1280]{1,0:T(8,128)(2,1)S(1)} %collective-permute-done.8.other_ref, f32[1,1280]{1,0:T(1,128)S(1)} %reshape.41.gain_ref, ...), custom_call_target="tpu_custom_call" | custom-call | tf_op jit(solution)/shard_map/ffn/pallas_call | solution.py:282
  46.3 0.0 collective-permute-done.9.own_ref.tokens_ref
  46.3 0.1 collective-permute-start.10
  46.5 1.9 %collective-permute-start.11 = (bf16[128,1280]{1,0:T(8,128)(2,1)S(1)}, bf16[128,1280]{1,0:T(8,128)(2,1)S(1)}, u32[]{:S(2)}, u32[]{:S(2)}) collective-permute-start(bf16[128,1280]{1,0:T(8,128)(2,1)S(1)} %get-tuple-element.56), channel_id=1, source_target_pairs={{0,2},{1,3},{2,0},{3,1},{4,6},{5,7},{6,4},{7,5},{8,10},{9,11},{10,... | collective-permute-start | bytes 983048 | tf_op jit(solution)/shard_map/ppermute | solution.py:246
  48.4 0.0 collective-permute-done.6.refs_0_
  48.4 0.2 finish.3
  48.6 0.1 collective-permute-start.7
  48.7 8.4 %collective-permute-done.10.other_ref = bf16[128,1280]{1,0:T(8,128)(2,1)S(1)} collective-permute-done((bf16[128,1280]{1,0:T(8,128)(2,1)S(1)}, bf16[128,1280]{1,0:T(8,128)(2,1)S(1)}, u32[]{:S(2)}, u32[]{:S(2)}) %collective-permute-start.10) | collective-permute-done | bytes 327712 | tf_op jit(solution)/shard_map/ppermute | solution.py:246
  57.0 4.1 %collective-permute-done.11.refs_0_ = bf16[128,1280]{1,0:T(8,128)(2,1)S(1)} collective-permute-done((bf16[128,1280]{1,0:T(8,128)(2,1)S(1)}, bf16[128,1280]{1,0:T(8,128)(2,1)S(1)}, u32[]{:S(2)}, u32[]{:S(2)}) %collective-permute-start.11) | collective-permute-done | bytes 327712 | tf_op jit(solution)/shard_map/ppermute | solution.py:246
  61.2 0.2 finish.4
  61.3 0.0 copy-start.4
  61.3 0.0 copy-start.8
  61.3 0.3 collective-permute-start.12
  61.6 6.1 %ffn.7 = (f32[128,1280]{1,0:T(8,128)S(1)}, f32[128,1]{1,0:T(8,128)S(1)}, bf16[128,1280]{1,0:T(8,128)(2,1)S(1)}) custom-call(s32[1]{0:T(128)} %bitcast.mine_ref, bf16[128,1280]{1,0:T(8,128)(2,1)S(1)} %collective-permute-done.9.own_ref.tokens_ref, bf16[128,1280]{1,0:T(8,128)(2,1)S(1)} %collective-permute-done.10.other_ref, f32[1,1280]{1,0:T(1,128)S(1)} %reshape.41.gain_ref, ...), custom_call_target="tpu_custom_call" | custom-call | tf_op jit(solution)/shard_map/ffn/pallas_call | solution.py:282
  67.7 0.0 copy-start.2
  67.7 1.2 %collective-permute-start.13 = (bf16[128,1280]{1,0:T(8,128)(2,1)S(1)}, bf16[128,1280]{1,0:T(8,128)(2,1)S(1)}, u32[]{:S(2)}, u32[]{:S(2)}) collective-permute-start(bf16[128,1280]{1,0:T(8,128)(2,1)S(1)} %get-tuple-element.66), channel_id=1, source_target_pairs={{0,2},{1,3},{2,0},{3,1},{4,6},{5,7},{6,4},{7,5},{8,10},{9,11},{10,... | collective-permute-start | bytes 983048 | tf_op jit(solution)/shard_map/ppermute | solution.py:246
  68.9 0.0 collective-permute-done.7.refs_0_
  68.9 6.1 %collective-permute-done.12.refs_1_ = bf16[128,1280]{1,0:T(8,128)(2,1)S(1)} collective-permute-done((bf16[128,1280]{1,0:T(8,128)(2,1)S(1)}, bf16[128,1280]{1,0:T(8,128)(2,1)S(1)}, u32[]{:S(2)}, u32[]{:S(2)}) %collective-permute-start.12) | collective-permute-done | bytes 327712 | tf_op jit(solution)/shard_map/ppermute | solution.py:246
  75.0 0.6 partial.1
  75.5 0.0 collective-permute-done.13.refs_0_
  75.6 0.2 finish.5
  75.7 2.4 %collective-permute-start.14 = (bf16[128,1280]{1,0:T(8,128)(2,1)S(1)}, bf16[128,1280]{1,0:T(8,128)(2,1)S(1)}, u32[]{:S(2)}, u32[]{:S(2)}) collective-permute-start(bf16[128,1280]{1,0:T(8,128)(2,1)S(1)} %get-tuple-element.67), channel_id=1, source_target_pairs={{0,2},{1,3},{2,0},{3,1},{4,6},{5,7},{6,4},{7,5},{8,10},{9,11},{10,... | collective-permute-start | bytes 983048 | tf_op jit(solution)/shard_map/ppermute | solution.py:246
  78.1 0.1 collective-permute-start.15
  78.2 2.5 %collective-permute-start.16 = (bf16[128,1280]{1,0:T(8,128)(2,1)S(1)}, bf16[128,1280]{1,0:T(8,128)(2,1)S(1)}, u32[]{:S(2)}, u32[]{:S(2)}) collective-permute-start(bf16[128,1280]{1,0:T(8,128)(2,1)S(1)} %finish.5), channel_id=1, source_target_pairs={{0,12},{1,13},{2,14},{3,15},{4,8},{5,9},{6,10},{7,11},{8,4},{9,5},... | collective-permute-start | bytes 983048 | tf_op jit(solution)/shard_map/ppermute | solution.py:246
  81.3 0.0 copy-done.8
  81.3 5.3 %collective-permute-done.14.refs_5_ = bf16[128,1280]{1,0:T(8,128)(2,1)S(1)} collective-permute-done((bf16[128,1280]{1,0:T(8,128)(2,1)S(1)}, bf16[128,1280]{1,0:T(8,128)(2,1)S(1)}, u32[]{:S(2)}, u32[]{:S(2)}) %collective-permute-start.14) | collective-permute-done | bytes 327712 | tf_op jit(solution)/shard_map/ppermute | solution.py:246
  86.6 6.4 %collective-permute-done.15.refs_6_ = bf16[128,1280]{1,0:T(8,128)(2,1)S(1)} collective-permute-done((bf16[128,1280]{1,0:T(8,128)(2,1)S(1)}, bf16[128,1280]{1,0:T(8,128)(2,1)S(1)}, u32[]{:S(2)}, u32[]{:S(2)}) %collective-permute-start.15) | collective-permute-done | bytes 327712 | tf_op jit(solution)/shard_map/ppermute | solution.py:246
  93.0 0.0 collective-permute-done.16.refs_10_
  93.0 3.0 %combine.1 = (bf16[320,1280]{1,0:T(8,128)(2,1)}, bf16[4,1280]{1,0:T(4,128)(2,1)S(1)}) custom-call(s32[1]{0:T(128)S(6)} %copy.15.refs_0_, f32[320,1280]{1,0:T(8,128)S(1)} %get-tuple-element.59.refs_1_, bf16[128,1280]{1,0:T(8,128)(2,1)S(1)} %get-tuple-element.42.own_ref.refs_2_, f32[128,1]{1,0:T(8,128)S(1)} %get-tuple-element.60.refs_3_, ...), custom_call_target="tpu_custom_call" | custom-call | tf_op jit(solution)/shard_map/combine/pallas_call | solution.py:315
  96.0 0.1 collective-permute-start.17
  96.1 1.2 collective-permute-done.17.refs_1_
  97.2 1.8 %collective-permute-start.18 = (bf16[8,1280]{1,0:T(8,128)(2,1)S(1)}, bf16[8,1280]{1,0:T(8,128)(2,1)S(1)}, u32[]{:S(2)}, u32[]{:S(2)}) collective-permute-start(bf16[8,1280]{1,0:T(8,128)(2,1)S(1)} %pad_maximum_fusion.2), channel_id=1, source_target_pairs={{0,2},{1,3},{2,0},{3,1},{4,6},{5,7},{6,4},{7,5},{8,10},{9,11},{10,... | collective-permute-start | bytes 61448 | tf_op jit(solution)/shard_map/ppermute | solution.py:246
  99.1 2.0 %collective-permute-done.18.refs_2_ = bf16[8,1280]{1,0:T(8,128)(2,1)S(1)} collective-permute-done((bf16[8,1280]{1,0:T(8,128)(2,1)S(1)}, bf16[8,1280]{1,0:T(8,128)(2,1)S(1)}, u32[]{:S(2)}, u32[]{:S(2)}) %collective-permute-start.18) | collective-permute-done | bytes 20512 | tf_op jit(solution)/shard_map/ppermute | solution.py:246
  101.1 1.3 %collective-permute-start.19 = (bf16[16,1280]{1,0:T(8,128)(2,1)S(1)}, bf16[16,1280]{1,0:T(8,128)(2,1)S(1)}, u32[]{:S(2)}, u32[]{:S(2)}) collective-permute-start(bf16[16,1280]{1,0:T(8,128)(2,1)S(1)} %pad_maximum_fusion.1), channel_id=1, source_target_pairs={{0,4},{1,5},{2,6},{3,7},{4,0},{5,1},{6,2},{7,3},{8,12},{9,13},{10,... | collective-permute-start | bytes 122888 | tf_op jit(solution)/shard_map/ppermute | solution.py:246
  102.4 2.8 %collective-permute-done.19.refs_3_ = bf16[16,1280]{1,0:T(8,128)(2,1)S(1)} collective-permute-done((bf16[16,1280]{1,0:T(8,128)(2,1)S(1)}, bf16[16,1280]{1,0:T(8,128)(2,1)S(1)}, u32[]{:S(2)}, u32[]{:S(2)}) %collective-permute-start.19) | collective-permute-done | bytes 40992 | tf_op jit(solution)/shard_map/ppermute | solution.py:246
  105.2 1.1 collective-permute-start.20
  107.0 4.5 %collective-permute-done.20.refs_4_ = bf16[32,1280]{1,0:T(8,128)(2,1)S(1)} collective-permute-done((bf16[32,1280]{1,0:T(8,128)(2,1)S(1)}, bf16[32,1280]{1,0:T(8,128)(2,1)S(1)}, u32[]{:S(2)}, u32[]{:S(2)}) %collective-permute-start.20) | collective-permute-done | bytes 81952 | tf_op jit(solution)/shard_map/ppermute | solution.py:246
  111.5 0.0 copy-done.2
  111.5 5.9 %contrast.1 = (f32[2,1280]{1,0:T(2,128)}, f32[1,1]{1,0:T(1,128)}, f32[1280,1280]{1,0:T(8,128)}) custom-call(s32[1]{0:T(128)} %bitcast.7.mine_ref, f32[1]{0:T(128)S(6)} %copy.16.scale_ref, bf16[1280,1280]{1,0:T(8,128)(2,1)S(1)} %copy-done.2, bf16[4,1280]{1,0:T(4,128)(2,1)S(1)} %get-tuple-element.72.refs_0_, ...), custom_call_target="tpu_custom_call" | custom-call | tf_op jit(solution)/shard_map/contrast/pallas_call | solution.py:338
  (12 shorter events, 0.1 us)
Async XLA Ops:
  0.6 22.8 %collective-permute-start.3 = (bf16[1280,1280]{1,0:T(8,128)(2,1)}, bf16[1280,1280]{1,0:T(8,128)(2,1)S(1)}, u32[]{:S(2)}, u32[]{:S(2)}) collective-permute-start(bf16[1280,1280]{1,0:T(8,128)(2,1)} %bitcast.10), channel_id=1, source_target_pairs={{0,1},{1,0},{2,3},{3,2},{4,5},{5,4},{6,7},{7,6},{8,9},{9,8},{10,11... | collective-permute-start | bytes 9830408 | tf_op jit(solution)/shard_map/ppermute | solution.py:246
  1.2 22.3 %collective-permute-start.4 = (bf16[1280,1280]{1,0:T(8,128)(2,1)}, bf16[1280,1280]{1,0:T(8,128)(2,1)}, u32[]{:S(2)}, u32[]{:S(2)}) collective-permute-start(bf16[1280,1280]{1,0:T(8,128)(2,1)} %bitcast.15), channel_id=1, source_target_pairs={{0,1},{1,0},{2,3},{3,2},{4,5},{5,4},{6,7},{7,6},{8,9},{9,8},{10,11... | collective-permute-start | bytes 9830408 | tf_op jit(solution)/shard_map/ppermute | solution.py:246
  1.2 1.1 copy-start.5
  2.4 0.7 copy-start.6
  3.1 8.2 %copy-start.7 = (f32[1280]{0:T(1024)S(1)}, f32[1280]{0:T(1024)}, u32[]{:S(2)}) copy-start(f32[1280]{0:T(1024)} %param.14) | copy-start | bytes 15364
  3.1 20.4 %copy-start = (bf16[1,1280,1280]{2,1,0:T(8,128)(2,1)S(1)}, bf16[1,1280,1280]{2,1,0:T(8,128)(2,1)}, u32[]{:S(2)}) copy-start(bf16[1,1280,1280]{2,1,0:T(8,128)(2,1)} %param.16) | copy-start | bytes 9830404
  3.1 20.4 %copy-start.1 = (bf16[1,1280,1280]{2,1,0:T(8,128)(2,1)S(1)}, bf16[1,1280,1280]{2,1,0:T(8,128)(2,1)}, u32[]{:S(2)}) copy-start(bf16[1,1280,1280]{2,1,0:T(8,128)(2,1)} %param.17) | copy-start | bytes 9830404
  3.1 20.4 %copy-start.3 = (bf16[1280,4]{0,1:T(4,128)(2,1)S(1)}, bf16[1280,4]{0,1:T(4,128)(2,1)}, u32[]{:S(2)}) copy-start(bf16[1280,4]{0,1:T(4,128)(2,1)} %param.15) | copy-start | bytes 30724
  4.1 16.7 %collective-permute-start = (bf16[128,1280]{1,0:T(8,128)(2,1)S(1)}, bf16[128,1280]{1,0:T(8,128)(2,1)S(1)}, u32[]{:S(2)}, u32[]{:S(2)}) collective-permute-start(bf16[128,1280]{1,0:T(8,128)(2,1)S(1)} %get-tuple-element.41), channel_id=1, source_target_pairs={{0,4},{1,5},{2,6},{3,7},{4,0},{5,1},{6,2},{7,3},{8,12},{9,13},{10,... | collective-permute-start | bytes 983048 | tf_op jit(solution)/shard_map/ppermute | solution.py:246
  7.1 13.6 %collective-permute-start.2 = (bf16[128,1280]{1,0:T(8,128)(2,1)S(1)}, bf16[128,1280]{1,0:T(8,128)(2,1)S(1)}, u32[]{:S(2)}, u32[]{:S(2)}) collective-permute-start(bf16[128,1280]{1,0:T(8,128)(2,1)S(1)} %get-tuple-element.42.own_ref.refs_2_), channel_id=1, source_target_pairs={{0,2},{1,3},{2,0},{3,1},{4,6},{5,7},{6,4},{7,5},{8,10},{9,11},{10,... | collective-permute-start | bytes 983048 | tf_op jit(solution)/shard_map/ppermute | solution.py:246
  8.7 20.9 %collective-permute-start.5 = (bf16[128,1280]{1,0:T(8,128)(2,1)S(1)}, bf16[128,1280]{1,0:T(8,128)(2,1)S(1)}, u32[]{:S(2)}, u32[]{:S(2)}) collective-permute-start(bf16[128,1280]{1,0:T(8,128)(2,1)S(1)} %get-tuple-element.45), channel_id=1, source_target_pairs={{0,8},{1,9},{2,10},{3,11},{4,12},{5,13},{6,14},{7,15},{8,0},{9,1},... | collective-permute-start | bytes 983048 | tf_op jit(solution)/shard_map/ppermute | solution.py:246
  20.8 11.4 %collective-permute-start.1 = (bf16[128,1280]{1,0:T(8,128)(2,1)S(1)}, bf16[128,1280]{1,0:T(8,128)(2,1)S(1)}, u32[]{:S(2)}, u32[]{:S(2)}) collective-permute-start(bf16[128,1280]{1,0:T(8,128)(2,1)S(1)} %collective-permute-done.own_ref.tokens_ref), channel_id=1, source_target_pairs={{0,2},{1,3},{2,0},{3,1},{4,6},{5,7},{6,4},{7,5},{8,10},{9,11},{10,... | collective-permute-start | bytes 983048 | tf_op jit(solution)/shard_map/ppermute | solution.py:246
  29.6 10.7 %collective-permute-start.8 = (bf16[128,1280]{1,0:T(8,128)(2,1)S(1)}, bf16[128,1280]{1,0:T(8,128)(2,1)S(1)}, u32[]{:S(2)}, u32[]{:S(2)}) collective-permute-start(bf16[128,1280]{1,0:T(8,128)(2,1)S(1)} %collective-permute-done.5.own_ref.tokens_ref), channel_id=1, source_target_pairs={{0,2},{1,3},{2,0},{3,1},{4,6},{5,7},{6,4},{7,5},{8,10},{9,11},{10,... | collective-permute-start | bytes 983048 | tf_op jit(solution)/shard_map/ppermute | solution.py:246
  29.7 16.7 %collective-permute-start.9 = (bf16[128,1280]{1,0:T(8,128)(2,1)S(1)}, bf16[128,1280]{1,0:T(8,128)(2,1)S(1)}, u32[]{:S(2)}, u32[]{:S(2)}) collective-permute-start(bf16[128,1280]{1,0:T(8,128)(2,1)S(1)} %get-tuple-element.55), channel_id=1, source_target_pairs={{0,12},{1,13},{2,14},{3,15},{4,8},{5,9},{6,10},{7,11},{8,4},{9,5},... | collective-permute-start | bytes 983048 | tf_op jit(solution)/shard_map/ppermute | solution.py:246
  38.2 10.2 %collective-permute-start.6 = (bf16[128,1280]{1,0:T(8,128)(2,1)S(1)}, bf16[128,1280]{1,0:T(8,128)(2,1)S(1)}, u32[]{:S(2)}, u32[]{:S(2)}) collective-permute-start(bf16[128,1280]{1,0:T(8,128)(2,1)S(1)} %get-tuple-element.49), channel_id=1, source_target_pairs={{0,2},{1,3},{2,0},{3,1},{4,6},{5,7},{6,4},{7,5},{8,10},{9,11},{10,... | collective-permute-start | bytes 983048 | tf_op jit(solution)/shard_map/ppermute | solution.py:246
  46.3 10.7 %collective-permute-start.10 = (bf16[128,1280]{1,0:T(8,128)(2,1)S(1)}, bf16[128,1280]{1,0:T(8,128)(2,1)S(1)}, u32[]{:S(2)}, u32[]{:S(2)}) collective-permute-start(bf16[128,1280]{1,0:T(8,128)(2,1)S(1)} %collective-permute-done.9.own_ref.tokens_ref), channel_id=1, source_target_pairs={{0,2},{1,3},{2,0},{3,1},{4,6},{5,7},{6,4},{7,5},{8,10},{9,11},{10,... | collective-permute-start | bytes 983048 | tf_op jit(solution)/shard_map/ppermute | solution.py:246
  46.5 14.7 %collective-permute-start.11 = (bf16[128,1280]{1,0:T(8,128)(2,1)S(1)}, bf16[128,1280]{1,0:T(8,128)(2,1)S(1)}, u32[]{:S(2)}, u32[]{:S(2)}) collective-permute-start(bf16[128,1280]{1,0:T(8,128)(2,1)S(1)} %get-tuple-element.56), channel_id=1, source_target_pairs={{0,2},{1,3},{2,0},{3,1},{4,6},{5,7},{6,4},{7,5},{8,10},{9,11},{10,... | collective-permute-start | bytes 983048 | tf_op jit(solution)/shard_map/ppermute | solution.py:246
  48.6 20.3 %collective-permute-start.7 = (bf16[128,1280]{1,0:T(8,128)(2,1)S(1)}, bf16[128,1280]{1,0:T(8,128)(2,1)S(1)}, u32[]{:S(2)}, u32[]{:S(2)}) collective-permute-start(bf16[128,1280]{1,0:T(8,128)(2,1)S(1)} %finish.3), channel_id=1, source_target_pairs={{0,4},{1,5},{2,6},{3,7},{4,0},{5,1},{6,2},{7,3},{8,12},{9,13},{10,... | collective-permute-start | bytes 983048 | tf_op jit(solution)/shard_map/ppermute | solution.py:246
  61.3 13.6 %copy-start.4 = (f32[2,16,80]{2,1,0:T(8,128)S(1)}, f32[2,16,80]{2,1,0:T(8,128)}, u32[]{:S(2)}) copy-start(f32[2,16,80]{2,1,0:T(8,128)} %query_ref.1) | copy-start | bytes 30724
  61.3 20.0 %copy-start.8 = (f32[1280]{0:T(1024)S(1)}, f32[1280]{0:T(1024)}, u32[]{:S(2)}) copy-start(f32[1280]{0:T(1024)} %param.18) | copy-start | bytes 15364
  61.3 13.6 %collective-permute-start.12 = (bf16[128,1280]{1,0:T(8,128)(2,1)S(1)}, bf16[128,1280]{1,0:T(8,128)(2,1)S(1)}, u32[]{:S(2)}, u32[]{:S(2)}) collective-permute-start(bf16[128,1280]{1,0:T(8,128)(2,1)S(1)} %finish.4), channel_id=1, source_target_pairs={{0,8},{1,9},{2,10},{3,11},{4,12},{5,13},{6,14},{7,15},{8,0},{9,1},... | collective-permute-start | bytes 983048 | tf_op jit(solution)/shard_map/ppermute | solution.py:246
  67.7 43.8 %copy-start.2 = (bf16[1280,1280]{1,0:T(8,128)(2,1)S(1)}, bf16[1280,1280]{1,0:T(8,128)(2,1)}, u32[]{:S(2)}) copy-start(bf16[1280,1280]{1,0:T(8,128)(2,1)} %proj_ref.1) | copy-start | bytes 9830404
  67.7 7.9 %collective-permute-start.13 = (bf16[128,1280]{1,0:T(8,128)(2,1)S(1)}, bf16[128,1280]{1,0:T(8,128)(2,1)S(1)}, u32[]{:S(2)}, u32[]{:S(2)}) collective-permute-start(bf16[128,1280]{1,0:T(8,128)(2,1)S(1)} %get-tuple-element.66), channel_id=1, source_target_pairs={{0,2},{1,3},{2,0},{3,1},{4,6},{5,7},{6,4},{7,5},{8,10},{9,11},{10,... | collective-permute-start | bytes 983048 | tf_op jit(solution)/shard_map/ppermute | solution.py:246
  75.7 10.9 %collective-permute-start.14 = (bf16[128,1280]{1,0:T(8,128)(2,1)S(1)}, bf16[128,1280]{1,0:T(8,128)(2,1)S(1)}, u32[]{:S(2)}, u32[]{:S(2)}) collective-permute-start(bf16[128,1280]{1,0:T(8,128)(2,1)S(1)} %get-tuple-element.67), channel_id=1, source_target_pairs={{0,2},{1,3},{2,0},{3,1},{4,6},{5,7},{6,4},{7,5},{8,10},{9,11},{10,... | collective-permute-start | bytes 983048 | tf_op jit(solution)/shard_map/ppermute | solution.py:246
  78.1 14.9 %collective-permute-start.15 = (bf16[128,1280]{1,0:T(8,128)(2,1)S(1)}, bf16[128,1280]{1,0:T(8,128)(2,1)S(1)}, u32[]{:S(2)}, u32[]{:S(2)}) collective-permute-start(bf16[128,1280]{1,0:T(8,128)(2,1)S(1)} %get-tuple-element.69), channel_id=1, source_target_pairs={{0,2},{1,3},{2,0},{3,1},{4,6},{5,7},{6,4},{7,5},{8,10},{9,11},{10,... | collective-permute-start | bytes 983048 | tf_op jit(solution)/shard_map/ppermute | solution.py:246
  78.2 14.8 %collective-permute-start.16 = (bf16[128,1280]{1,0:T(8,128)(2,1)S(1)}, bf16[128,1280]{1,0:T(8,128)(2,1)S(1)}, u32[]{:S(2)}, u32[]{:S(2)}) collective-permute-start(bf16[128,1280]{1,0:T(8,128)(2,1)S(1)} %finish.5), channel_id=1, source_target_pairs={{0,12},{1,13},{2,14},{3,15},{4,8},{5,9},{6,10},{7,11},{8,4},{9,5},... | collective-permute-start | bytes 983048 | tf_op jit(solution)/shard_map/ppermute | solution.py:246
  96.0 1.2 %collective-permute-start.17 = (bf16[4,1280]{1,0:T(4,128)(2,1)S(1)}, bf16[4,1280]{1,0:T(4,128)(2,1)S(1)}, u32[]{:S(2)}, u32[]{:S(2)}) collective-permute-start(bf16[4,1280]{1,0:T(4,128)(2,1)S(1)} %get-tuple-element.72.refs_0_), channel_id=1, source_target_pairs={{0,1},{1,0},{2,3},{3,2},{4,5},{5,4},{6,7},{7,6},{8,9},{9,8},{10,11... | collective-permute-start | bytes 30728 | tf_op jit(solution)/shard_map/ppermute | solution.py:246
  97.2 3.8 %collective-permute-start.18 = (bf16[8,1280]{1,0:T(8,128)(2,1)S(1)}, bf16[8,1280]{1,0:T(8,128)(2,1)S(1)}, u32[]{:S(2)}, u32[]{:S(2)}) collective-permute-start(bf16[8,1280]{1,0:T(8,128)(2,1)S(1)} %pad_maximum_fusion.2), channel_id=1, source_target_pairs={{0,2},{1,3},{2,0},{3,1},{4,6},{5,7},{6,4},{7,5},{8,10},{9,11},{10,... | collective-permute-start | bytes 61448 | tf_op jit(solution)/shard_map/ppermute | solution.py:246
  101.1 4.1 %collective-permute-start.19 = (bf16[16,1280]{1,0:T(8,128)(2,1)S(1)}, bf16[16,1280]{1,0:T(8,128)(2,1)S(1)}, u32[]{:S(2)}, u32[]{:S(2)}) collective-permute-start(bf16[16,1280]{1,0:T(8,128)(2,1)S(1)} %pad_maximum_fusion.1), channel_id=1, source_target_pairs={{0,4},{1,5},{2,6},{3,7},{4,0},{5,1},{6,2},{7,3},{8,12},{9,13},{10,... | collective-permute-start | bytes 122888 | tf_op jit(solution)/shard_map/ppermute | solution.py:246
  105.2 6.3 %collective-permute-start.20 = (bf16[32,1280]{1,0:T(8,128)(2,1)S(1)}, bf16[32,1280]{1,0:T(8,128)(2,1)S(1)}, u32[]{:S(2)}, u32[]{:S(2)}) collective-permute-start(bf16[32,1280]{1,0:T(8,128)(2,1)S(1)} %pad_maximum_fusion), channel_id=1, source_target_pairs={{0,8},{1,9},{2,10},{3,11},{4,12},{5,13},{6,14},{7,15},{8,0},{9,1},... | collective-permute-start | bytes 245768 | tf_op jit(solution)/shard_map/ppermute | solution.py:246

commit v4 on v3

--- a/solution.py
+++ b/solution.py
@@ -54,7 +54,7 @@
     earlier = (iota((rows, rows), 0) <= iota((rows, rows), 1)).astype(F32).astype(BF16)
     count = dot(onehot.astype(BF16), earlier)
     slot = jnp.sum((count - 1.0) * onehot, axis=0, keepdims=True).astype(jnp.int32)
-    place = (ids ^ mine_ref[0]) * cap + slot
+    place = (ids ^ (mine_ref[0] // SPLIT)) * cap + slot
     place_ref[...] = place
     select = (iota((experts * cap, rows), 0) == place).astype(F32).astype(BF16)
     buffer = dot(select, tokens_ref[...]).astype(BF16)
@@ -62,35 +62,39 @@
         chunks[k][...] = buffer[k * cap : (k + 1) * cap]
 
 
-def ffn_kernel(mine_ref, own_ref, other_ref, gain_ref, router_ref, in_a, out_a, in_b, out_b, *outs):
-    kept_ref, gate_ref, *sent_refs, x_ref, hidden_ref = outs
-    cap = own_ref.shape[0]
-    gain = gain_ref[...]
-    own = layer_norm(own_ref[...].astype(F32), gain).astype(BF16)
-    x_ref[:cap] = own
-    x_ref[cap:] = layer_norm(other_ref[...].astype(F32), gain).astype(BF16)
+def ffn_kernel(own, mine_ref, rows_ref, gain_ref, router_ref, in_a, out_a, in_b, out_b, *outs):
+    *outs, x_ref, hidden_ref = outs
+    normed = layer_norm(rows_ref[...].astype(F32), gain_ref[...]).astype(BF16)
+    x_ref[...] = normed
     ff, width = out_a.shape
     for index, w_in in enumerate((in_a, in_b)):
         for at in range(0, ff, TILE):
             pre = dot(x_ref[...], w_in[:, at : at + TILE])
             hidden_ref[index, :, at : at + TILE] = jax.nn.gelu(pre, approximate=True).astype(BF16)
-    router = router_ref[...].astype(F32)
-    column = jnp.where(iota(router.shape, 0) == mine_ref[0], router, 0.0)
-    column = jnp.sum(column, axis=0, keepdims=True)
-    gate_ref[...] = jax.nn.sigmoid(jnp.sum(own.astype(F32) * column, axis=1, keepdims=True))
+    if own:
+        router = router_ref[...].astype(F32)
+        column = jnp.where(iota(router.shape, 0) == mine_ref[0] // SPLIT, router, 0.0)
+        column = jnp.sum(column, axis=0, keepdims=True)
+        gate = jnp.sum(normed.astype(F32) * column, axis=1, keepdims=True)
+        outs[1][...] = jax.nn.sigmoid(gate)
     for at in range(0, width, TILE):
         total = None
         for index, w_out in enumerate((out_a, out_b)):
             part = dot(hidden_ref[index], w_out[:, at : at + TILE]).astype(BF16).astype(F32)
             total = part if total is None else total + part
-        kept_ref[:, at : at + TILE] = total[:cap]
-        for sent_ref, term in zip(sent_refs, split3(total[cap:])):
-            sent_ref[:, at : at + TILE] = term
+        if own:
+            outs[0][:, at : at + TILE] = total
+        else:
+            for out_ref, term in zip(outs, split3(total)):
+                out_ref[:, at : at + TILE] = term[: out_ref.shape[0]]
 
 
 def finish_kernel(tokens_ref, gate_ref, kept_ref, *refs):
-    got_refs, mixed_ref = refs[:-1], refs[-1]
-    total = kept_ref[...] + sum(got_ref[...].astype(F32) for got_ref in got_refs)
+    got_ref, *low_refs, mixed_ref = refs
+    total = kept_ref[...] + got_ref[...].astype(F32)
+    for low_ref in low_refs:
+        many = low_ref.shape[0]
+        total = jnp.concatenate([total[:many] + low_ref[...].astype(F32), total[many:]], axis=0)
     mixed_ref[...] = (tokens_ref[...].astype(F32) + gate_ref[...] * total).astype(BF16)
 
 
@@ -240,13 +244,13 @@
     cap = -(-capacity // 16) * 16
     ff = w_in.shape[2]
     me = lax.axis_index("dp").astype(jnp.int32)
-    mine = (me // SPLIT).reshape(1)
+    mine = me.reshape(1)
 
     def swap(values, bits):
         return lax.ppermute(values, "dp", [(i, i ^ bits) for i in range(devices)])
 
     weights = [w_in[0], w_out[0]]
-    weights = weights + [swap(w, 1) for w in weights]
+    weights = weights + [swap(after(w, mine), 1) for w in weights]
     *chunks, place = call(
         functools.partial(dispatch_kernel, experts, cap),
         "dispatch",
@@ -255,48 +259,49 @@
         8,
         flops=FIRST,
     )(mine, route.reshape(1, rows), tokens.reshape(rows, width))
-    held = {0: chunks[0]}
-    for k in range(1, min(experts, 3)):
+    def expert(own, values, terms, *others):
+        outs = [((cap // (n + 1), width), BF16) for n in range(terms)]
+        if own:
+            outs = [((cap, width), F32), ((cap, 1), F32)]
+        return call(
+            functools.partial(ffn_kernel, own),
+            "own" if own else "other",
+            outs,
+            [SMEM] + [VMEM] * 7,
+            18,
+            [pltpu.VMEM((cap, width), BF16), pltpu.VMEM((2, cap, ff), BF16)],
+        )(mine, after(values, *others), moe_gain.reshape(1, width), router.T, *weights)
+
+    def finish(k, *others):
+        kept, gate = owns[k]
+        (final[k],) = call(finish_kernel, "finish", [((cap, width), BF16)], [VMEM] * 4, 4)(
+            held[k], gate, after(kept, *others), swap(lefts[k][0], 2)
+        )
+
+    held, owns, lefts, final = {0: chunks[0]}, {}, {}, {}
+    for k in (1, 2):
         held[k] = swap(chunks[k], SPLIT * k)
-    parts, done, final = {}, [], {}
-
-    def finish(k, early=None):
-        kept, gate, leave = parts[k]
-        (final[k],) = call(finish_kernel, "finish", [((cap, width), BF16)], [VMEM] * 4, 4)(
-            held[k],
-            gate,
-            kept if early is None else after(kept, early),
-            swap(leave, 2),
-        )
-
-    for k in range(experts):
-        waits = done[-1:]
-        if k > 2:
-            held[k] = swap(after(chunks[k], done[0], held[k - 1]), SPLIT * k)
-        if k < 2 and k + 1 < experts:
-            waits = waits + [held[k + 1]]
-        partner = swap(after(held[k], done[k - 1 if k > 2 else 0]) if k > 1 else held[k], 2)
-        if k == 3:
-            finish(2, early=partner)
-            waits = waits + [final[2]]
-        kept, gate, *leave = call(
-            ffn_kernel,
-            "ffn",
-            [((cap, width), F32), ((cap, 1), F32)] + [((cap, width), BF16)] * (1 if k else 2),
-            [SMEM] + [VMEM] * 8,
-            20,
-            [pltpu.VMEM((2 * cap, width), BF16), pltpu.VMEM((2, 2 * cap, ff), BF16)],
-        )(
-            mine,
-            held[k],
-            after(partner, *waits),
-            moe_gain.reshape(1, width),
-            router.T,
-            *weights,
-        )
-        parts[k] = (kept, gate, leave[0] if k else leave)
-        done.append(leave[0])
-    finish(1)
+    partner = {0: swap(held[0], 2)}
+    owns[0] = expert(True, held[0], 0)
+    partner[1] = swap(after(held[1], owns[0][0]), 2)
+    owns[1] = expert(True, held[1], 0, partner[1], held[2], partner[0])
+    partner[2] = swap(after(held[2], owns[0][0]), 2)
+    lefts[1] = expert(False, partner[1], 1, owns[1][0])
+    owns[2] = expert(True, held[2], 0, lefts[1][0])
+    lefts[2] = expert(False, partner[2], 1, owns[2][0])
+    finish(1, lefts[2][0])
+    last = final[1]
+    for k in range(3, experts):
+        held[k] = swap(after(chunks[k], held[k - 1]), SPLIT * k)
+        partner[k] = swap(after(held[k], lefts[2][0]), 2)
+        owns[k] = expert(True, held[k], 0, last)
+        last = owns[k][0]
+    finish(2, last)
+    last = final[2]
+    for k in range(3, experts):
+        lefts[k] = expert(False, partner[k], 1, last)
+        last = lefts[k][0]
+    lefts[0] = expert(False, partner[0], 2, last)
     early = [1, 2]
     partial, query = call(
         functools.partial(partial_kernel, early),
@@ -307,10 +312,9 @@
         [pltpu.VMEM((2 * cap, width), BF16)],
     )(pool_query, place, *[swap(final[k], SPLIT * k) for k in early])
     for k in range(3, experts):
-        finish(k, early=partial)
-    result = final[experts - 1]
-    kept, gate, leave = parts[0]
-    got = [swap(after(term, result), 2) for term in leave]
+        finish(k, partial)
+    kept, gate = owns[0]
+    got = [swap(after(term, partial), 2) for term in lefts[0]]
     late = list(range(3, experts))
     mixed, pooled = call(
         functools.partial(combine_kernel, late),
@@ -343,7 +347,7 @@
         24,
         [pltpu.VMEM((width, width), F32), pltpu.SemaphoreType.DMA((-(-width // TILE),))],
         in_hbm=1,
-    )(me.reshape(1), logit_scale, proj, *pieces)
+    )(mine, logit_scale, proj, *pieces)
     return (
         mixed.reshape(count, length, width),
         d_pooled.reshape(count, 2, width),

time: 118 us -> 104 us (0.88)
  waiting for transfers between devices: 50.2 us -> 37.9 us
  Pallas kernels: 35.2 us -> 30.1 us
  starting transfers between devices: 28 us -> 31.8 us
    ppermute x21, waiting for transfers between devices: 50.2 us -> 37.9 us  [swap(): return lax.ppermute(values, 'dp', [(i, i ^ bits) for i in range(devices)])]
    pallas_call x4 -> x8, Pallas kernels: 24.2 us -> 18.9 us  [expert(): call(functools.partial(ffn_kernel, own), 'own' if own else 'other', outs,...]
    ppermute x21, starting transfers between devices: 28 us -> 31.8 us  [swap(): return lax.ppermute(values, 'dp', [(i, i ^ bits) for i in range(devices)])]
  transfers between devices with their start and end apart: 21 -> 21, of which waited for: 10 -> 14; matrix products, arithmetic and copies ran while one was open for 0% -> 0% of each run, Pallas kernels for 22% -> 20%
where the time goes in v4:
time: 104 us
  waiting for transfers between devices  37.9 us (36%)
  starting transfers between devices  31.8 us (31%)
  Pallas kernels  30.1 us (29%)
  between operations  2.3 us (2%)
  local copies, waits for them, and re-layouts  1.87 us (2%)
    ppermute x21, waiting for transfers between devices, swap(): return lax.ppermute(values, 'dp', [(i, i ^ bits) for i in range(devices)])  37.9 us
    ppermute x21, starting transfers between devices, swap(): return lax.ppermute(values, 'dp', [(i, i ^ bits) for i in range(devices)])  31.8 us
    pallas_call x8, Pallas kernels, expert(): call(functools.partial(ffn_kernel, own), 'own' if own else 'other', outs,...  18.9 us
    pallas_call x1, Pallas kernels, on_device(): call(functools.partial(tail_kernel, devices), 'contrast', [((2, width), F...  5.94 us
    pallas_call x1, Pallas kernels, on_device(): call(functools.partial(combine_kernel, late), 'combine', [((rows, width),...  2.95 us
  transfers between devices with their start and end apart: 21, of which 14 were waited for; matrix products, arithmetic and copies ran while one was open for 0% of the time, Pallas kernels for 20%

profile of v4, /device:TPU:0, one launch (start us, length us, event | category | flops | bytes accessed | tf_op | source)
XLA Modules:
  0.0 104.1 jit_solution(18147575071419681731)
XLA Ops:
  0.6 0.5 collective-permute-start.2
  1.2 0.1 collective-permute-start.1
  1.2 1.1 %copy-done.5 = bf16[1,320,1280]{2,1,0:T(8,128)(2,1)S(1)} copy-done((bf16[1,320,1280]{2,1,0:T(8,128)(2,1)S(1)}, bf16[1,320,1280]{2,1,0:T(8,128)(2,1)}, u32[]{:S(2)}) %copy-start.5) | copy-done | bytes 819224
  2.4 0.7 copy-done.6
  3.1 1.0 dispatch.1
  4.1 3.1 %collective-permute-start = (bf16[128,1280]{1,0:T(8,128)(2,1)S(1)}, bf16[128,1280]{1,0:T(8,128)(2,1)S(1)}, u32[]{:S(2)}, u32[]{:S(2)}) collective-permute-start(bf16[128,1280]{1,0:T(8,128)(2,1)S(1)} %get-tuple-element.45), channel_id=1, source_target_pairs={{0,4},{1,5},{2,6},{3,7},{4,0},{5,1},{6,2},{7,3},{8,12},{9,13},{10,... | collective-permute-start | bytes 983048 | tf_op jit(solution)/shard_map/ppermute | solution.py:250
  7.1 2.6 %collective-permute-start.4 = (bf16[128,1280]{1,0:T(8,128)(2,1)S(1)}, bf16[128,1280]{1,0:T(8,128)(2,1)S(1)}, u32[]{:S(2)}, u32[]{:S(2)}) collective-permute-start(bf16[128,1280]{1,0:T(8,128)(2,1)S(1)} %get-tuple-element.51), channel_id=1, source_target_pairs={{0,8},{1,9},{2,10},{3,11},{4,12},{5,13},{6,14},{7,15},{8,0},{9,1},... | collective-permute-start | bytes 983048 | tf_op jit(solution)/shard_map/ppermute | solution.py:250
  9.7 1.5 %collective-permute-start.5 = (bf16[128,1280]{1,0:T(8,128)(2,1)S(1)}, bf16[128,1280]{1,0:T(8,128)(2,1)S(1)}, u32[]{:S(2)}, u32[]{:S(2)}) collective-permute-start(bf16[128,1280]{1,0:T(8,128)(2,1)S(1)} %get-tuple-element.46.rows_ref.refs_2_), channel_id=1, source_target_pairs={{0,2},{1,3},{2,0},{3,1},{4,6},{5,7},{6,4},{7,5},{8,10},{9,11},{10,... | collective-permute-start | bytes 983048 | tf_op jit(solution)/shard_map/ppermute | solution.py:250
  11.3 0.0 collective-permute-done.2.out_b
  11.3 0.3 collective-permute-done.1.in_b
  11.5 0.0 copy-done.1
  11.5 2.4 %own.4 = (f32[128,1280]{1,0:T(8,128)S(1)}, f32[128,1]{1,0:T(8,128)S(1)}) custom-call(s32[1]{0:T(128)} %bitcast.mine_ref, bf16[128,1280]{1,0:T(8,128)(2,1)S(1)} %get-tuple-element.46.rows_ref.refs_2_, f32[1,1280]{1,0:T(1,128)S(1)} %reshape.42.gain_ref, bf16[4,1280]{1,0:T(4,128)(2,1)S(1)} %bitcast.27, bf16[1280,1280]{1,0:T(8,128)(2,1)S(1)} %bitcast.10, ...), custom_call_target="tpu_custom_call" | custom-call | tf_op jit(solution)/shard_map/own/pallas_call | solution.py:266
  13.9 8.1 %collective-permute-done.rows_ref.tokens_ref = bf16[128,1280]{1,0:T(8,128)(2,1)S(1)} collective-permute-done((bf16[128,1280]{1,0:T(8,128)(2,1)S(1)}, bf16[128,1280]{1,0:T(8,128)(2,1)S(1)}, u32[]{:S(2)}, u32[]{:S(2)}) %collective-permute-start) | collective-permute-done | bytes 327712 | tf_op jit(solution)/shard_map/ppermute | solution.py:250
  22.0 1.7 %collective-permute-start.3 = (bf16[128,1280]{1,0:T(8,128)(2,1)S(1)}, bf16[128,1280]{1,0:T(8,128)(2,1)S(1)}, u32[]{:S(2)}, u32[]{:S(2)}) collective-permute-start(bf16[128,1280]{1,0:T(8,128)(2,1)S(1)} %collective-permute-done.rows_ref.tokens_ref), channel_id=1, source_target_pairs={{0,2},{1,3},{2,0},{3,1},{4,6},{5,7},{6,4},{7,5},{8,10},{9,11},{10,... | collective-permute-start | bytes 983048 | tf_op jit(solution)/shard_map/ppermute | solution.py:250
  23.7 0.8 collective-permute-done.4.rows_ref.tokens_ref
  24.5 1.5 %collective-permute-start.6 = (bf16[128,1280]{1,0:T(8,128)(2,1)S(1)}, bf16[128,1280]{1,0:T(8,128)(2,1)S(1)}, u32[]{:S(2)}, u32[]{:S(2)}) collective-permute-start(bf16[128,1280]{1,0:T(8,128)(2,1)S(1)} %collective-permute-done.4.rows_ref.tokens_ref), channel_id=1, source_target_pairs={{0,2},{1,3},{2,0},{3,1},{4,6},{5,7},{6,4},{7,5},{8,10},{9,11},{10,... | collective-permute-start | bytes 983048 | tf_op jit(solution)/shard_map/ppermute | solution.py:250
  26.0 2.5 %collective-permute-start.9 = (bf16[128,1280]{1,0:T(8,128)(2,1)S(1)}, bf16[128,1280]{1,0:T(8,128)(2,1)S(1)}, u32[]{:S(2)}, u32[]{:S(2)}) collective-permute-start(bf16[128,1280]{1,0:T(8,128)(2,1)S(1)} %get-tuple-element.63), channel_id=1, source_target_pairs={{0,12},{1,13},{2,14},{3,15},{4,8},{5,9},{6,10},{7,11},{8,4},{9,5},... | collective-permute-start | bytes 983048 | tf_op jit(solution)/shard_map/ppermute | solution.py:250
  28.5 0.0 collective-permute-done.5.rows_ref
  28.5 4.1 %collective-permute-done.3.rows_ref = bf16[128,1280]{1,0:T(8,128)(2,1)S(1)} collective-permute-done((bf16[128,1280]{1,0:T(8,128)(2,1)S(1)}, bf16[128,1280]{1,0:T(8,128)(2,1)S(1)}, u32[]{:S(2)}, u32[]{:S(2)}) %collective-permute-start.3) | collective-permute-done | bytes 327712 | tf_op jit(solution)/shard_map/ppermute | solution.py:250
  32.6 2.4 %own.5 = (f32[128,1280]{1,0:T(8,128)S(1)}, f32[128,1]{1,0:T(8,128)S(1)}) custom-call(s32[1]{0:T(128)} %bitcast.mine_ref, bf16[128,1280]{1,0:T(8,128)(2,1)S(1)} %collective-permute-done.rows_ref.tokens_ref, f32[1,1280]{1,0:T(1,128)S(1)} %reshape.42.gain_ref, bf16[4,1280]{1,0:T(4,128)(2,1)S(1)} %bitcast.28, bf16[1280,1280]{1,0:T(8,128)(2,1)S(1)} %bitcast.11, ...), custom_call_target="tpu_custom_call" | custom-call | tf_op jit(solution)/shard_map/own/pallas_call | solution.py:266
  35.0 2.3 %other.4 = bf16[128,1280]{1,0:T(8,128)(2,1)S(1)} custom-call(s32[1]{0:T(128)} %bitcast.mine_ref, bf16[128,1280]{1,0:T(8,128)(2,1)S(1)} %collective-permute-done.3.rows_ref, f32[1,1280]{1,0:T(1,128)S(1)} %reshape.42.gain_ref, bf16[4,1280]{1,0:T(4,128)(2,1)S(1)} %bitcast.29, bf16[1280,1280]{1,0:T(8,128)(2,1)S(1)} %bitcast.12, bf16[1280,1280]{1,0:T(8,128)(2,1)S(1)} %bitcast.21, ...), custom_call_target="tpu_custom_call" | custom-call | tf_op jit(solution)/shard_map/other/pallas_call | solution.py:266
  37.4 1.8 %collective-permute-start.7 = (bf16[128,1280]{1,0:T(8,128)(2,1)S(1)}, bf16[128,1280]{1,0:T(8,128)(2,1)S(1)}, u32[]{:S(2)}, u32[]{:S(2)}) collective-permute-start(bf16[128,1280]{1,0:T(8,128)(2,1)S(1)} %other.4), channel_id=1, source_target_pairs={{0,2},{1,3},{2,0},{3,1},{4,6},{5,7},{6,4},{7,5},{8,10},{9,11},{10,... | collective-permute-start | bytes 983048 | tf_op jit(solution)/shard_map/ppermute | solution.py:250
  39.1 2.4 %own.6 = (f32[128,1280]{1,0:T(8,128)S(1)}, f32[128,1]{1,0:T(8,128)S(1)}) custom-call(s32[1]{0:T(128)} %bitcast.mine_ref, bf16[128,1280]{1,0:T(8,128)(2,1)S(1)} %collective-permute-done.4.rows_ref.tokens_ref, f32[1,1280]{1,0:T(1,128)S(1)} %reshape.42.gain_ref, bf16[4,1280]{1,0:T(4,128)(2,1)S(1)} %bitcast.30, bf16[1280,1280]{1,0:T(8,128)(2,1)S(1)} %bitcast.13, ...), custom_call_target="tpu_custom_call" | custom-call | tf_op jit(solution)/shard_map/own/pallas_call | solution.py:266
  41.6 0.0 collective-permute-done.6.rows_ref
  41.6 2.3 %other.5 = bf16[128,1280]{1,0:T(8,128)(2,1)S(1)} custom-call(s32[1]{0:T(128)} %bitcast.mine_ref, bf16[128,1280]{1,0:T(8,128)(2,1)S(1)} %collective-permute-done.6.rows_ref, f32[1,1280]{1,0:T(1,128)S(1)} %reshape.42.gain_ref, bf16[4,1280]{1,0:T(4,128)(2,1)S(1)} %bitcast.31, bf16[1280,1280]{1,0:T(8,128)(2,1)S(1)} %bitcast.14, bf16[1280,1280]{1,0:T(8,128)(2,1)S(1)} %bitcast.23, ...), custom_call_target="tpu_custom_call" | custom-call | tf_op jit(solution)/shard_map/other/pallas_call | solution.py:266
  43.9 0.4 collective-permute-start.10
  44.3 0.0 collective-permute-done.9.rows_ref.tokens_ref
  44.3 1.7 %collective-permute-start.12 = (bf16[128,1280]{1,0:T(8,128)(2,1)S(1)}, bf16[128,1280]{1,0:T(8,128)(2,1)S(1)}, u32[]{:S(2)}, u32[]{:S(2)}) collective-permute-start(bf16[128,1280]{1,0:T(8,128)(2,1)S(1)} %collective-permute-done.9.rows_ref.tokens_ref), channel_id=1, source_target_pairs={{0,2},{1,3},{2,0},{3,1},{4,6},{5,7},{6,4},{7,5},{8,10},{9,11},{10,... | collective-permute-start | bytes 983048 | tf_op jit(solution)/shard_map/ppermute | solution.py:250
  46.0 1.6 %collective-permute-done.7.refs_0_ = bf16[128,1280]{1,0:T(8,128)(2,1)S(1)} collective-permute-done((bf16[128,1280]{1,0:T(8,128)(2,1)S(1)}, bf16[128,1280]{1,0:T(8,128)(2,1)S(1)}, u32[]{:S(2)}, u32[]{:S(2)}) %collective-permute-start.7) | collective-permute-done | bytes 327712 | tf_op jit(solution)/shard_map/ppermute | solution.py:250
  47.6 0.3 finish.3
  47.9 0.1 collective-permute-start.8
  48.0 2.4 %own.7 = (f32[128,1280]{1,0:T(8,128)S(1)}, f32[128,1]{1,0:T(8,128)S(1)}) custom-call(s32[1]{0:T(128)} %bitcast.mine_ref, bf16[128,1280]{1,0:T(8,128)(2,1)S(1)} %collective-permute-done.9.rows_ref.tokens_ref, f32[1,1280]{1,0:T(1,128)S(1)} %reshape.42.gain_ref, bf16[4,1280]{1,0:T(4,128)(2,1)S(1)} %bitcast.32, bf16[1280,1280]{1,0:T(8,128)(2,1)S(1)} %bitcast.15, ...), custom_call_target="tpu_custom_call" | custom-call | tf_op jit(solution)/shard_map/own/pallas_call | solution.py:266
  50.4 4.2 %collective-permute-done.10.refs_0_ = bf16[128,1280]{1,0:T(8,128)(2,1)S(1)} collective-permute-done((bf16[128,1280]{1,0:T(8,128)(2,1)S(1)}, bf16[128,1280]{1,0:T(8,128)(2,1)S(1)}, u32[]{:S(2)}, u32[]{:S(2)}) %collective-permute-start.10) | collective-permute-done | bytes 327712 | tf_op jit(solution)/shard_map/ppermute | solution.py:250
  54.6 0.2 finish.4
  54.8 0.6 collective-permute-start.11
  55.4 3.9 %collective-permute-done.12.rows_ref = bf16[128,1280]{1,0:T(8,128)(2,1)S(1)} collective-permute-done((bf16[128,1280]{1,0:T(8,128)(2,1)S(1)}, bf16[128,1280]{1,0:T(8,128)(2,1)S(1)}, u32[]{:S(2)}, u32[]{:S(2)}) %collective-permute-start.12) | collective-permute-done | bytes 327712 | tf_op jit(solution)/shard_map/ppermute | solution.py:250
  59.3 2.3 %other.6 = bf16[128,1280]{1,0:T(8,128)(2,1)S(1)} custom-call(s32[1]{0:T(128)} %bitcast.mine_ref, bf16[128,1280]{1,0:T(8,128)(2,1)S(1)} %collective-permute-done.12.rows_ref, f32[1,1280]{1,0:T(1,128)S(1)} %reshape.42.gain_ref, bf16[4,1280]{1,0:T(4,128)(2,1)S(1)} %bitcast.33, bf16[1280,1280]{1,0:T(8,128)(2,1)S(1)} %bitcast.16, ...), custom_call_target="tpu_custom_call" | custom-call | tf_op jit(solution)/shard_map/other/pallas_call | solution.py:266
  61.6 0.0 copy-start.4
  61.6 0.0 copy-start.8
  61.6 1.4 %collective-permute-start.15 = (bf16[128,1280]{1,0:T(8,128)(2,1)S(1)}, bf16[128,1280]{1,0:T(8,128)(2,1)S(1)}, u32[]{:S(2)}, u32[]{:S(2)}) collective-permute-start(bf16[128,1280]{1,0:T(8,128)(2,1)S(1)} %other.6), channel_id=1, source_target_pairs={{0,2},{1,3},{2,0},{3,1},{4,6},{5,7},{6,4},{7,5},{8,10},{9,11},{10,... | collective-permute-start | bytes 983048 | tf_op jit(solution)/shard_map/ppermute | solution.py:250
  63.0 2.3 %other.7 = (bf16[128,1280]{1,0:T(8,128)(2,1)S(1)}, bf16[64,1280]{1,0:T(8,128)(2,1)S(1)}) custom-call(s32[1]{0:T(128)} %bitcast.mine_ref, bf16[128,1280]{1,0:T(8,128)(2,1)S(1)} %collective-permute-done.5.rows_ref, f32[1,1280]{1,0:T(1,128)S(1)} %reshape.42.gain_ref, bf16[4,1280]{1,0:T(4,128)(2,1)S(1)} %bitcast.34, bf16[1280,1280]{1,0:T(8,128)(2,1)S(1)} %bitcast.17, ...), custom_call_target="tpu_custom_call" | custom-call | tf_op jit(solution)/shard_map/other/pallas_call | solution.py:266
  65.4 0.0 copy-start.2
  65.4 0.0 collective-permute-done.8.refs_0_
  65.4 2.1 %collective-permute-done.11.refs_1_ = bf16[128,1280]{1,0:T(8,128)(2,1)S(1)} collective-permute-done((bf16[128,1280]{1,0:T(8,128)(2,1)S(1)}, bf16[128,1280]{1,0:T(8,128)(2,1)S(1)}, u32[]{:S(2)}, u32[]{:S(2)}) %collective-permute-start.11) | collective-permute-done | bytes 327712 | tf_op jit(solution)/shard_map/ppermute | solution.py:250
  67.5 0.6 partial.1
  68.1 0.8 collective-permute-start.13
  69.0 0.1 collective-permute-done.15.refs_0_
  69.0 0.2 finish.5
  69.2 2.5 %collective-permute-start.16 = (bf16[128,1280]{1,0:T(8,128)(2,1)S(1)}, bf16[128,1280]{1,0:T(8,128)(2,1)S(1)}, u32[]{:S(2)}, u32[]{:S(2)}) collective-permute-start(bf16[128,1280]{1,0:T(8,128)(2,1)S(1)} %finish.5), channel_id=1, source_target_pairs={{0,12},{1,13},{2,14},{3,15},{4,8},{5,9},{6,10},{7,11},{8,4},{9,5},... | collective-permute-start | bytes 983048 | tf_op jit(solution)/shard_map/ppermute | solution.py:250
  71.7 2.5 %collective-permute-start.14 = (bf16[64,1280]{1,0:T(8,128)(2,1)S(1)}, bf16[64,1280]{1,0:T(8,128)(2,1)S(1)}, u32[]{:S(2)}, u32[]{:S(2)}) collective-permute-start(bf16[64,1280]{1,0:T(8,128)(2,1)S(1)} %get-tuple-element.75), channel_id=1, source_target_pairs={{0,2},{1,3},{2,0},{3,1},{4,6},{5,7},{6,4},{7,5},{8,10},{9,11},{10,... | collective-permute-start | bytes 491528 | tf_op jit(solution)/shard_map/ppermute | solution.py:250
  74.8 4.7 %collective-permute-done.14.refs_6_ = bf16[64,1280]{1,0:T(8,128)(2,1)S(1)} collective-permute-done((bf16[64,1280]{1,0:T(8,128)(2,1)S(1)}, bf16[64,1280]{1,0:T(8,128)(2,1)S(1)}, u32[]{:S(2)}, u32[]{:S(2)}) %collective-permute-start.14) | collective-permute-done | bytes 163872 | tf_op jit(solution)/shard_map/ppermute | solution.py:250
  79.6 0.0 collective-permute-done.13.refs_5_
  79.6 0.0 collective-permute-done.16.refs_10_
  79.6 2.9 %combine.1 = (bf16[320,1280]{1,0:T(8,128)(2,1)}, bf16[4,1280]{1,0:T(4,128)(2,1)S(1)}) custom-call(s32[1]{0:T(128)S(6)} %copy.15.refs_0_, f32[320,1280]{1,0:T(8,128)S(1)} %get-tuple-element.67.refs_1_, bf16[128,1280]{1,0:T(8,128)(2,1)S(1)} %get-tuple-element.46.rows_ref.refs_2_, f32[128,1]{1,0:T(8,128)S(1)} %get-tuple-element.68.refs_3_, ...), custom_call_target="tpu_custom_call" | custom-call | tf_op jit(solution)/shard_map/combine/pallas_call | solution.py:319
  82.5 0.1 collective-permute-start.17
  82.6 1.2 %collective-permute-done.17.refs_1_ = bf16[4,1280]{1,0:T(4,128)(2,1)S(1)} collective-permute-done((bf16[4,1280]{1,0:T(4,128)(2,1)S(1)}, bf16[4,1280]{1,0:T(4,128)(2,1)S(1)}, u32[]{:S(2)}, u32[]{:S(2)}) %collective-permute-start.17) | collective-permute-done | bytes 10272 | tf_op jit(solution)/shard_map/ppermute | solution.py:250
  83.8 1.1 %collective-permute-start.18 = (bf16[8,1280]{1,0:T(8,128)(2,1)S(1)}, bf16[8,1280]{1,0:T(8,128)(2,1)S(1)}, u32[]{:S(2)}, u32[]{:S(2)}) collective-permute-start(bf16[8,1280]{1,0:T(8,128)(2,1)S(1)} %pad_maximum_fusion.2), channel_id=1, source_target_pairs={{0,2},{1,3},{2,0},{3,1},{4,6},{5,7},{6,4},{7,5},{8,10},{9,11},{10,... | collective-permute-start | bytes 61448 | tf_op jit(solution)/shard_map/ppermute | solution.py:250
  84.9 2.7 %collective-permute-done.18.refs_2_ = bf16[8,1280]{1,0:T(8,128)(2,1)S(1)} collective-permute-done((bf16[8,1280]{1,0:T(8,128)(2,1)S(1)}, bf16[8,1280]{1,0:T(8,128)(2,1)S(1)}, u32[]{:S(2)}, u32[]{:S(2)}) %collective-permute-start.18) | collective-permute-done | bytes 20512 | tf_op jit(solution)/shard_map/ppermute | solution.py:250
  87.7 2.9 %collective-permute-start.19 = (bf16[16,1280]{1,0:T(8,128)(2,1)S(1)}, bf16[16,1280]{1,0:T(8,128)(2,1)S(1)}, u32[]{:S(2)}, u32[]{:S(2)}) collective-permute-start(bf16[16,1280]{1,0:T(8,128)(2,1)S(1)} %pad_maximum_fusion.1), channel_id=1, source_target_pairs={{0,4},{1,5},{2,6},{3,7},{4,0},{5,1},{6,2},{7,3},{8,12},{9,13},{10,... | collective-permute-start | bytes 122888 | tf_op jit(solution)/shard_map/ppermute | solution.py:250
  90.5 2.0 %collective-permute-done.19.refs_3_ = bf16[16,1280]{1,0:T(8,128)(2,1)S(1)} collective-permute-done((bf16[16,1280]{1,0:T(8,128)(2,1)S(1)}, bf16[16,1280]{1,0:T(8,128)(2,1)S(1)}, u32[]{:S(2)}, u32[]{:S(2)}) %collective-permute-start.19) | collective-permute-done | bytes 40992 | tf_op jit(solution)/shard_map/ppermute | solution.py:250
  92.6 2.5 %collective-permute-start.20 = (bf16[32,1280]{1,0:T(8,128)(2,1)S(1)}, bf16[32,1280]{1,0:T(8,128)(2,1)S(1)}, u32[]{:S(2)}, u32[]{:S(2)}) collective-permute-start(bf16[32,1280]{1,0:T(8,128)(2,1)S(1)} %pad_maximum_fusion), channel_id=1, source_target_pairs={{0,8},{1,9},{2,10},{3,11},{4,12},{5,13},{6,14},{7,15},{8,0},{9,1},... | collective-permute-start | bytes 245768 | tf_op jit(solution)/shard_map/ppermute | solution.py:250
  95.7 2.2 %collective-permute-done.20.refs_4_ = bf16[32,1280]{1,0:T(8,128)(2,1)S(1)} collective-permute-done((bf16[32,1280]{1,0:T(8,128)(2,1)S(1)}, bf16[32,1280]{1,0:T(8,128)(2,1)S(1)}, u32[]{:S(2)}, u32[]{:S(2)}) %collective-permute-start.20) | collective-permute-done | bytes 81952 | tf_op jit(solution)/shard_map/ppermute | solution.py:250
  98.0 0.0 copy-done.2
  98.0 5.9 %contrast.1 = (f32[2,1280]{1,0:T(2,128)}, f32[1,1]{1,0:T(1,128)}, f32[1280,1280]{1,0:T(8,128)}) custom-call(s32[1]{0:T(128)} %bitcast.mine_ref, f32[1]{0:T(128)S(6)} %copy.16.scale_ref, bf16[1280,1280]{1,0:T(8,128)(2,1)S(1)} %copy-done.2, bf16[4,1280]{1,0:T(4,128)(2,1)S(1)} %get-tuple-element.80.refs_0_, ...), custom_call_target="tpu_custom_call" | custom-call | tf_op jit(solution)/shard_map/contrast/pallas_call | solution.py:342
  (16 shorter events, 0.1 us)
Async XLA Ops:
  0.6 10.6 %collective-permute-start.2 = (bf16[1280,1280]{1,0:T(8,128)(2,1)}, bf16[1280,1280]{1,0:T(8,128)(2,1)S(1)}, u32[]{:S(2)}, u32[]{:S(2)}) collective-permute-start(bf16[1280,1280]{1,0:T(8,128)(2,1)} %bitcast.18), channel_id=1, source_target_pairs={{0,1},{1,0},{2,3},{3,2},{4,5},{5,4},{6,7},{7,6},{8,9},{9,8},{10,11... | collective-permute-start | bytes 9830408 | tf_op jit(solution)/shard_map/ppermute | solution.py:250
  1.2 10.4 %collective-permute-start.1 = (bf16[1280,1280]{1,0:T(8,128)(2,1)}, bf16[1280,1280]{1,0:T(8,128)(2,1)S(1)}, u32[]{:S(2)}, u32[]{:S(2)}) collective-permute-start(bf16[1280,1280]{1,0:T(8,128)(2,1)} %bitcast.9), channel_id=1, source_target_pairs={{0,1},{1,0},{2,3},{3,2},{4,5},{5,4},{6,7},{7,6},{8,9},{9,8},{10,11... | collective-permute-start | bytes 9830408 | tf_op jit(solution)/shard_map/ppermute | solution.py:250
  1.2 1.1 %copy-start.5 = (bf16[1,320,1280]{2,1,0:T(8,128)(2,1)S(1)}, bf16[1,320,1280]{2,1,0:T(8,128)(2,1)}, u32[]{:S(2)}) copy-start(bf16[1,320,1280]{2,1,0:T(8,128)(2,1)} %param.11) | copy-start | bytes 2457604
  2.4 0.7 copy-start.6
  3.1 8.2 %copy-start.7 = (f32[1280]{0:T(1024)S(1)}, f32[1280]{0:T(1024)}, u32[]{:S(2)}) copy-start(f32[1280]{0:T(1024)} %param.14) | copy-start | bytes 15364
  3.1 8.5 %copy-start = (bf16[1,1280,1280]{2,1,0:T(8,128)(2,1)S(1)}, bf16[1,1280,1280]{2,1,0:T(8,128)(2,1)}, u32[]{:S(2)}) copy-start(bf16[1,1280,1280]{2,1,0:T(8,128)(2,1)} %param.16) | copy-start | bytes 9830404
  3.1 8.5 %copy-start.1 = (bf16[1,1280,1280]{2,1,0:T(8,128)(2,1)S(1)}, bf16[1,1280,1280]{2,1,0:T(8,128)(2,1)}, u32[]{:S(2)}) copy-start(bf16[1,1280,1280]{2,1,0:T(8,128)(2,1)} %param.17) | copy-start | bytes 9830404
  3.1 8.5 %copy-start.3 = (bf16[1280,4]{0,1:T(4,128)(2,1)S(1)}, bf16[1280,4]{0,1:T(4,128)(2,1)}, u32[]{:S(2)}) copy-start(bf16[1280,4]{0,1:T(4,128)(2,1)} %param.15) | copy-start | bytes 30724
  4.1 17.9 %collective-permute-start = (bf16[128,1280]{1,0:T(8,128)(2,1)S(1)}, bf16[128,1280]{1,0:T(8,128)(2,1)S(1)}, u32[]{:S(2)}, u32[]{:S(2)}) collective-permute-start(bf16[128,1280]{1,0:T(8,128)(2,1)S(1)} %get-tuple-element.45), channel_id=1, source_target_pairs={{0,4},{1,5},{2,6},{3,7},{4,0},{5,1},{6,2},{7,3},{8,12},{9,13},{10,... | collective-permute-start | bytes 983048 | tf_op jit(solution)/shard_map/ppermute | solution.py:250
  7.1 17.4 %collective-permute-start.4 = (bf16[128,1280]{1,0:T(8,128)(2,1)S(1)}, bf16[128,1280]{1,0:T(8,128)(2,1)S(1)}, u32[]{:S(2)}, u32[]{:S(2)}) collective-permute-start(bf16[128,1280]{1,0:T(8,128)(2,1)S(1)} %get-tuple-element.51), channel_id=1, source_target_pairs={{0,8},{1,9},{2,10},{3,11},{4,12},{5,13},{6,14},{7,15},{8,0},{9,1},... | collective-permute-start | bytes 983048 | tf_op jit(solution)/shard_map/ppermute | solution.py:250
  9.7 18.8 %collective-permute-start.5 = (bf16[128,1280]{1,0:T(8,128)(2,1)S(1)}, bf16[128,1280]{1,0:T(8,128)(2,1)S(1)}, u32[]{:S(2)}, u32[]{:S(2)}) collective-permute-start(bf16[128,1280]{1,0:T(8,128)(2,1)S(1)} %get-tuple-element.46.rows_ref.refs_2_), channel_id=1, source_target_pairs={{0,2},{1,3},{2,0},{3,1},{4,6},{5,7},{6,4},{7,5},{8,10},{9,11},{10,... | collective-permute-start | bytes 983048 | tf_op jit(solution)/shard_map/ppermute | solution.py:250
  22.0 10.6 %collective-permute-start.3 = (bf16[128,1280]{1,0:T(8,128)(2,1)S(1)}, bf16[128,1280]{1,0:T(8,128)(2,1)S(1)}, u32[]{:S(2)}, u32[]{:S(2)}) collective-permute-start(bf16[128,1280]{1,0:T(8,128)(2,1)S(1)} %collective-permute-done.rows_ref.tokens_ref), channel_id=1, source_target_pairs={{0,2},{1,3},{2,0},{3,1},{4,6},{5,7},{6,4},{7,5},{8,10},{9,11},{10,... | collective-permute-start | bytes 983048 | tf_op jit(solution)/shard_map/ppermute | solution.py:250
  24.5 17.0 %collective-permute-start.6 = (bf16[128,1280]{1,0:T(8,128)(2,1)S(1)}, bf16[128,1280]{1,0:T(8,128)(2,1)S(1)}, u32[]{:S(2)}, u32[]{:S(2)}) collective-permute-start(bf16[128,1280]{1,0:T(8,128)(2,1)S(1)} %collective-permute-done.4.rows_ref.tokens_ref), channel_id=1, source_target_pairs={{0,2},{1,3},{2,0},{3,1},{4,6},{5,7},{6,4},{7,5},{8,10},{9,11},{10,... | collective-permute-start | bytes 983048 | tf_op jit(solution)/shard_map/ppermute | solution.py:250
  26.0 18.3 %collective-permute-start.9 = (bf16[128,1280]{1,0:T(8,128)(2,1)S(1)}, bf16[128,1280]{1,0:T(8,128)(2,1)S(1)}, u32[]{:S(2)}, u32[]{:S(2)}) collective-permute-start(bf16[128,1280]{1,0:T(8,128)(2,1)S(1)} %get-tuple-element.63), channel_id=1, source_target_pairs={{0,12},{1,13},{2,14},{3,15},{4,8},{5,9},{6,10},{7,11},{8,4},{9,5},... | collective-permute-start | bytes 983048 | tf_op jit(solution)/shard_map/ppermute | solution.py:250
  37.4 10.2 %collective-permute-start.7 = (bf16[128,1280]{1,0:T(8,128)(2,1)S(1)}, bf16[128,1280]{1,0:T(8,128)(2,1)S(1)}, u32[]{:S(2)}, u32[]{:S(2)}) collective-permute-start(bf16[128,1280]{1,0:T(8,128)(2,1)S(1)} %other.4), channel_id=1, source_target_pairs={{0,2},{1,3},{2,0},{3,1},{4,6},{5,7},{6,4},{7,5},{8,10},{9,11},{10,... | collective-permute-start | bytes 983048 | tf_op jit(solution)/shard_map/ppermute | solution.py:250
  43.9 10.7 %collective-permute-start.10 = (bf16[128,1280]{1,0:T(8,128)(2,1)S(1)}, bf16[128,1280]{1,0:T(8,128)(2,1)S(1)}, u32[]{:S(2)}, u32[]{:S(2)}) collective-permute-start(bf16[128,1280]{1,0:T(8,128)(2,1)S(1)} %other.5), channel_id=1, source_target_pairs={{0,2},{1,3},{2,0},{3,1},{4,6},{5,7},{6,4},{7,5},{8,10},{9,11},{10,... | collective-permute-start | bytes 983048 | tf_op jit(solution)/shard_map/ppermute | solution.py:250
  44.3 15.0 %collective-permute-start.12 = (bf16[128,1280]{1,0:T(8,128)(2,1)S(1)}, bf16[128,1280]{1,0:T(8,128)(2,1)S(1)}, u32[]{:S(2)}, u32[]{:S(2)}) collective-permute-start(bf16[128,1280]{1,0:T(8,128)(2,1)S(1)} %collective-permute-done.9.rows_ref.tokens_ref), channel_id=1, source_target_pairs={{0,2},{1,3},{2,0},{3,1},{4,6},{5,7},{6,4},{7,5},{8,10},{9,11},{10,... | collective-permute-start | bytes 983048 | tf_op jit(solution)/shard_map/ppermute | solution.py:250
  47.9 17.5 %collective-permute-start.8 = (bf16[128,1280]{1,0:T(8,128)(2,1)S(1)}, bf16[128,1280]{1,0:T(8,128)(2,1)S(1)}, u32[]{:S(2)}, u32[]{:S(2)}) collective-permute-start(bf16[128,1280]{1,0:T(8,128)(2,1)S(1)} %finish.3), channel_id=1, source_target_pairs={{0,4},{1,5},{2,6},{3,7},{4,0},{5,1},{6,2},{7,3},{8,12},{9,13},{10,... | collective-permute-start | bytes 983048 | tf_op jit(solution)/shard_map/ppermute | solution.py:250
  54.8 12.8 %collective-permute-start.11 = (bf16[128,1280]{1,0:T(8,128)(2,1)S(1)}, bf16[128,1280]{1,0:T(8,128)(2,1)S(1)}, u32[]{:S(2)}, u32[]{:S(2)}) collective-permute-start(bf16[128,1280]{1,0:T(8,128)(2,1)S(1)} %finish.4), channel_id=1, source_target_pairs={{0,8},{1,9},{2,10},{3,11},{4,12},{5,13},{6,14},{7,15},{8,0},{9,1},... | collective-permute-start | bytes 983048 | tf_op jit(solution)/shard_map/ppermute | solution.py:250
  61.6 6.0 %copy-start.4 = (f32[2,16,80]{2,1,0:T(8,128)S(1)}, f32[2,16,80]{2,1,0:T(8,128)}, u32[]{:S(2)}) copy-start(f32[2,16,80]{2,1,0:T(8,128)} %query_ref.1) | copy-start | bytes 30724
  61.6 13.2 %copy-start.8 = (f32[1280]{0:T(1024)S(1)}, f32[1280]{0:T(1024)}, u32[]{:S(2)}) copy-start(f32[1280]{0:T(1024)} %param.18) | copy-start | bytes 15364
  61.6 7.4 %collective-permute-start.15 = (bf16[128,1280]{1,0:T(8,128)(2,1)S(1)}, bf16[128,1280]{1,0:T(8,128)(2,1)S(1)}, u32[]{:S(2)}, u32[]{:S(2)}) collective-permute-start(bf16[128,1280]{1,0:T(8,128)(2,1)S(1)} %other.6), channel_id=1, source_target_pairs={{0,2},{1,3},{2,0},{3,1},{4,6},{5,7},{6,4},{7,5},{8,10},{9,11},{10,... | collective-permute-start | bytes 983048 | tf_op jit(solution)/shard_map/ppermute | solution.py:250
  65.4 32.6 %copy-start.2 = (bf16[1280,1280]{1,0:T(8,128)(2,1)S(1)}, bf16[1280,1280]{1,0:T(8,128)(2,1)}, u32[]{:S(2)}) copy-start(bf16[1280,1280]{1,0:T(8,128)(2,1)} %proj_ref.1) | copy-start | bytes 9830404
  68.1 11.4 %collective-permute-start.13 = (bf16[128,1280]{1,0:T(8,128)(2,1)S(1)}, bf16[128,1280]{1,0:T(8,128)(2,1)S(1)}, u32[]{:S(2)}, u32[]{:S(2)}) collective-permute-start(bf16[128,1280]{1,0:T(8,128)(2,1)S(1)} %get-tuple-element.73), channel_id=1, source_target_pairs={{0,2},{1,3},{2,0},{3,1},{4,6},{5,7},{6,4},{7,5},{8,10},{9,11},{10,... | collective-permute-start | bytes 983048 | tf_op jit(solution)/shard_map/ppermute | solution.py:250
  69.2 10.4 %collective-permute-start.16 = (bf16[128,1280]{1,0:T(8,128)(2,1)S(1)}, bf16[128,1280]{1,0:T(8,128)(2,1)S(1)}, u32[]{:S(2)}, u32[]{:S(2)}) collective-permute-start(bf16[128,1280]{1,0:T(8,128)(2,1)S(1)} %finish.5), channel_id=1, source_target_pairs={{0,12},{1,13},{2,14},{3,15},{4,8},{5,9},{6,10},{7,11},{8,4},{9,5},... | collective-permute-start | bytes 983048 | tf_op jit(solution)/shard_map/ppermute | solution.py:250
  71.7 7.9 %collective-permute-start.14 = (bf16[64,1280]{1,0:T(8,128)(2,1)S(1)}, bf16[64,1280]{1,0:T(8,128)(2,1)S(1)}, u32[]{:S(2)}, u32[]{:S(2)}) collective-permute-start(bf16[64,1280]{1,0:T(8,128)(2,1)S(1)} %get-tuple-element.75), channel_id=1, source_target_pairs={{0,2},{1,3},{2,0},{3,1},{4,6},{5,7},{6,4},{7,5},{8,10},{9,11},{10,... | collective-permute-start | bytes 491528 | tf_op jit(solution)/shard_map/ppermute | solution.py:250
  82.5 1.2 %collective-permute-start.17 = (bf16[4,1280]{1,0:T(4,128)(2,1)S(1)}, bf16[4,1280]{1,0:T(4,128)(2,1)S(1)}, u32[]{:S(2)}, u32[]{:S(2)}) collective-permute-start(bf16[4,1280]{1,0:T(4,128)(2,1)S(1)} %get-tuple-element.80.refs_0_), channel_id=1, source_target_pairs={{0,1},{1,0},{2,3},{3,2},{4,5},{5,4},{6,7},{7,6},{8,9},{9,8},{10,11... | collective-permute-start | bytes 30728 | tf_op jit(solution)/shard_map/ppermute | solution.py:250
  83.8 3.8 %collective-permute-start.18 = (bf16[8,1280]{1,0:T(8,128)(2,1)S(1)}, bf16[8,1280]{1,0:T(8,128)(2,1)S(1)}, u32[]{:S(2)}, u32[]{:S(2)}) collective-permute-start(bf16[8,1280]{1,0:T(8,128)(2,1)S(1)} %pad_maximum_fusion.2), channel_id=1, source_target_pairs={{0,2},{1,3},{2,0},{3,1},{4,6},{5,7},{6,4},{7,5},{8,10},{9,11},{10,... | collective-permute-start | bytes 61448 | tf_op jit(solution)/shard_map/ppermute | solution.py:250
  87.7 4.9 %collective-permute-start.19 = (bf16[16,1280]{1,0:T(8,128)(2,1)S(1)}, bf16[16,1280]{1,0:T(8,128)(2,1)S(1)}, u32[]{:S(2)}, u32[]{:S(2)}) collective-permute-start(bf16[16,1280]{1,0:T(8,128)(2,1)S(1)} %pad_maximum_fusion.1), channel_id=1, source_target_pairs={{0,4},{1,5},{2,6},{3,7},{4,0},{5,1},{6,2},{7,3},{8,12},{9,13},{10,... | collective-permute-start | bytes 122888 | tf_op jit(solution)/shard_map/ppermute | solution.py:250
  92.6 5.4 %collective-permute-start.20 = (bf16[32,1280]{1,0:T(8,128)(2,1)S(1)}, bf16[32,1280]{1,0:T(8,128)(2,1)S(1)}, u32[]{:S(2)}, u32[]{:S(2)}) collective-permute-start(bf16[32,1280]{1,0:T(8,128)(2,1)S(1)} %pad_maximum_fusion), channel_id=1, source_target_pairs={{0,8},{1,9},{2,10},{3,11},{4,12},{5,13},{6,14},{7,15},{8,0},{9,1},... | collective-permute-start | bytes 245768 | tf_op jit(solution)/shard_map/ppermute | solution.py:250

commit v5 on v4

--- a/solution.py
+++ b/solution.py
@@ -160,14 +160,20 @@
     pieces, (d_pooled_ref, loss_ref, grad_ref, store, sems) = refs[:-5], refs[-5:]
     exact = lax.Precision.HIGHEST
     me, scale = mine_ref[0], scale_ref[0]
+    levels = len(pieces) - 1
+
+    def held_at(pair):
+        apart = pair ^ me
+        return sum(((apart >> level) & 1) << (levels - 1 - level) for level in range(levels)) * 4
+
     at, pooled, labels = 0, 0.0, 0.0
     for piece in pieces:
         many = piece.shape[0]
         row, col = iota((2 * pairs, many), 0), iota((2 * pairs, many), 1) + at
-        wanted = jnp.where(row < pairs, (row ^ me) * 4, ((row - pairs) ^ me) * 4 + 1)
+        wanted = jnp.where(row < pairs, held_at(row), held_at(row - pairs) + 1)
         pooled = pooled + dot((col == wanted).astype(F32).astype(BF16), piece[...])
         row, col = iota((pairs, many), 0), iota((pairs, many), 1) + at
-        wanted = (col == (row ^ me) * 4 + 2).astype(F32).astype(BF16)
+        wanted = (col == held_at(row) + 2).astype(F32).astype(BF16)
         labels = labels + dot(wanted, piece[:, :128])
         at = at + many
     pooled, labels = pooled.astype(BF16), labels[:, :1]
@@ -284,11 +290,11 @@
     partner = {0: swap(held[0], 2)}
     owns[0] = expert(True, held[0], 0)
     partner[1] = swap(after(held[1], owns[0][0]), 2)
-    owns[1] = expert(True, held[1], 0, partner[1], held[2], partner[0])
+    owns[2] = expert(True, held[2], 0, held[1], partner[0])
+    owns[1] = expert(True, held[1], 0, partner[1], owns[2][0])
     partner[2] = swap(after(held[2], owns[0][0]), 2)
     lefts[1] = expert(False, partner[1], 1, owns[1][0])
-    owns[2] = expert(True, held[2], 0, lefts[1][0])
-    lefts[2] = expert(False, partner[2], 1, owns[2][0])
+    lefts[2] = expert(False, partner[2], 1, lefts[1][0])
     finish(1, lefts[2][0])
     last = final[1]
     for k in range(3, experts):
@@ -335,10 +341,10 @@
         query,
         *[swap(final[k], SPLIT * k) for k in late],
     )
-    pieces, bits = [pooled], 1
-    while bits < devices:
+    pieces, bits = [pooled], devices // 2
+    while bits:
         pieces.append(swap(jnp.concatenate(pieces, axis=0), bits))
-        bits = bits * 2
+        bits = bits // 2
     d_pooled, loss, grad_proj = call(
         functools.partial(tail_kernel, devices),
         "contrast",

time: 104 us -> 104 us (level)
  waiting for transfers between devices: 37.9 us -> 36.7 us
    ppermute x21, waiting for transfers between devices: 37.9 us -> 36.7 us  [swap(): return lax.ppermute(values, 'dp', [(i, i ^ bits) for i in range(devices)])]
  transfers between devices with their start and end apart: 21 -> 21, of which waited for: 14 -> 15; matrix products, arithmetic and copies ran while one was open for 0% -> 0% of each run, Pallas kernels for 20% -> 20%
where the time goes in v5:
time: 104 us; the launch traced here: 103 us
  waiting for transfers between devices  36.7 us (35%)
  starting transfers between devices  32.5 us (31%)
  Pallas kernels  30.1 us (29%)
  between operations  2.29 us (2%)
  local copies, waits for them, and re-layouts  1.87 us (2%)
    ppermute x21, waiting for transfers between devices, swap(): return lax.ppermute(values, 'dp', [(i, i ^ bits) for i in range(devices)])  36.7 us
    ppermute x21, starting transfers between devices, swap(): return lax.ppermute(values, 'dp', [(i, i ^ bits) for i in range(devices)])  32.5 us
    pallas_call x8, Pallas kernels, expert(): call(functools.partial(ffn_kernel, own), 'own' if own else 'other', outs,...  18.9 us
    pallas_call x1, Pallas kernels, on_device(): call(functools.partial(tail_kernel, devices), 'contrast', [((2, width), F...  5.95 us
    pallas_call x1, Pallas kernels, on_device(): call(functools.partial(combine_kernel, late), 'combine', [((rows, width),...  2.95 us
  transfers between devices with their start and end apart: 21, of which 15 were waited for; matrix products, arithmetic and copies ran while one was open for 0% of the time, Pallas kernels for 20%

profile of v5, /device:TPU:0, one launch (start us, length us, event | category | flops | bytes accessed | tf_op | source)
XLA Modules:
  0.0 103.5 jit_solution(10101480053434678843)
XLA Ops:
  0.6 0.5 collective-permute-start.2
  1.2 0.1 collective-permute-start.1
  1.2 1.1 %copy-done.5 = bf16[1,320,1280]{2,1,0:T(8,128)(2,1)S(1)} copy-done((bf16[1,320,1280]{2,1,0:T(8,128)(2,1)S(1)}, bf16[1,320,1280]{2,1,0:T(8,128)(2,1)}, u32[]{:S(2)}) %copy-start.5) | copy-done | bytes 819224
  2.4 0.7 copy-done.6
  3.1 1.0 dispatch.1
  4.1 3.1 %collective-permute-start = (bf16[128,1280]{1,0:T(8,128)(2,1)S(1)}, bf16[128,1280]{1,0:T(8,128)(2,1)S(1)}, u32[]{:S(2)}, u32[]{:S(2)}) collective-permute-start(bf16[128,1280]{1,0:T(8,128)(2,1)S(1)} %get-tuple-element.45), channel_id=1, source_target_pairs={{0,4},{1,5},{2,6},{3,7},{4,0},{5,1},{6,2},{7,3},{8,12},{9,13},{10,... | collective-permute-start | bytes 983048 | tf_op jit(solution)/shard_map/ppermute | solution.py:256
  7.1 2.6 %collective-permute-start.4 = (bf16[128,1280]{1,0:T(8,128)(2,1)S(1)}, bf16[128,1280]{1,0:T(8,128)(2,1)S(1)}, u32[]{:S(2)}, u32[]{:S(2)}) collective-permute-start(bf16[128,1280]{1,0:T(8,128)(2,1)S(1)} %get-tuple-element.51), channel_id=1, source_target_pairs={{0,8},{1,9},{2,10},{3,11},{4,12},{5,13},{6,14},{7,15},{8,0},{9,1},... | collective-permute-start | bytes 983048 | tf_op jit(solution)/shard_map/ppermute | solution.py:256
  9.7 1.5 %collective-permute-start.5 = (bf16[128,1280]{1,0:T(8,128)(2,1)S(1)}, bf16[128,1280]{1,0:T(8,128)(2,1)S(1)}, u32[]{:S(2)}, u32[]{:S(2)}) collective-permute-start(bf16[128,1280]{1,0:T(8,128)(2,1)S(1)} %get-tuple-element.46.rows_ref.refs_2_), channel_id=1, source_target_pairs={{0,2},{1,3},{2,0},{3,1},{4,6},{5,7},{6,4},{7,5},{8,10},{9,11},{10,... | collective-permute-start | bytes 983048 | tf_op jit(solution)/shard_map/ppermute | solution.py:256
  11.2 0.0 copy-done.7
  11.3 0.0 collective-permute-done.2.out_b
  11.3 0.3 collective-permute-done.1.in_b
  11.5 0.0 copy-done
  11.5 2.4 %own.4 = (f32[128,1280]{1,0:T(8,128)S(1)}, f32[128,1]{1,0:T(8,128)S(1)}) custom-call(s32[1]{0:T(128)} %bitcast.mine_ref, bf16[128,1280]{1,0:T(8,128)(2,1)S(1)} %get-tuple-element.46.rows_ref.refs_2_, f32[1,1280]{1,0:T(1,128)S(1)} %reshape.42.gain_ref, bf16[4,1280]{1,0:T(4,128)(2,1)S(1)} %bitcast.27, bf16[1280,1280]{1,0:T(8,128)(2,1)S(1)} %bitcast.10, ...), custom_call_target="tpu_custom_call" | custom-call | tf_op jit(solution)/shard_map/own/pallas_call | solution.py:272
  13.9 8.1 %collective-permute-done.rows_ref.tokens_ref = bf16[128,1280]{1,0:T(8,128)(2,1)S(1)} collective-permute-done((bf16[128,1280]{1,0:T(8,128)(2,1)S(1)}, bf16[128,1280]{1,0:T(8,128)(2,1)S(1)}, u32[]{:S(2)}, u32[]{:S(2)}) %collective-permute-start) | collective-permute-done | bytes 327712 | tf_op jit(solution)/shard_map/ppermute | solution.py:256
  22.0 1.7 %collective-permute-start.3 = (bf16[128,1280]{1,0:T(8,128)(2,1)S(1)}, bf16[128,1280]{1,0:T(8,128)(2,1)S(1)}, u32[]{:S(2)}, u32[]{:S(2)}) collective-permute-start(bf16[128,1280]{1,0:T(8,128)(2,1)S(1)} %collective-permute-done.rows_ref.tokens_ref), channel_id=1, source_target_pairs={{0,2},{1,3},{2,0},{3,1},{4,6},{5,7},{6,4},{7,5},{8,10},{9,11},{10,... | collective-permute-start | bytes 983048 | tf_op jit(solution)/shard_map/ppermute | solution.py:256
  23.7 0.8 collective-permute-done.4.rows_ref.tokens_ref
  24.5 1.5 %collective-permute-start.6 = (bf16[128,1280]{1,0:T(8,128)(2,1)S(1)}, bf16[128,1280]{1,0:T(8,128)(2,1)S(1)}, u32[]{:S(2)}, u32[]{:S(2)}) collective-permute-start(bf16[128,1280]{1,0:T(8,128)(2,1)S(1)} %collective-permute-done.4.rows_ref.tokens_ref), channel_id=1, source_target_pairs={{0,2},{1,3},{2,0},{3,1},{4,6},{5,7},{6,4},{7,5},{8,10},{9,11},{10,... | collective-permute-start | bytes 983048 | tf_op jit(solution)/shard_map/ppermute | solution.py:256
  26.0 2.5 %collective-permute-start.9 = (bf16[128,1280]{1,0:T(8,128)(2,1)S(1)}, bf16[128,1280]{1,0:T(8,128)(2,1)S(1)}, u32[]{:S(2)}, u32[]{:S(2)}) collective-permute-start(bf16[128,1280]{1,0:T(8,128)(2,1)S(1)} %get-tuple-element.63), channel_id=1, source_target_pairs={{0,12},{1,13},{2,14},{3,15},{4,8},{5,9},{6,10},{7,11},{8,4},{9,5},... | collective-permute-start | bytes 983048 | tf_op jit(solution)/shard_map/ppermute | solution.py:256
  28.5 0.0 collective-permute-done.5.rows_ref
  28.5 2.4 %own.5 = (f32[128,1280]{1,0:T(8,128)S(1)}, f32[128,1]{1,0:T(8,128)S(1)}) custom-call(s32[1]{0:T(128)} %bitcast.mine_ref, bf16[128,1280]{1,0:T(8,128)(2,1)S(1)} %collective-permute-done.4.rows_ref.tokens_ref, f32[1,1280]{1,0:T(1,128)S(1)} %reshape.42.gain_ref, bf16[4,1280]{1,0:T(4,128)(2,1)S(1)} %bitcast.28, bf16[1280,1280]{1,0:T(8,128)(2,1)S(1)} %bitcast.11, ...), custom_call_target="tpu_custom_call" | custom-call | tf_op jit(solution)/shard_map/own/pallas_call | solution.py:272
  30.9 1.7 %collective-permute-done.3.rows_ref = bf16[128,1280]{1,0:T(8,128)(2,1)S(1)} collective-permute-done((bf16[128,1280]{1,0:T(8,128)(2,1)S(1)}, bf16[128,1280]{1,0:T(8,128)(2,1)S(1)}, u32[]{:S(2)}, u32[]{:S(2)}) %collective-permute-start.3) | collective-permute-done | bytes 327712 | tf_op jit(solution)/shard_map/ppermute | solution.py:256
  32.6 2.4 %own.6 = (f32[128,1280]{1,0:T(8,128)S(1)}, f32[128,1]{1,0:T(8,128)S(1)}) custom-call(s32[1]{0:T(128)} %bitcast.mine_ref, bf16[128,1280]{1,0:T(8,128)(2,1)S(1)} %collective-permute-done.rows_ref.tokens_ref, f32[1,1280]{1,0:T(1,128)S(1)} %reshape.42.gain_ref, bf16[4,1280]{1,0:T(4,128)(2,1)S(1)} %bitcast.29, bf16[1280,1280]{1,0:T(8,128)(2,1)S(1)} %bitcast.12, ...), custom_call_target="tpu_custom_call" | custom-call | tf_op jit(solution)/shard_map/own/pallas_call | solution.py:272
  35.0 2.3 %other.4 = bf16[128,1280]{1,0:T(8,128)(2,1)S(1)} custom-call(s32[1]{0:T(128)} %bitcast.mine_ref, bf16[128,1280]{1,0:T(8,128)(2,1)S(1)} %collective-permute-done.3.rows_ref, f32[1,1280]{1,0:T(1,128)S(1)} %reshape.42.gain_ref, bf16[4,1280]{1,0:T(4,128)(2,1)S(1)} %bitcast.30, bf16[1280,1280]{1,0:T(8,128)(2,1)S(1)} %bitcast.13, bf16[1280,1280]{1,0:T(8,128)(2,1)S(1)} %bitcast.22, ...), custom_call_target="tpu_custom_call" | custom-call | tf_op jit(solution)/shard_map/other/pallas_call | solution.py:272
  37.4 1.8 %collective-permute-start.7 = (bf16[128,1280]{1,0:T(8,128)(2,1)S(1)}, bf16[128,1280]{1,0:T(8,128)(2,1)S(1)}, u32[]{:S(2)}, u32[]{:S(2)}) collective-permute-start(bf16[128,1280]{1,0:T(8,128)(2,1)S(1)} %other.4), channel_id=1, source_target_pairs={{0,2},{1,3},{2,0},{3,1},{4,6},{5,7},{6,4},{7,5},{8,10},{9,11},{10,... | collective-permute-start | bytes 983048 | tf_op jit(solution)/shard_map/ppermute | solution.py:256
  39.1 0.0 collective-permute-done.6.rows_ref
  39.1 2.3 %other.5 = bf16[128,1280]{1,0:T(8,128)(2,1)S(1)} custom-call(s32[1]{0:T(128)} %bitcast.mine_ref, bf16[128,1280]{1,0:T(8,128)(2,1)S(1)} %collective-permute-done.6.rows_ref, f32[1,1280]{1,0:T(1,128)S(1)} %reshape.42.gain_ref, bf16[4,1280]{1,0:T(4,128)(2,1)S(1)} %bitcast.31, bf16[1280,1280]{1,0:T(8,128)(2,1)S(1)} %bitcast.14, bf16[1280,1280]{1,0:T(8,128)(2,1)S(1)} %bitcast.23, ...), custom_call_target="tpu_custom_call" | custom-call | tf_op jit(solution)/shard_map/other/pallas_call | solution.py:272
  41.5 1.7 %collective-permute-start.10 = (bf16[128,1280]{1,0:T(8,128)(2,1)S(1)}, bf16[128,1280]{1,0:T(8,128)(2,1)S(1)}, u32[]{:S(2)}, u32[]{:S(2)}) collective-permute-start(bf16[128,1280]{1,0:T(8,128)(2,1)S(1)} %other.5), channel_id=1, source_target_pairs={{0,2},{1,3},{2,0},{3,1},{4,6},{5,7},{6,4},{7,5},{8,10},{9,11},{10,... | collective-permute-start | bytes 983048 | tf_op jit(solution)/shard_map/ppermute | solution.py:256
  43.2 0.0 collective-permute-done.9.rows_ref.tokens_ref
  43.2 0.4 collective-permute-start.12
  43.6 4.5 %collective-permute-done.7.refs_0_ = bf16[128,1280]{1,0:T(8,128)(2,1)S(1)} collective-permute-done((bf16[128,1280]{1,0:T(8,128)(2,1)S(1)}, bf16[128,1280]{1,0:T(8,128)(2,1)S(1)}, u32[]{:S(2)}, u32[]{:S(2)}) %collective-permute-start.7) | collective-permute-done | bytes 327712 | tf_op jit(solution)/shard_map/ppermute | solution.py:256
  48.1 0.3 finish.3
  48.4 0.1 collective-permute-start.8
  48.5 2.4 %own.7 = (f32[128,1280]{1,0:T(8,128)S(1)}, f32[128,1]{1,0:T(8,128)S(1)}) custom-call(s32[1]{0:T(128)} %bitcast.mine_ref, bf16[128,1280]{1,0:T(8,128)(2,1)S(1)} %collective-permute-done.9.rows_ref.tokens_ref, f32[1,1280]{1,0:T(1,128)S(1)} %reshape.42.gain_ref, bf16[4,1280]{1,0:T(4,128)(2,1)S(1)} %bitcast.32, bf16[1280,1280]{1,0:T(8,128)(2,1)S(1)} %bitcast.15, ...), custom_call_target="tpu_custom_call" | custom-call | tf_op jit(solution)/shard_map/own/pallas_call | solution.py:272
  50.9 4.2 %collective-permute-done.10.refs_0_ = bf16[128,1280]{1,0:T(8,128)(2,1)S(1)} collective-permute-done((bf16[128,1280]{1,0:T(8,128)(2,1)S(1)}, bf16[128,1280]{1,0:T(8,128)(2,1)S(1)}, u32[]{:S(2)}, u32[]{:S(2)}) %collective-permute-start.10) | collective-permute-done | bytes 327712 | tf_op jit(solution)/shard_map/ppermute | solution.py:256
  55.1 0.2 finish.4
  55.3 0.8 collective-permute-start.11
  56.1 3.2 %collective-permute-done.12.rows_ref = bf16[128,1280]{1,0:T(8,128)(2,1)S(1)} collective-permute-done((bf16[128,1280]{1,0:T(8,128)(2,1)S(1)}, bf16[128,1280]{1,0:T(8,128)(2,1)S(1)}, u32[]{:S(2)}, u32[]{:S(2)}) %collective-permute-start.12) | collective-permute-done | bytes 327712 | tf_op jit(solution)/shard_map/ppermute | solution.py:256
  59.3 2.3 %other.6 = bf16[128,1280]{1,0:T(8,128)(2,1)S(1)} custom-call(s32[1]{0:T(128)} %bitcast.mine_ref, bf16[128,1280]{1,0:T(8,128)(2,1)S(1)} %collective-permute-done.12.rows_ref, f32[1,1280]{1,0:T(1,128)S(1)} %reshape.42.gain_ref, bf16[4,1280]{1,0:T(4,128)(2,1)S(1)} %bitcast.33, bf16[1280,1280]{1,0:T(8,128)(2,1)S(1)} %bitcast.16, ...), custom_call_target="tpu_custom_call" | custom-call | tf_op jit(solution)/shard_map/other/pallas_call | solution.py:272
  61.6 0.0 copy-start.4
  61.6 0.0 copy-start.8
  61.6 1.4 %collective-permute-start.15 = (bf16[128,1280]{1,0:T(8,128)(2,1)S(1)}, bf16[128,1280]{1,0:T(8,128)(2,1)S(1)}, u32[]{:S(2)}, u32[]{:S(2)}) collective-permute-start(bf16[128,1280]{1,0:T(8,128)(2,1)S(1)} %other.6), channel_id=1, source_target_pairs={{0,2},{1,3},{2,0},{3,1},{4,6},{5,7},{6,4},{7,5},{8,10},{9,11},{10,... | collective-permute-start | bytes 983048 | tf_op jit(solution)/shard_map/ppermute | solution.py:256
  63.0 2.3 %other.7 = (bf16[128,1280]{1,0:T(8,128)(2,1)S(1)}, bf16[64,1280]{1,0:T(8,128)(2,1)S(1)}) custom-call(s32[1]{0:T(128)} %bitcast.mine_ref, bf16[128,1280]{1,0:T(8,128)(2,1)S(1)} %collective-permute-done.5.rows_ref, f32[1,1280]{1,0:T(1,128)S(1)} %reshape.42.gain_ref, bf16[4,1280]{1,0:T(4,128)(2,1)S(1)} %bitcast.34, bf16[1280,1280]{1,0:T(8,128)(2,1)S(1)} %bitcast.17, ...), custom_call_target="tpu_custom_call" | custom-call | tf_op jit(solution)/shard_map/other/pallas_call | solution.py:272
  65.4 0.0 copy-start.2
  65.4 0.0 collective-permute-done.8.refs_0_
  65.4 1.5 %collective-permute-done.11.refs_1_ = bf16[128,1280]{1,0:T(8,128)(2,1)S(1)} collective-permute-done((bf16[128,1280]{1,0:T(8,128)(2,1)S(1)}, bf16[128,1280]{1,0:T(8,128)(2,1)S(1)}, u32[]{:S(2)}, u32[]{:S(2)}) %collective-permute-start.11) | collective-permute-done | bytes 327712 | tf_op jit(solution)/shard_map/ppermute | solution.py:256
  66.9 0.6 partial.1
  67.5 1.6 %collective-permute-start.13 = (bf16[128,1280]{1,0:T(8,128)(2,1)S(1)}, bf16[128,1280]{1,0:T(8,128)(2,1)S(1)}, u32[]{:S(2)}, u32[]{:S(2)}) collective-permute-start(bf16[128,1280]{1,0:T(8,128)(2,1)S(1)} %get-tuple-element.73), channel_id=1, source_target_pairs={{0,2},{1,3},{2,0},{3,1},{4,6},{5,7},{6,4},{7,5},{8,10},{9,11},{10,... | collective-permute-start | bytes 983048 | tf_op jit(solution)/shard_map/ppermute | solution.py:256
  69.1 1.7 %collective-permute-done.15.refs_0_ = bf16[128,1280]{1,0:T(8,128)(2,1)S(1)} collective-permute-done((bf16[128,1280]{1,0:T(8,128)(2,1)S(1)}, bf16[128,1280]{1,0:T(8,128)(2,1)S(1)}, u32[]{:S(2)}, u32[]{:S(2)}) %collective-permute-start.15) | collective-permute-done | bytes 327712 | tf_op jit(solution)/shard_map/ppermute | solution.py:256
  70.8 0.2 finish.5
  70.9 2.6 %collective-permute-start.16 = (bf16[128,1280]{1,0:T(8,128)(2,1)S(1)}, bf16[128,1280]{1,0:T(8,128)(2,1)S(1)}, u32[]{:S(2)}, u32[]{:S(2)}) collective-permute-start(bf16[128,1280]{1,0:T(8,128)(2,1)S(1)} %finish.5), channel_id=1, source_target_pairs={{0,12},{1,13},{2,14},{3,15},{4,8},{5,9},{6,10},{7,11},{8,4},{9,5},... | collective-permute-start | bytes 983048 | tf_op jit(solution)/shard_map/ppermute | solution.py:256
  73.6 1.6 %collective-permute-start.14 = (bf16[64,1280]{1,0:T(8,128)(2,1)S(1)}, bf16[64,1280]{1,0:T(8,128)(2,1)S(1)}, u32[]{:S(2)}, u32[]{:S(2)}) collective-permute-start(bf16[64,1280]{1,0:T(8,128)(2,1)S(1)} %get-tuple-element.75), channel_id=1, source_target_pairs={{0,2},{1,3},{2,0},{3,1},{4,6},{5,7},{6,4},{7,5},{8,10},{9,11},{10,... | collective-permute-start | bytes 491528 | tf_op jit(solution)/shard_map/ppermute | solution.py:256
  75.8 3.5 %collective-permute-done.14.refs_6_ = bf16[64,1280]{1,0:T(8,128)(2,1)S(1)} collective-permute-done((bf16[64,1280]{1,0:T(8,128)(2,1)S(1)}, bf16[64,1280]{1,0:T(8,128)(2,1)S(1)}, u32[]{:S(2)}, u32[]{:S(2)}) %collective-permute-start.14) | collective-permute-done | bytes 163872 | tf_op jit(solution)/shard_map/ppermute | solution.py:256
  79.3 0.0 collective-permute-done.13.refs_5_
  79.3 0.7 collective-permute-done.16.refs_10_
  80.0 3.0 %combine.1 = (bf16[320,1280]{1,0:T(8,128)(2,1)}, bf16[4,1280]{1,0:T(4,128)(2,1)S(1)}) custom-call(s32[1]{0:T(128)S(6)} %copy.15.refs_0_, f32[320,1280]{1,0:T(8,128)S(1)} %get-tuple-element.67.refs_1_, bf16[128,1280]{1,0:T(8,128)(2,1)S(1)} %get-tuple-element.46.rows_ref.refs_2_, f32[128,1]{1,0:T(8,128)S(1)} %get-tuple-element.68.refs_3_, ...), custom_call_target="tpu_custom_call" | custom-call | tf_op jit(solution)/shard_map/combine/pallas_call | solution.py:325
  83.0 3.3 %collective-permute-start.17 = (bf16[4,1280]{1,0:T(4,128)(2,1)S(1)}, bf16[4,1280]{1,0:T(4,128)(2,1)S(1)}, u32[]{:S(2)}, u32[]{:S(2)}) collective-permute-start(bf16[4,1280]{1,0:T(4,128)(2,1)S(1)} %get-tuple-element.80.refs_0_), channel_id=1, source_target_pairs={{0,8},{1,9},{2,10},{3,11},{4,12},{5,13},{6,14},{7,15},{8,0},{9,1},... | collective-permute-start | bytes 30728 | tf_op jit(solution)/shard_map/ppermute | solution.py:256
  86.3 1.7 %collective-permute-done.17.refs_1_ = bf16[4,1280]{1,0:T(4,128)(2,1)S(1)} collective-permute-done((bf16[4,1280]{1,0:T(4,128)(2,1)S(1)}, bf16[4,1280]{1,0:T(4,128)(2,1)S(1)}, u32[]{:S(2)}, u32[]{:S(2)}) %collective-permute-start.17) | collective-permute-done | bytes 10272 | tf_op jit(solution)/shard_map/ppermute | solution.py:256
  88.0 1.5 %collective-permute-start.18 = (bf16[8,1280]{1,0:T(8,128)(2,1)S(1)}, bf16[8,1280]{1,0:T(8,128)(2,1)S(1)}, u32[]{:S(2)}, u32[]{:S(2)}) collective-permute-start(bf16[8,1280]{1,0:T(8,128)(2,1)S(1)} %pad_maximum_fusion.2), channel_id=1, source_target_pairs={{0,4},{1,5},{2,6},{3,7},{4,0},{5,1},{6,2},{7,3},{8,12},{9,13},{10,... | collective-permute-start | bytes 61448 | tf_op jit(solution)/shard_map/ppermute | solution.py:256
  89.5 2.3 %collective-permute-done.18.refs_2_ = bf16[8,1280]{1,0:T(8,128)(2,1)S(1)} collective-permute-done((bf16[8,1280]{1,0:T(8,128)(2,1)S(1)}, bf16[8,1280]{1,0:T(8,128)(2,1)S(1)}, u32[]{:S(2)}, u32[]{:S(2)}) %collective-permute-start.18) | collective-permute-done | bytes 20512 | tf_op jit(solution)/shard_map/ppermute | solution.py:256
  91.8 2.2 %collective-permute-start.19 = (bf16[16,1280]{1,0:T(8,128)(2,1)S(1)}, bf16[16,1280]{1,0:T(8,128)(2,1)S(1)}, u32[]{:S(2)}, u32[]{:S(2)}) collective-permute-start(bf16[16,1280]{1,0:T(8,128)(2,1)S(1)} %pad_maximum_fusion.1), channel_id=1, source_target_pairs={{0,2},{1,3},{2,0},{3,1},{4,6},{5,7},{6,4},{7,5},{8,10},{9,11},{10,... | collective-permute-start | bytes 122888 | tf_op jit(solution)/shard_map/ppermute | solution.py:256
  94.0 2.0 %collective-permute-done.19.refs_3_ = bf16[16,1280]{1,0:T(8,128)(2,1)S(1)} collective-permute-done((bf16[16,1280]{1,0:T(8,128)(2,1)S(1)}, bf16[16,1280]{1,0:T(8,128)(2,1)S(1)}, u32[]{:S(2)}, u32[]{:S(2)}) %collective-permute-start.19) | collective-permute-done | bytes 40992 | tf_op jit(solution)/shard_map/ppermute | solution.py:256
  96.0 0.1 collective-permute-start.20
  96.8 0.6 collective-permute-done.20.refs_4_
  97.4 6.0 %contrast.1 = (f32[2,1280]{1,0:T(2,128)}, f32[1,1]{1,0:T(1,128)}, f32[1280,1280]{1,0:T(8,128)}) custom-call(s32[1]{0:T(128)} %bitcast.mine_ref, f32[1]{0:T(128)S(6)} %copy.16.scale_ref, bf16[1280,1280]{1,0:T(8,128)(2,1)S(1)} %copy-done.2, bf16[4,1280]{1,0:T(4,128)(2,1)S(1)} %get-tuple-element.80.refs_0_, ...), custom_call_target="tpu_custom_call" | custom-call | tf_op jit(solution)/shard_map/contrast/pallas_call | solution.py:348
  (16 shorter events, 0.1 us)
Async XLA Ops:
  0.6 10.6 %collective-permute-start.2 = (bf16[1280,1280]{1,0:T(8,128)(2,1)}, bf16[1280,1280]{1,0:T(8,128)(2,1)S(1)}, u32[]{:S(2)}, u32[]{:S(2)}) collective-permute-start(bf16[1280,1280]{1,0:T(8,128)(2,1)} %bitcast.18), channel_id=1, source_target_pairs={{0,1},{1,0},{2,3},{3,2},{4,5},{5,4},{6,7},{7,6},{8,9},{9,8},{10,11... | collective-permute-start | bytes 9830408 | tf_op jit(solution)/shard_map/ppermute | solution.py:256
  1.2 10.4 %collective-permute-start.1 = (bf16[1280,1280]{1,0:T(8,128)(2,1)}, bf16[1280,1280]{1,0:T(8,128)(2,1)S(1)}, u32[]{:S(2)}, u32[]{:S(2)}) collective-permute-start(bf16[1280,1280]{1,0:T(8,128)(2,1)} %bitcast.9), channel_id=1, source_target_pairs={{0,1},{1,0},{2,3},{3,2},{4,5},{5,4},{6,7},{7,6},{8,9},{9,8},{10,11... | collective-permute-start | bytes 9830408 | tf_op jit(solution)/shard_map/ppermute | solution.py:256
  1.2 1.1 %copy-start.5 = (bf16[1,320,1280]{2,1,0:T(8,128)(2,1)S(1)}, bf16[1,320,1280]{2,1,0:T(8,128)(2,1)}, u32[]{:S(2)}) copy-start(bf16[1,320,1280]{2,1,0:T(8,128)(2,1)} %param.11) | copy-start | bytes 2457604
  2.4 0.7 copy-start.6
  3.1 8.2 %copy-start.7 = (f32[1280]{0:T(1024)S(1)}, f32[1280]{0:T(1024)}, u32[]{:S(2)}) copy-start(f32[1280]{0:T(1024)} %param.14) | copy-start | bytes 15364
  3.1 8.5 %copy-start = (bf16[1,1280,1280]{2,1,0:T(8,128)(2,1)S(1)}, bf16[1,1280,1280]{2,1,0:T(8,128)(2,1)}, u32[]{:S(2)}) copy-start(bf16[1,1280,1280]{2,1,0:T(8,128)(2,1)} %param.16) | copy-start | bytes 9830404
  3.1 8.5 %copy-start.1 = (bf16[1,1280,1280]{2,1,0:T(8,128)(2,1)S(1)}, bf16[1,1280,1280]{2,1,0:T(8,128)(2,1)}, u32[]{:S(2)}) copy-start(bf16[1,1280,1280]{2,1,0:T(8,128)(2,1)} %param.17) | copy-start | bytes 9830404
  3.1 8.5 %copy-start.3 = (bf16[1280,4]{0,1:T(4,128)(2,1)S(1)}, bf16[1280,4]{0,1:T(4,128)(2,1)}, u32[]{:S(2)}) copy-start(bf16[1280,4]{0,1:T(4,128)(2,1)} %param.15) | copy-start | bytes 30724
  4.1 17.9 %collective-permute-start = (bf16[128,1280]{1,0:T(8,128)(2,1)S(1)}, bf16[128,1280]{1,0:T(8,128)(2,1)S(1)}, u32[]{:S(2)}, u32[]{:S(2)}) collective-permute-start(bf16[128,1280]{1,0:T(8,128)(2,1)S(1)} %get-tuple-element.45), channel_id=1, source_target_pairs={{0,4},{1,5},{2,6},{3,7},{4,0},{5,1},{6,2},{7,3},{8,12},{9,13},{10,... | collective-permute-start | bytes 983048 | tf_op jit(solution)/shard_map/ppermute | solution.py:256
  7.1 17.4 %collective-permute-start.4 = (bf16[128,1280]{1,0:T(8,128)(2,1)S(1)}, bf16[128,1280]{1,0:T(8,128)(2,1)S(1)}, u32[]{:S(2)}, u32[]{:S(2)}) collective-permute-start(bf16[128,1280]{1,0:T(8,128)(2,1)S(1)} %get-tuple-element.51), channel_id=1, source_target_pairs={{0,8},{1,9},{2,10},{3,11},{4,12},{5,13},{6,14},{7,15},{8,0},{9,1},... | collective-permute-start | bytes 983048 | tf_op jit(solution)/shard_map/ppermute | solution.py:256
  9.7 18.8 %collective-permute-start.5 = (bf16[128,1280]{1,0:T(8,128)(2,1)S(1)}, bf16[128,1280]{1,0:T(8,128)(2,1)S(1)}, u32[]{:S(2)}, u32[]{:S(2)}) collective-permute-start(bf16[128,1280]{1,0:T(8,128)(2,1)S(1)} %get-tuple-element.46.rows_ref.refs_2_), channel_id=1, source_target_pairs={{0,2},{1,3},{2,0},{3,1},{4,6},{5,7},{6,4},{7,5},{8,10},{9,11},{10,... | collective-permute-start | bytes 983048 | tf_op jit(solution)/shard_map/ppermute | solution.py:256
  22.0 10.6 %collective-permute-start.3 = (bf16[128,1280]{1,0:T(8,128)(2,1)S(1)}, bf16[128,1280]{1,0:T(8,128)(2,1)S(1)}, u32[]{:S(2)}, u32[]{:S(2)}) collective-permute-start(bf16[128,1280]{1,0:T(8,128)(2,1)S(1)} %collective-permute-done.rows_ref.tokens_ref), channel_id=1, source_target_pairs={{0,2},{1,3},{2,0},{3,1},{4,6},{5,7},{6,4},{7,5},{8,10},{9,11},{10,... | collective-permute-start | bytes 983048 | tf_op jit(solution)/shard_map/ppermute | solution.py:256
  24.5 14.6 %collective-permute-start.6 = (bf16[128,1280]{1,0:T(8,128)(2,1)S(1)}, bf16[128,1280]{1,0:T(8,128)(2,1)S(1)}, u32[]{:S(2)}, u32[]{:S(2)}) collective-permute-start(bf16[128,1280]{1,0:T(8,128)(2,1)S(1)} %collective-permute-done.4.rows_ref.tokens_ref), channel_id=1, source_target_pairs={{0,2},{1,3},{2,0},{3,1},{4,6},{5,7},{6,4},{7,5},{8,10},{9,11},{10,... | collective-permute-start | bytes 983048 | tf_op jit(solution)/shard_map/ppermute | solution.py:256
  26.0 17.1 %collective-permute-start.9 = (bf16[128,1280]{1,0:T(8,128)(2,1)S(1)}, bf16[128,1280]{1,0:T(8,128)(2,1)S(1)}, u32[]{:S(2)}, u32[]{:S(2)}) collective-permute-start(bf16[128,1280]{1,0:T(8,128)(2,1)S(1)} %get-tuple-element.63), channel_id=1, source_target_pairs={{0,12},{1,13},{2,14},{3,15},{4,8},{5,9},{6,10},{7,11},{8,4},{9,5},... | collective-permute-start | bytes 983048 | tf_op jit(solution)/shard_map/ppermute | solution.py:256
  37.4 10.7 %collective-permute-start.7 = (bf16[128,1280]{1,0:T(8,128)(2,1)S(1)}, bf16[128,1280]{1,0:T(8,128)(2,1)S(1)}, u32[]{:S(2)}, u32[]{:S(2)}) collective-permute-start(bf16[128,1280]{1,0:T(8,128)(2,1)S(1)} %other.4), channel_id=1, source_target_pairs={{0,2},{1,3},{2,0},{3,1},{4,6},{5,7},{6,4},{7,5},{8,10},{9,11},{10,... | collective-permute-start | bytes 983048 | tf_op jit(solution)/shard_map/ppermute | solution.py:256
  41.5 13.6 %collective-permute-start.10 = (bf16[128,1280]{1,0:T(8,128)(2,1)S(1)}, bf16[128,1280]{1,0:T(8,128)(2,1)S(1)}, u32[]{:S(2)}, u32[]{:S(2)}) collective-permute-start(bf16[128,1280]{1,0:T(8,128)(2,1)S(1)} %other.5), channel_id=1, source_target_pairs={{0,2},{1,3},{2,0},{3,1},{4,6},{5,7},{6,4},{7,5},{8,10},{9,11},{10,... | collective-permute-start | bytes 983048 | tf_op jit(solution)/shard_map/ppermute | solution.py:256
  43.2 16.1 %collective-permute-start.12 = (bf16[128,1280]{1,0:T(8,128)(2,1)S(1)}, bf16[128,1280]{1,0:T(8,128)(2,1)S(1)}, u32[]{:S(2)}, u32[]{:S(2)}) collective-permute-start(bf16[128,1280]{1,0:T(8,128)(2,1)S(1)} %collective-permute-done.9.rows_ref.tokens_ref), channel_id=1, source_target_pairs={{0,2},{1,3},{2,0},{3,1},{4,6},{5,7},{6,4},{7,5},{8,10},{9,11},{10,... | collective-permute-start | bytes 983048 | tf_op jit(solution)/shard_map/ppermute | solution.py:256
  48.4 17.0 %collective-permute-start.8 = (bf16[128,1280]{1,0:T(8,128)(2,1)S(1)}, bf16[128,1280]{1,0:T(8,128)(2,1)S(1)}, u32[]{:S(2)}, u32[]{:S(2)}) collective-permute-start(bf16[128,1280]{1,0:T(8,128)(2,1)S(1)} %finish.3), channel_id=1, source_target_pairs={{0,4},{1,5},{2,6},{3,7},{4,0},{5,1},{6,2},{7,3},{8,12},{9,13},{10,... | collective-permute-start | bytes 983048 | tf_op jit(solution)/shard_map/ppermute | solution.py:256
  55.3 11.7 %collective-permute-start.11 = (bf16[128,1280]{1,0:T(8,128)(2,1)S(1)}, bf16[128,1280]{1,0:T(8,128)(2,1)S(1)}, u32[]{:S(2)}, u32[]{:S(2)}) collective-permute-start(bf16[128,1280]{1,0:T(8,128)(2,1)S(1)} %finish.4), channel_id=1, source_target_pairs={{0,8},{1,9},{2,10},{3,11},{4,12},{5,13},{6,14},{7,15},{8,0},{9,1},... | collective-permute-start | bytes 983048 | tf_op jit(solution)/shard_map/ppermute | solution.py:256
  61.6 5.4 %copy-start.4 = (f32[2,16,80]{2,1,0:T(8,128)S(1)}, f32[2,16,80]{2,1,0:T(8,128)}, u32[]{:S(2)}) copy-start(f32[2,16,80]{2,1,0:T(8,128)} %query_ref.1) | copy-start | bytes 30724
  61.6 14.2 %copy-start.8 = (f32[1280]{0:T(1024)S(1)}, f32[1280]{0:T(1024)}, u32[]{:S(2)}) copy-start(f32[1280]{0:T(1024)} %param.18) | copy-start | bytes 15364
  61.6 9.2 %collective-permute-start.15 = (bf16[128,1280]{1,0:T(8,128)(2,1)S(1)}, bf16[128,1280]{1,0:T(8,128)(2,1)S(1)}, u32[]{:S(2)}, u32[]{:S(2)}) collective-permute-start(bf16[128,1280]{1,0:T(8,128)(2,1)S(1)} %other.6), channel_id=1, source_target_pairs={{0,2},{1,3},{2,0},{3,1},{4,6},{5,7},{6,4},{7,5},{8,10},{9,11},{10,... | collective-permute-start | bytes 983048 | tf_op jit(solution)/shard_map/ppermute | solution.py:256
  65.4 32.0 %copy-start.2 = (bf16[1280,1280]{1,0:T(8,128)(2,1)S(1)}, bf16[1280,1280]{1,0:T(8,128)(2,1)}, u32[]{:S(2)}) copy-start(bf16[1280,1280]{1,0:T(8,128)(2,1)} %proj_ref.1) | copy-start | bytes 9830404
  67.5 11.8 %collective-permute-start.13 = (bf16[128,1280]{1,0:T(8,128)(2,1)S(1)}, bf16[128,1280]{1,0:T(8,128)(2,1)S(1)}, u32[]{:S(2)}, u32[]{:S(2)}) collective-permute-start(bf16[128,1280]{1,0:T(8,128)(2,1)S(1)} %get-tuple-element.73), channel_id=1, source_target_pairs={{0,2},{1,3},{2,0},{3,1},{4,6},{5,7},{6,4},{7,5},{8,10},{9,11},{10,... | collective-permute-start | bytes 983048 | tf_op jit(solution)/shard_map/ppermute | solution.py:256
  70.9 9.0 %collective-permute-start.16 = (bf16[128,1280]{1,0:T(8,128)(2,1)S(1)}, bf16[128,1280]{1,0:T(8,128)(2,1)S(1)}, u32[]{:S(2)}, u32[]{:S(2)}) collective-permute-start(bf16[128,1280]{1,0:T(8,128)(2,1)S(1)} %finish.5), channel_id=1, source_target_pairs={{0,12},{1,13},{2,14},{3,15},{4,8},{5,9},{6,10},{7,11},{8,4},{9,5},... | collective-permute-start | bytes 983048 | tf_op jit(solution)/shard_map/ppermute | solution.py:256
  73.6 5.7 %collective-permute-start.14 = (bf16[64,1280]{1,0:T(8,128)(2,1)S(1)}, bf16[64,1280]{1,0:T(8,128)(2,1)S(1)}, u32[]{:S(2)}, u32[]{:S(2)}) collective-permute-start(bf16[64,1280]{1,0:T(8,128)(2,1)S(1)} %get-tuple-element.75), channel_id=1, source_target_pairs={{0,2},{1,3},{2,0},{3,1},{4,6},{5,7},{6,4},{7,5},{8,10},{9,11},{10,... | collective-permute-start | bytes 491528 | tf_op jit(solution)/shard_map/ppermute | solution.py:256
  83.0 5.0 %collective-permute-start.17 = (bf16[4,1280]{1,0:T(4,128)(2,1)S(1)}, bf16[4,1280]{1,0:T(4,128)(2,1)S(1)}, u32[]{:S(2)}, u32[]{:S(2)}) collective-permute-start(bf16[4,1280]{1,0:T(4,128)(2,1)S(1)} %get-tuple-element.80.refs_0_), channel_id=1, source_target_pairs={{0,8},{1,9},{2,10},{3,11},{4,12},{5,13},{6,14},{7,15},{8,0},{9,1},... | collective-permute-start | bytes 30728 | tf_op jit(solution)/shard_map/ppermute | solution.py:256
  88.0 3.8 %collective-permute-start.18 = (bf16[8,1280]{1,0:T(8,128)(2,1)S(1)}, bf16[8,1280]{1,0:T(8,128)(2,1)S(1)}, u32[]{:S(2)}, u32[]{:S(2)}) collective-permute-start(bf16[8,1280]{1,0:T(8,128)(2,1)S(1)} %pad_maximum_fusion.2), channel_id=1, source_target_pairs={{0,4},{1,5},{2,6},{3,7},{4,0},{5,1},{6,2},{7,3},{8,12},{9,13},{10,... | collective-permute-start | bytes 61448 | tf_op jit(solution)/shard_map/ppermute | solution.py:256
  91.8 4.2 %collective-permute-start.19 = (bf16[16,1280]{1,0:T(8,128)(2,1)S(1)}, bf16[16,1280]{1,0:T(8,128)(2,1)S(1)}, u32[]{:S(2)}, u32[]{:S(2)}) collective-permute-start(bf16[16,1280]{1,0:T(8,128)(2,1)S(1)} %pad_maximum_fusion.1), channel_id=1, source_target_pairs={{0,2},{1,3},{2,0},{3,1},{4,6},{5,7},{6,4},{7,5},{8,10},{9,11},{10,... | collective-permute-start | bytes 122888 | tf_op jit(solution)/shard_map/ppermute | solution.py:256
  96.0 1.3 %collective-permute-start.20 = (bf16[32,1280]{1,0:T(8,128)(2,1)S(1)}, bf16[32,1280]{1,0:T(8,128)(2,1)S(1)}, u32[]{:S(2)}, u32[]{:S(2)}) collective-permute-start(bf16[32,1280]{1,0:T(8,128)(2,1)S(1)} %pad_maximum_fusion), channel_id=1, source_target_pairs={{0,1},{1,0},{2,3},{3,2},{4,5},{5,4},{6,7},{7,6},{8,9},{9,8},{10,11... | collective-permute-start | bytes 245768 | tf_op jit(solution)/shard_map/ppermute | solution.py:256

commit v6 on v5

--- a/solution.py
+++ b/solution.py
@@ -107,14 +107,16 @@
     return (feature >= head * HEAD_DIM) & (feature < (head + 1) * HEAD_DIM)
 
 
-def partial_kernel(early, query_ref, place_ref, *refs):
-    parts, sum_ref, rows_ref, buffer = refs[:-3], *refs[-3:]
+def partial_kernel(early, late, query_ref, place_ref, *refs):
+    parts, (sum_ref, rows_ref, select_ref, buffer) = refs[:-4], refs[-4:]
     cap, width = parts[0].shape
     for at, part_ref in enumerate(parts):
         buffer[at * cap : (at + 1) * cap] = part_ref[...]
     place = place_ref[...]
     select = jnp.concatenate([chosen(place, k * cap, cap) for k in early], axis=0)
     sum_ref[...] = dot(select, buffer[...], ((0,), (0,)))
+    select = jnp.concatenate([chosen(place, k * cap, cap) for k in [0] + late], axis=0)
+    select_ref[...] = select.T
     feature = iota((1, width), 1)
     inner = feature - HEAD_DIM * sum(
         (feature >= h * HEAD_DIM).astype(jnp.int32) for h in range(1, HEADS)
@@ -126,17 +128,15 @@
         rows_ref[modal : modal + 1] = jnp.sum(wide, axis=0, keepdims=True)
 
 
-def combine_kernel(late, *refs):
-    label_ref, sum_ref, tokens_ref, gate_ref, kept_ref, high_ref, low_ref, place_ref = refs[:8]
+def combine_kernel(*refs):
+    label_ref, sum_ref, tokens_ref, gate_ref, kept_ref, high_ref, low_ref, select_ref = refs[:8]
     gain_ref, query_ref, *backs, mixed_ref, pooled_ref, buffer = refs[8:]
     cap = kept_ref.shape[0]
     rows, width = mixed_ref.shape
     finish_kernel(tokens_ref, gate_ref, kept_ref, high_ref, low_ref, buffer.at[:cap])
     for at, back_ref in enumerate(backs):
         buffer[(at + 1) * cap : (at + 2) * cap] = back_ref[...]
-    place = place_ref[...]
-    select = jnp.concatenate([chosen(place, k * cap, cap) for k in [0] + late], axis=0)
-    mixed = sum_ref[...] + dot(select, buffer[...], ((0,), (0,)))
+    mixed = sum_ref[...] + dot(select_ref[...], buffer[...])
     mixed_ref[...] = mixed.astype(BF16)
     z = layer_norm(mixed, gain_ref[...])
     head, feature = iota((width, HEADS), 1), iota((width, HEADS), 0)
@@ -309,10 +309,11 @@
         last = lefts[k][0]
     lefts[0] = expert(False, partner[0], 2, last)
     early = [1, 2]
-    partial, query = call(
-        functools.partial(partial_kernel, early),
+    late = list(range(3, experts))
+    partial, query, select = call(
+        functools.partial(partial_kernel, early, late),
         "partial",
-        [((rows, width), F32), ((2, width), F32)],
+        [((rows, width), F32), ((2, width), F32), ((rows, (1 + len(late)) * cap), BF16)],
         [VMEM] * 4,
         8,
         [pltpu.VMEM((2 * cap, width), BF16)],
@@ -321,9 +322,8 @@
         finish(k, partial)
     kept, gate = owns[0]
     got = [swap(after(term, partial), 2) for term in lefts[0]]
-    late = list(range(3, experts))
     mixed, pooled = call(
-        functools.partial(combine_kernel, late),
+        combine_kernel,
         "combine",
         [((rows, width), BF16), ((4, width), BF16)],
         [SMEM] + [VMEM] * (9 + len(late)),
@@ -336,7 +336,7 @@
         gate,
         kept,
         *got,
-        place,
+        select,
         out_gain.reshape(1, width),
         query,
         *[swap(final[k], SPLIT * k) for k in late],

time: 104 us -> 104 us (level)
  no operation moved by 1% of the time
where the time goes in v6:
time: 104 us; the launch traced here: 103 us
  waiting for transfers between devices  36.7 us (35%)
  starting transfers between devices  32.5 us (31%)
  Pallas kernels  30 us (29%)
  between operations  2.29 us (2%)
  local copies, waits for them, and re-layouts  1.87 us (2%)
    ppermute x21, waiting for transfers between devices, swap(): return lax.ppermute(values, 'dp', [(i, i ^ bits) for i in range(devices)])  36.7 us
    ppermute x21, starting transfers between devices, swap(): return lax.ppermute(values, 'dp', [(i, i ^ bits) for i in range(devices)])  32.5 us
    pallas_call x8, Pallas kernels, expert(): call(functools.partial(ffn_kernel, own), 'own' if own else 'other', outs,...  18.9 us
    pallas_call x1, Pallas kernels, on_device(): call(functools.partial(tail_kernel, devices), 'contrast', [((2, width), F...  5.95 us
    pallas_call x1, Pallas kernels, on_device(): call(combine_kernel, 'combine', [((rows, width), BF16), ((4, width), BF16...  2.87 us
  transfers between devices with their start and end apart: 21, of which 15 were waited for; matrix products, arithmetic and copies ran while one was open for 0% of the time, Pallas kernels for 20%

profile of v6, /device:TPU:0, one launch (start us, length us, event | category | flops | bytes accessed | tf_op | source)
XLA Modules:
  0.0 103.4 jit_solution(9656566376228604538)
XLA Ops:
  0.6 0.5 collective-permute-start.2
  1.2 0.1 collective-permute-start.1
  1.2 1.1 %copy-done.5 = bf16[1,320,1280]{2,1,0:T(8,128)(2,1)S(1)} copy-done((bf16[1,320,1280]{2,1,0:T(8,128)(2,1)S(1)}, bf16[1,320,1280]{2,1,0:T(8,128)(2,1)}, u32[]{:S(2)}) %copy-start.5) | copy-done | bytes 819224
  2.4 0.7 copy-done.6
  3.1 1.0 dispatch.1
  4.1 3.1 %collective-permute-start = (bf16[128,1280]{1,0:T(8,128)(2,1)S(1)}, bf16[128,1280]{1,0:T(8,128)(2,1)S(1)}, u32[]{:S(2)}, u32[]{:S(2)}) collective-permute-start(bf16[128,1280]{1,0:T(8,128)(2,1)S(1)} %get-tuple-element.46), channel_id=1, source_target_pairs={{0,4},{1,5},{2,6},{3,7},{4,0},{5,1},{6,2},{7,3},{8,12},{9,13},{10,... | collective-permute-start | bytes 983048 | tf_op jit(solution)/shard_map/ppermute | solution.py:256
  7.1 2.6 %collective-permute-start.4 = (bf16[128,1280]{1,0:T(8,128)(2,1)S(1)}, bf16[128,1280]{1,0:T(8,128)(2,1)S(1)}, u32[]{:S(2)}, u32[]{:S(2)}) collective-permute-start(bf16[128,1280]{1,0:T(8,128)(2,1)S(1)} %get-tuple-element.52), channel_id=1, source_target_pairs={{0,8},{1,9},{2,10},{3,11},{4,12},{5,13},{6,14},{7,15},{8,0},{9,1},... | collective-permute-start | bytes 983048 | tf_op jit(solution)/shard_map/ppermute | solution.py:256
  9.7 1.5 %collective-permute-start.5 = (bf16[128,1280]{1,0:T(8,128)(2,1)S(1)}, bf16[128,1280]{1,0:T(8,128)(2,1)S(1)}, u32[]{:S(2)}, u32[]{:S(2)}) collective-permute-start(bf16[128,1280]{1,0:T(8,128)(2,1)S(1)} %get-tuple-element.47.rows_ref.refs_2_), channel_id=1, source_target_pairs={{0,2},{1,3},{2,0},{3,1},{4,6},{5,7},{6,4},{7,5},{8,10},{9,11},{10,... | collective-permute-start | bytes 983048 | tf_op jit(solution)/shard_map/ppermute | solution.py:256
  11.3 0.0 collective-permute-done.2.out_b
  11.3 0.3 collective-permute-done.1.in_b
  11.5 2.4 %own.4 = (f32[128,1280]{1,0:T(8,128)S(1)}, f32[128,1]{1,0:T(8,128)S(1)}) custom-call(s32[1]{0:T(128)} %bitcast.mine_ref, bf16[128,1280]{1,0:T(8,128)(2,1)S(1)} %get-tuple-element.47.rows_ref.refs_2_, f32[1,1280]{1,0:T(1,128)S(1)} %reshape.42.gain_ref, bf16[4,1280]{1,0:T(4,128)(2,1)S(1)} %bitcast.27, bf16[1280,1280]{1,0:T(8,128)(2,1)S(1)} %bitcast.10, ...), custom_call_target="tpu_custom_call" | custom-call | tf_op jit(solution)/shard_map/own/pallas_call | solution.py:272
  13.9 8.1 %collective-permute-done.rows_ref.tokens_ref = bf16[128,1280]{1,0:T(8,128)(2,1)S(1)} collective-permute-done((bf16[128,1280]{1,0:T(8,128)(2,1)S(1)}, bf16[128,1280]{1,0:T(8,128)(2,1)S(1)}, u32[]{:S(2)}, u32[]{:S(2)}) %collective-permute-start) | collective-permute-done | bytes 327712 | tf_op jit(solution)/shard_map/ppermute | solution.py:256
  22.0 1.7 %collective-permute-start.3 = (bf16[128,1280]{1,0:T(8,128)(2,1)S(1)}, bf16[128,1280]{1,0:T(8,128)(2,1)S(1)}, u32[]{:S(2)}, u32[]{:S(2)}) collective-permute-start(bf16[128,1280]{1,0:T(8,128)(2,1)S(1)} %collective-permute-done.rows_ref.tokens_ref), channel_id=1, source_target_pairs={{0,2},{1,3},{2,0},{3,1},{4,6},{5,7},{6,4},{7,5},{8,10},{9,11},{10,... | collective-permute-start | bytes 983048 | tf_op jit(solution)/shard_map/ppermute | solution.py:256
  23.7 0.8 collective-permute-done.4.rows_ref.tokens_ref
  24.5 1.5 %collective-permute-start.6 = (bf16[128,1280]{1,0:T(8,128)(2,1)S(1)}, bf16[128,1280]{1,0:T(8,128)(2,1)S(1)}, u32[]{:S(2)}, u32[]{:S(2)}) collective-permute-start(bf16[128,1280]{1,0:T(8,128)(2,1)S(1)} %collective-permute-done.4.rows_ref.tokens_ref), channel_id=1, source_target_pairs={{0,2},{1,3},{2,0},{3,1},{4,6},{5,7},{6,4},{7,5},{8,10},{9,11},{10,... | collective-permute-start | bytes 983048 | tf_op jit(solution)/shard_map/ppermute | solution.py:256
  26.0 2.5 %collective-permute-start.9 = (bf16[128,1280]{1,0:T(8,128)(2,1)S(1)}, bf16[128,1280]{1,0:T(8,128)(2,1)S(1)}, u32[]{:S(2)}, u32[]{:S(2)}) collective-permute-start(bf16[128,1280]{1,0:T(8,128)(2,1)S(1)} %get-tuple-element.64), channel_id=1, source_target_pairs={{0,12},{1,13},{2,14},{3,15},{4,8},{5,9},{6,10},{7,11},{8,4},{9,5},... | collective-permute-start | bytes 983048 | tf_op jit(solution)/shard_map/ppermute | solution.py:256
  28.5 0.0 collective-permute-done.5.rows_ref
  28.5 2.4 %own.5 = (f32[128,1280]{1,0:T(8,128)S(1)}, f32[128,1]{1,0:T(8,128)S(1)}) custom-call(s32[1]{0:T(128)} %bitcast.mine_ref, bf16[128,1280]{1,0:T(8,128)(2,1)S(1)} %collective-permute-done.4.rows_ref.tokens_ref, f32[1,1280]{1,0:T(1,128)S(1)} %reshape.42.gain_ref, bf16[4,1280]{1,0:T(4,128)(2,1)S(1)} %bitcast.28, bf16[1280,1280]{1,0:T(8,128)(2,1)S(1)} %bitcast.11, ...), custom_call_target="tpu_custom_call" | custom-call | tf_op jit(solution)/shard_map/own/pallas_call | solution.py:272
  30.9 1.7 %collective-permute-done.3.rows_ref = bf16[128,1280]{1,0:T(8,128)(2,1)S(1)} collective-permute-done((bf16[128,1280]{1,0:T(8,128)(2,1)S(1)}, bf16[128,1280]{1,0:T(8,128)(2,1)S(1)}, u32[]{:S(2)}, u32[]{:S(2)}) %collective-permute-start.3) | collective-permute-done | bytes 327712 | tf_op jit(solution)/shard_map/ppermute | solution.py:256
  32.6 2.4 %own.6 = (f32[128,1280]{1,0:T(8,128)S(1)}, f32[128,1]{1,0:T(8,128)S(1)}) custom-call(s32[1]{0:T(128)} %bitcast.mine_ref, bf16[128,1280]{1,0:T(8,128)(2,1)S(1)} %collective-permute-done.rows_ref.tokens_ref, f32[1,1280]{1,0:T(1,128)S(1)} %reshape.42.gain_ref, bf16[4,1280]{1,0:T(4,128)(2,1)S(1)} %bitcast.29, bf16[1280,1280]{1,0:T(8,128)(2,1)S(1)} %bitcast.12, ...), custom_call_target="tpu_custom_call" | custom-call | tf_op jit(solution)/shard_map/own/pallas_call | solution.py:272
  35.0 2.3 %other.4 = bf16[128,1280]{1,0:T(8,128)(2,1)S(1)} custom-call(s32[1]{0:T(128)} %bitcast.mine_ref, bf16[128,1280]{1,0:T(8,128)(2,1)S(1)} %collective-permute-done.3.rows_ref, f32[1,1280]{1,0:T(1,128)S(1)} %reshape.42.gain_ref, bf16[4,1280]{1,0:T(4,128)(2,1)S(1)} %bitcast.30, bf16[1280,1280]{1,0:T(8,128)(2,1)S(1)} %bitcast.13, bf16[1280,1280]{1,0:T(8,128)(2,1)S(1)} %bitcast.22, ...), custom_call_target="tpu_custom_call" | custom-call | tf_op jit(solution)/shard_map/other/pallas_call | solution.py:272
  37.4 1.8 %collective-permute-start.7 = (bf16[128,1280]{1,0:T(8,128)(2,1)S(1)}, bf16[128,1280]{1,0:T(8,128)(2,1)S(1)}, u32[]{:S(2)}, u32[]{:S(2)}) collective-permute-start(bf16[128,1280]{1,0:T(8,128)(2,1)S(1)} %other.4), channel_id=1, source_target_pairs={{0,2},{1,3},{2,0},{3,1},{4,6},{5,7},{6,4},{7,5},{8,10},{9,11},{10,... | collective-permute-start | bytes 983048 | tf_op jit(solution)/shard_map/ppermute | solution.py:256
  39.1 0.0 collective-permute-done.6.rows_ref
  39.1 2.3 %other.5 = bf16[128,1280]{1,0:T(8,128)(2,1)S(1)} custom-call(s32[1]{0:T(128)} %bitcast.mine_ref, bf16[128,1280]{1,0:T(8,128)(2,1)S(1)} %collective-permute-done.6.rows_ref, f32[1,1280]{1,0:T(1,128)S(1)} %reshape.42.gain_ref, bf16[4,1280]{1,0:T(4,128)(2,1)S(1)} %bitcast.31, bf16[1280,1280]{1,0:T(8,128)(2,1)S(1)} %bitcast.14, bf16[1280,1280]{1,0:T(8,128)(2,1)S(1)} %bitcast.23, ...), custom_call_target="tpu_custom_call" | custom-call | tf_op jit(solution)/shard_map/other/pallas_call | solution.py:272
  41.5 1.7 %collective-permute-start.10 = (bf16[128,1280]{1,0:T(8,128)(2,1)S(1)}, bf16[128,1280]{1,0:T(8,128)(2,1)S(1)}, u32[]{:S(2)}, u32[]{:S(2)}) collective-permute-start(bf16[128,1280]{1,0:T(8,128)(2,1)S(1)} %other.5), channel_id=1, source_target_pairs={{0,2},{1,3},{2,0},{3,1},{4,6},{5,7},{6,4},{7,5},{8,10},{9,11},{10,... | collective-permute-start | bytes 983048 | tf_op jit(solution)/shard_map/ppermute | solution.py:256
  43.2 0.0 collective-permute-done.9.rows_ref.tokens_ref
  43.2 0.4 collective-permute-start.12
  43.6 4.5 %collective-permute-done.7.refs_0_ = bf16[128,1280]{1,0:T(8,128)(2,1)S(1)} collective-permute-done((bf16[128,1280]{1,0:T(8,128)(2,1)S(1)}, bf16[128,1280]{1,0:T(8,128)(2,1)S(1)}, u32[]{:S(2)}, u32[]{:S(2)}) %collective-permute-start.7) | collective-permute-done | bytes 327712 | tf_op jit(solution)/shard_map/ppermute | solution.py:256
  48.1 0.3 finish.3
  48.4 0.1 collective-permute-start.8
  48.5 2.4 %own.7 = (f32[128,1280]{1,0:T(8,128)S(1)}, f32[128,1]{1,0:T(8,128)S(1)}) custom-call(s32[1]{0:T(128)} %bitcast.mine_ref, bf16[128,1280]{1,0:T(8,128)(2,1)S(1)} %collective-permute-done.9.rows_ref.tokens_ref, f32[1,1280]{1,0:T(1,128)S(1)} %reshape.42.gain_ref, bf16[4,1280]{1,0:T(4,128)(2,1)S(1)} %bitcast.32, bf16[1280,1280]{1,0:T(8,128)(2,1)S(1)} %bitcast.15, ...), custom_call_target="tpu_custom_call" | custom-call | tf_op jit(solution)/shard_map/own/pallas_call | solution.py:272
  50.9 4.2 %collective-permute-done.10.refs_0_ = bf16[128,1280]{1,0:T(8,128)(2,1)S(1)} collective-permute-done((bf16[128,1280]{1,0:T(8,128)(2,1)S(1)}, bf16[128,1280]{1,0:T(8,128)(2,1)S(1)}, u32[]{:S(2)}, u32[]{:S(2)}) %collective-permute-start.10) | collective-permute-done | bytes 327712 | tf_op jit(solution)/shard_map/ppermute | solution.py:256
  55.1 0.2 finish.4
  55.3 0.8 collective-permute-start.11
  56.1 3.2 %collective-permute-done.12.rows_ref = bf16[128,1280]{1,0:T(8,128)(2,1)S(1)} collective-permute-done((bf16[128,1280]{1,0:T(8,128)(2,1)S(1)}, bf16[128,1280]{1,0:T(8,128)(2,1)S(1)}, u32[]{:S(2)}, u32[]{:S(2)}) %collective-permute-start.12) | collective-permute-done | bytes 327712 | tf_op jit(solution)/shard_map/ppermute | solution.py:256
  59.3 2.3 %other.6 = bf16[128,1280]{1,0:T(8,128)(2,1)S(1)} custom-call(s32[1]{0:T(128)} %bitcast.mine_ref, bf16[128,1280]{1,0:T(8,128)(2,1)S(1)} %collective-permute-done.12.rows_ref, f32[1,1280]{1,0:T(1,128)S(1)} %reshape.42.gain_ref, bf16[4,1280]{1,0:T(4,128)(2,1)S(1)} %bitcast.33, bf16[1280,1280]{1,0:T(8,128)(2,1)S(1)} %bitcast.16, ...), custom_call_target="tpu_custom_call" | custom-call | tf_op jit(solution)/shard_map/other/pallas_call | solution.py:272
  61.6 0.0 copy-start.4
  61.6 0.0 copy-start.8
  61.6 1.4 %collective-permute-start.15 = (bf16[128,1280]{1,0:T(8,128)(2,1)S(1)}, bf16[128,1280]{1,0:T(8,128)(2,1)S(1)}, u32[]{:S(2)}, u32[]{:S(2)}) collective-permute-start(bf16[128,1280]{1,0:T(8,128)(2,1)S(1)} %other.6), channel_id=1, source_target_pairs={{0,2},{1,3},{2,0},{3,1},{4,6},{5,7},{6,4},{7,5},{8,10},{9,11},{10,... | collective-permute-start | bytes 983048 | tf_op jit(solution)/shard_map/ppermute | solution.py:256
  63.0 2.3 %other.7 = (bf16[128,1280]{1,0:T(8,128)(2,1)S(1)}, bf16[64,1280]{1,0:T(8,128)(2,1)S(1)}) custom-call(s32[1]{0:T(128)} %bitcast.mine_ref, bf16[128,1280]{1,0:T(8,128)(2,1)S(1)} %collective-permute-done.5.rows_ref, f32[1,1280]{1,0:T(1,128)S(1)} %reshape.42.gain_ref, bf16[4,1280]{1,0:T(4,128)(2,1)S(1)} %bitcast.34, bf16[1280,1280]{1,0:T(8,128)(2,1)S(1)} %bitcast.17, ...), custom_call_target="tpu_custom_call" | custom-call | tf_op jit(solution)/shard_map/other/pallas_call | solution.py:272
  65.4 0.0 copy-start.2
  65.4 0.0 collective-permute-done.8.refs_0_
  65.4 1.5 %collective-permute-done.11.refs_1_ = bf16[128,1280]{1,0:T(8,128)(2,1)S(1)} collective-permute-done((bf16[128,1280]{1,0:T(8,128)(2,1)S(1)}, bf16[128,1280]{1,0:T(8,128)(2,1)S(1)}, u32[]{:S(2)}, u32[]{:S(2)}) %collective-permute-start.11) | collective-permute-done | bytes 327712 | tf_op jit(solution)/shard_map/ppermute | solution.py:256
  66.9 0.0 copy-done.4
  66.9 0.6 partial.1
  67.5 1.6 %collective-permute-start.13 = (bf16[128,1280]{1,0:T(8,128)(2,1)S(1)}, bf16[128,1280]{1,0:T(8,128)(2,1)S(1)}, u32[]{:S(2)}, u32[]{:S(2)}) collective-permute-start(bf16[128,1280]{1,0:T(8,128)(2,1)S(1)} %get-tuple-element.74), channel_id=1, source_target_pairs={{0,2},{1,3},{2,0},{3,1},{4,6},{5,7},{6,4},{7,5},{8,10},{9,11},{10,... | collective-permute-start | bytes 983048 | tf_op jit(solution)/shard_map/ppermute | solution.py:256
  69.1 1.7 %collective-permute-done.15.refs_0_ = bf16[128,1280]{1,0:T(8,128)(2,1)S(1)} collective-permute-done((bf16[128,1280]{1,0:T(8,128)(2,1)S(1)}, bf16[128,1280]{1,0:T(8,128)(2,1)S(1)}, u32[]{:S(2)}, u32[]{:S(2)}) %collective-permute-start.15) | collective-permute-done | bytes 327712 | tf_op jit(solution)/shard_map/ppermute | solution.py:256
  70.8 0.2 finish.5
  70.9 2.6 %collective-permute-start.16 = (bf16[128,1280]{1,0:T(8,128)(2,1)S(1)}, bf16[128,1280]{1,0:T(8,128)(2,1)S(1)}, u32[]{:S(2)}, u32[]{:S(2)}) collective-permute-start(bf16[128,1280]{1,0:T(8,128)(2,1)S(1)} %finish.5), channel_id=1, source_target_pairs={{0,12},{1,13},{2,14},{3,15},{4,8},{5,9},{6,10},{7,11},{8,4},{9,5},... | collective-permute-start | bytes 983048 | tf_op jit(solution)/shard_map/ppermute | solution.py:256
  73.6 1.6 %collective-permute-start.14 = (bf16[64,1280]{1,0:T(8,128)(2,1)S(1)}, bf16[64,1280]{1,0:T(8,128)(2,1)S(1)}, u32[]{:S(2)}, u32[]{:S(2)}) collective-permute-start(bf16[64,1280]{1,0:T(8,128)(2,1)S(1)} %get-tuple-element.76), channel_id=1, source_target_pairs={{0,2},{1,3},{2,0},{3,1},{4,6},{5,7},{6,4},{7,5},{8,10},{9,11},{10,... | collective-permute-start | bytes 491528 | tf_op jit(solution)/shard_map/ppermute | solution.py:256
  75.8 0.0 copy-done.8
  75.8 3.5 %collective-permute-done.14.refs_6_ = bf16[64,1280]{1,0:T(8,128)(2,1)S(1)} collective-permute-done((bf16[64,1280]{1,0:T(8,128)(2,1)S(1)}, bf16[64,1280]{1,0:T(8,128)(2,1)S(1)}, u32[]{:S(2)}, u32[]{:S(2)}) %collective-permute-start.14) | collective-permute-done | bytes 163872 | tf_op jit(solution)/shard_map/ppermute | solution.py:256
  79.3 0.0 collective-permute-done.13.refs_5_
  79.3 0.7 collective-permute-done.16.refs_10_
  80.0 2.9 %combine.1 = (bf16[320,1280]{1,0:T(8,128)(2,1)}, bf16[4,1280]{1,0:T(4,128)(2,1)S(1)}) custom-call(s32[1]{0:T(128)S(6)} %copy.15.refs_0_, f32[320,1280]{1,0:T(8,128)S(1)} %get-tuple-element.68.refs_1_, bf16[128,1280]{1,0:T(8,128)(2,1)S(1)} %get-tuple-element.47.rows_ref.refs_2_, f32[128,1]{1,0:T(8,128)S(1)} %get-tuple-element.69.refs_3_, ...), custom_call_target="tpu_custom_call" | custom-call | tf_op jit(solution)/shard_map/combine/pallas_call | solution.py:325
  82.9 3.3 %collective-permute-start.17 = (bf16[4,1280]{1,0:T(4,128)(2,1)S(1)}, bf16[4,1280]{1,0:T(4,128)(2,1)S(1)}, u32[]{:S(2)}, u32[]{:S(2)}) collective-permute-start(bf16[4,1280]{1,0:T(4,128)(2,1)S(1)} %get-tuple-element.82.refs_0_), channel_id=1, source_target_pairs={{0,8},{1,9},{2,10},{3,11},{4,12},{5,13},{6,14},{7,15},{8,0},{9,1},... | collective-permute-start | bytes 30728 | tf_op jit(solution)/shard_map/ppermute | solution.py:256
  86.2 1.7 %collective-permute-done.17.refs_1_ = bf16[4,1280]{1,0:T(4,128)(2,1)S(1)} collective-permute-done((bf16[4,1280]{1,0:T(4,128)(2,1)S(1)}, bf16[4,1280]{1,0:T(4,128)(2,1)S(1)}, u32[]{:S(2)}, u32[]{:S(2)}) %collective-permute-start.17) | collective-permute-done | bytes 10272 | tf_op jit(solution)/shard_map/ppermute | solution.py:256
  87.9 1.5 %collective-permute-start.18 = (bf16[8,1280]{1,0:T(8,128)(2,1)S(1)}, bf16[8,1280]{1,0:T(8,128)(2,1)S(1)}, u32[]{:S(2)}, u32[]{:S(2)}) collective-permute-start(bf16[8,1280]{1,0:T(8,128)(2,1)S(1)} %pad_maximum_fusion.2), channel_id=1, source_target_pairs={{0,4},{1,5},{2,6},{3,7},{4,0},{5,1},{6,2},{7,3},{8,12},{9,13},{10,... | collective-permute-start | bytes 61448 | tf_op jit(solution)/shard_map/ppermute | solution.py:256
  89.4 2.3 %collective-permute-done.18.refs_2_ = bf16[8,1280]{1,0:T(8,128)(2,1)S(1)} collective-permute-done((bf16[8,1280]{1,0:T(8,128)(2,1)S(1)}, bf16[8,1280]{1,0:T(8,128)(2,1)S(1)}, u32[]{:S(2)}, u32[]{:S(2)}) %collective-permute-start.18) | collective-permute-done | bytes 20512 | tf_op jit(solution)/shard_map/ppermute | solution.py:256
  91.8 2.2 %collective-permute-start.19 = (bf16[16,1280]{1,0:T(8,128)(2,1)S(1)}, bf16[16,1280]{1,0:T(8,128)(2,1)S(1)}, u32[]{:S(2)}, u32[]{:S(2)}) collective-permute-start(bf16[16,1280]{1,0:T(8,128)(2,1)S(1)} %pad_maximum_fusion.1), channel_id=1, source_target_pairs={{0,2},{1,3},{2,0},{3,1},{4,6},{5,7},{6,4},{7,5},{8,10},{9,11},{10,... | collective-permute-start | bytes 122888 | tf_op jit(solution)/shard_map/ppermute | solution.py:256
  94.0 2.0 %collective-permute-done.19.refs_3_ = bf16[16,1280]{1,0:T(8,128)(2,1)S(1)} collective-permute-done((bf16[16,1280]{1,0:T(8,128)(2,1)S(1)}, bf16[16,1280]{1,0:T(8,128)(2,1)S(1)}, u32[]{:S(2)}, u32[]{:S(2)}) %collective-permute-start.19) | collective-permute-done | bytes 40992 | tf_op jit(solution)/shard_map/ppermute | solution.py:256
  96.0 0.1 collective-permute-start.20
  96.7 0.6 collective-permute-done.20.refs_4_
  97.3 6.0 %contrast.1 = (f32[2,1280]{1,0:T(2,128)}, f32[1,1]{1,0:T(1,128)}, f32[1280,1280]{1,0:T(8,128)}) custom-call(s32[1]{0:T(128)} %bitcast.mine_ref, f32[1]{0:T(128)S(6)} %copy.16.scale_ref, bf16[1280,1280]{1,0:T(8,128)(2,1)S(1)} %copy-done.2, bf16[4,1280]{1,0:T(4,128)(2,1)S(1)} %get-tuple-element.82.refs_0_, ...), custom_call_target="tpu_custom_call" | custom-call | tf_op jit(solution)/shard_map/contrast/pallas_call | solution.py:348
  (16 shorter events, 0.1 us)
Async XLA Ops:
  0.6 10.6 %collective-permute-start.2 = (bf16[1280,1280]{1,0:T(8,128)(2,1)}, bf16[1280,1280]{1,0:T(8,128)(2,1)S(1)}, u32[]{:S(2)}, u32[]{:S(2)}) collective-permute-start(bf16[1280,1280]{1,0:T(8,128)(2,1)} %bitcast.18), channel_id=1, source_target_pairs={{0,1},{1,0},{2,3},{3,2},{4,5},{5,4},{6,7},{7,6},{8,9},{9,8},{10,11... | collective-permute-start | bytes 9830408 | tf_op jit(solution)/shard_map/ppermute | solution.py:256
  1.2 10.4 %collective-permute-start.1 = (bf16[1280,1280]{1,0:T(8,128)(2,1)}, bf16[1280,1280]{1,0:T(8,128)(2,1)S(1)}, u32[]{:S(2)}, u32[]{:S(2)}) collective-permute-start(bf16[1280,1280]{1,0:T(8,128)(2,1)} %bitcast.9), channel_id=1, source_target_pairs={{0,1},{1,0},{2,3},{3,2},{4,5},{5,4},{6,7},{7,6},{8,9},{9,8},{10,11... | collective-permute-start | bytes 9830408 | tf_op jit(solution)/shard_map/ppermute | solution.py:256
  1.2 1.1 %copy-start.5 = (bf16[1,320,1280]{2,1,0:T(8,128)(2,1)S(1)}, bf16[1,320,1280]{2,1,0:T(8,128)(2,1)}, u32[]{:S(2)}) copy-start(bf16[1,320,1280]{2,1,0:T(8,128)(2,1)} %param.11) | copy-start | bytes 2457604
  2.4 0.7 copy-start.6
  3.1 8.2 %copy-start.7 = (f32[1280]{0:T(1024)S(1)}, f32[1280]{0:T(1024)}, u32[]{:S(2)}) copy-start(f32[1280]{0:T(1024)} %param.14) | copy-start | bytes 15364
  3.1 8.5 %copy-start = (bf16[1,1280,1280]{2,1,0:T(8,128)(2,1)S(1)}, bf16[1,1280,1280]{2,1,0:T(8,128)(2,1)}, u32[]{:S(2)}) copy-start(bf16[1,1280,1280]{2,1,0:T(8,128)(2,1)} %param.16) | copy-start | bytes 9830404
  3.1 8.5 %copy-start.1 = (bf16[1,1280,1280]{2,1,0:T(8,128)(2,1)S(1)}, bf16[1,1280,1280]{2,1,0:T(8,128)(2,1)}, u32[]{:S(2)}) copy-start(bf16[1,1280,1280]{2,1,0:T(8,128)(2,1)} %param.17) | copy-start | bytes 9830404
  3.1 8.5 %copy-start.3 = (bf16[1280,4]{0,1:T(4,128)(2,1)S(1)}, bf16[1280,4]{0,1:T(4,128)(2,1)}, u32[]{:S(2)}) copy-start(bf16[1280,4]{0,1:T(4,128)(2,1)} %param.15) | copy-start | bytes 30724
  4.1 17.9 %collective-permute-start = (bf16[128,1280]{1,0:T(8,128)(2,1)S(1)}, bf16[128,1280]{1,0:T(8,128)(2,1)S(1)}, u32[]{:S(2)}, u32[]{:S(2)}) collective-permute-start(bf16[128,1280]{1,0:T(8,128)(2,1)S(1)} %get-tuple-element.46), channel_id=1, source_target_pairs={{0,4},{1,5},{2,6},{3,7},{4,0},{5,1},{6,2},{7,3},{8,12},{9,13},{10,... | collective-permute-start | bytes 983048 | tf_op jit(solution)/shard_map/ppermute | solution.py:256
  7.1 17.4 %collective-permute-start.4 = (bf16[128,1280]{1,0:T(8,128)(2,1)S(1)}, bf16[128,1280]{1,0:T(8,128)(2,1)S(1)}, u32[]{:S(2)}, u32[]{:S(2)}) collective-permute-start(bf16[128,1280]{1,0:T(8,128)(2,1)S(1)} %get-tuple-element.52), channel_id=1, source_target_pairs={{0,8},{1,9},{2,10},{3,11},{4,12},{5,13},{6,14},{7,15},{8,0},{9,1},... | collective-permute-start | bytes 983048 | tf_op jit(solution)/shard_map/ppermute | solution.py:256
  9.7 18.8 %collective-permute-start.5 = (bf16[128,1280]{1,0:T(8,128)(2,1)S(1)}, bf16[128,1280]{1,0:T(8,128)(2,1)S(1)}, u32[]{:S(2)}, u32[]{:S(2)}) collective-permute-start(bf16[128,1280]{1,0:T(8,128)(2,1)S(1)} %get-tuple-element.47.rows_ref.refs_2_), channel_id=1, source_target_pairs={{0,2},{1,3},{2,0},{3,1},{4,6},{5,7},{6,4},{7,5},{8,10},{9,11},{10,... | collective-permute-start | bytes 983048 | tf_op jit(solution)/shard_map/ppermute | solution.py:256
  22.0 10.6 %collective-permute-start.3 = (bf16[128,1280]{1,0:T(8,128)(2,1)S(1)}, bf16[128,1280]{1,0:T(8,128)(2,1)S(1)}, u32[]{:S(2)}, u32[]{:S(2)}) collective-permute-start(bf16[128,1280]{1,0:T(8,128)(2,1)S(1)} %collective-permute-done.rows_ref.tokens_ref), channel_id=1, source_target_pairs={{0,2},{1,3},{2,0},{3,1},{4,6},{5,7},{6,4},{7,5},{8,10},{9,11},{10,... | collective-permute-start | bytes 983048 | tf_op jit(solution)/shard_map/ppermute | solution.py:256
  24.5 14.6 %collective-permute-start.6 = (bf16[128,1280]{1,0:T(8,128)(2,1)S(1)}, bf16[128,1280]{1,0:T(8,128)(2,1)S(1)}, u32[]{:S(2)}, u32[]{:S(2)}) collective-permute-start(bf16[128,1280]{1,0:T(8,128)(2,1)S(1)} %collective-permute-done.4.rows_ref.tokens_ref), channel_id=1, source_target_pairs={{0,2},{1,3},{2,0},{3,1},{4,6},{5,7},{6,4},{7,5},{8,10},{9,11},{10,... | collective-permute-start | bytes 983048 | tf_op jit(solution)/shard_map/ppermute | solution.py:256
  26.0 17.1 %collective-permute-start.9 = (bf16[128,1280]{1,0:T(8,128)(2,1)S(1)}, bf16[128,1280]{1,0:T(8,128)(2,1)S(1)}, u32[]{:S(2)}, u32[]{:S(2)}) collective-permute-start(bf16[128,1280]{1,0:T(8,128)(2,1)S(1)} %get-tuple-element.64), channel_id=1, source_target_pairs={{0,12},{1,13},{2,14},{3,15},{4,8},{5,9},{6,10},{7,11},{8,4},{9,5},... | collective-permute-start | bytes 983048 | tf_op jit(solution)/shard_map/ppermute | solution.py:256
  37.4 10.7 %collective-permute-start.7 = (bf16[128,1280]{1,0:T(8,128)(2,1)S(1)}, bf16[128,1280]{1,0:T(8,128)(2,1)S(1)}, u32[]{:S(2)}, u32[]{:S(2)}) collective-permute-start(bf16[128,1280]{1,0:T(8,128)(2,1)S(1)} %other.4), channel_id=1, source_target_pairs={{0,2},{1,3},{2,0},{3,1},{4,6},{5,7},{6,4},{7,5},{8,10},{9,11},{10,... | collective-permute-start | bytes 983048 | tf_op jit(solution)/shard_map/ppermute | solution.py:256
  41.5 13.6 %collective-permute-start.10 = (bf16[128,1280]{1,0:T(8,128)(2,1)S(1)}, bf16[128,1280]{1,0:T(8,128)(2,1)S(1)}, u32[]{:S(2)}, u32[]{:S(2)}) collective-permute-start(bf16[128,1280]{1,0:T(8,128)(2,1)S(1)} %other.5), channel_id=1, source_target_pairs={{0,2},{1,3},{2,0},{3,1},{4,6},{5,7},{6,4},{7,5},{8,10},{9,11},{10,... | collective-permute-start | bytes 983048 | tf_op jit(solution)/shard_map/ppermute | solution.py:256
  43.2 16.1 %collective-permute-start.12 = (bf16[128,1280]{1,0:T(8,128)(2,1)S(1)}, bf16[128,1280]{1,0:T(8,128)(2,1)S(1)}, u32[]{:S(2)}, u32[]{:S(2)}) collective-permute-start(bf16[128,1280]{1,0:T(8,128)(2,1)S(1)} %collective-permute-done.9.rows_ref.tokens_ref), channel_id=1, source_target_pairs={{0,2},{1,3},{2,0},{3,1},{4,6},{5,7},{6,4},{7,5},{8,10},{9,11},{10,... | collective-permute-start | bytes 983048 | tf_op jit(solution)/shard_map/ppermute | solution.py:256
  48.4 17.0 %collective-permute-start.8 = (bf16[128,1280]{1,0:T(8,128)(2,1)S(1)}, bf16[128,1280]{1,0:T(8,128)(2,1)S(1)}, u32[]{:S(2)}, u32[]{:S(2)}) collective-permute-start(bf16[128,1280]{1,0:T(8,128)(2,1)S(1)} %finish.3), channel_id=1, source_target_pairs={{0,4},{1,5},{2,6},{3,7},{4,0},{5,1},{6,2},{7,3},{8,12},{9,13},{10,... | collective-permute-start | bytes 983048 | tf_op jit(solution)/shard_map/ppermute | solution.py:256
  55.3 11.7 %collective-permute-start.11 = (bf16[128,1280]{1,0:T(8,128)(2,1)S(1)}, bf16[128,1280]{1,0:T(8,128)(2,1)S(1)}, u32[]{:S(2)}, u32[]{:S(2)}) collective-permute-start(bf16[128,1280]{1,0:T(8,128)(2,1)S(1)} %finish.4), channel_id=1, source_target_pairs={{0,8},{1,9},{2,10},{3,11},{4,12},{5,13},{6,14},{7,15},{8,0},{9,1},... | collective-permute-start | bytes 983048 | tf_op jit(solution)/shard_map/ppermute | solution.py:256
  61.6 5.4 %copy-start.4 = (f32[2,16,80]{2,1,0:T(8,128)S(1)}, f32[2,16,80]{2,1,0:T(8,128)}, u32[]{:S(2)}) copy-start(f32[2,16,80]{2,1,0:T(8,128)} %query_ref.1) | copy-start | bytes 30724
  61.6 14.2 %copy-start.8 = (f32[1280]{0:T(1024)S(1)}, f32[1280]{0:T(1024)}, u32[]{:S(2)}) copy-start(f32[1280]{0:T(1024)} %param.18) | copy-start | bytes 15364
  61.6 9.2 %collective-permute-start.15 = (bf16[128,1280]{1,0:T(8,128)(2,1)S(1)}, bf16[128,1280]{1,0:T(8,128)(2,1)S(1)}, u32[]{:S(2)}, u32[]{:S(2)}) collective-permute-start(bf16[128,1280]{1,0:T(8,128)(2,1)S(1)} %other.6), channel_id=1, source_target_pairs={{0,2},{1,3},{2,0},{3,1},{4,6},{5,7},{6,4},{7,5},{8,10},{9,11},{10,... | collective-permute-start | bytes 983048 | tf_op jit(solution)/shard_map/ppermute | solution.py:256
  65.4 31.9 %copy-start.2 = (bf16[1280,1280]{1,0:T(8,128)(2,1)S(1)}, bf16[1280,1280]{1,0:T(8,128)(2,1)}, u32[]{:S(2)}) copy-start(bf16[1280,1280]{1,0:T(8,128)(2,1)} %proj_ref.1) | copy-start | bytes 9830404
  67.5 11.8 %collective-permute-start.13 = (bf16[128,1280]{1,0:T(8,128)(2,1)S(1)}, bf16[128,1280]{1,0:T(8,128)(2,1)S(1)}, u32[]{:S(2)}, u32[]{:S(2)}) collective-permute-start(bf16[128,1280]{1,0:T(8,128)(2,1)S(1)} %get-tuple-element.74), channel_id=1, source_target_pairs={{0,2},{1,3},{2,0},{3,1},{4,6},{5,7},{6,4},{7,5},{8,10},{9,11},{10,... | collective-permute-start | bytes 983048 | tf_op jit(solution)/shard_map/ppermute | solution.py:256
  70.9 9.0 %collective-permute-start.16 = (bf16[128,1280]{1,0:T(8,128)(2,1)S(1)}, bf16[128,1280]{1,0:T(8,128)(2,1)S(1)}, u32[]{:S(2)}, u32[]{:S(2)}) collective-permute-start(bf16[128,1280]{1,0:T(8,128)(2,1)S(1)} %finish.5), channel_id=1, source_target_pairs={{0,12},{1,13},{2,14},{3,15},{4,8},{5,9},{6,10},{7,11},{8,4},{9,5},... | collective-permute-start | bytes 983048 | tf_op jit(solution)/shard_map/ppermute | solution.py:256
  73.6 5.7 %collective-permute-start.14 = (bf16[64,1280]{1,0:T(8,128)(2,1)S(1)}, bf16[64,1280]{1,0:T(8,128)(2,1)S(1)}, u32[]{:S(2)}, u32[]{:S(2)}) collective-permute-start(bf16[64,1280]{1,0:T(8,128)(2,1)S(1)} %get-tuple-element.76), channel_id=1, source_target_pairs={{0,2},{1,3},{2,0},{3,1},{4,6},{5,7},{6,4},{7,5},{8,10},{9,11},{10,... | collective-permute-start | bytes 491528 | tf_op jit(solution)/shard_map/ppermute | solution.py:256
  82.9 5.0 %collective-permute-start.17 = (bf16[4,1280]{1,0:T(4,128)(2,1)S(1)}, bf16[4,1280]{1,0:T(4,128)(2,1)S(1)}, u32[]{:S(2)}, u32[]{:S(2)}) collective-permute-start(bf16[4,1280]{1,0:T(4,128)(2,1)S(1)} %get-tuple-element.82.refs_0_), channel_id=1, source_target_pairs={{0,8},{1,9},{2,10},{3,11},{4,12},{5,13},{6,14},{7,15},{8,0},{9,1},... | collective-permute-start | bytes 30728 | tf_op jit(solution)/shard_map/ppermute | solution.py:256
  87.9 3.8 %collective-permute-start.18 = (bf16[8,1280]{1,0:T(8,128)(2,1)S(1)}, bf16[8,1280]{1,0:T(8,128)(2,1)S(1)}, u32[]{:S(2)}, u32[]{:S(2)}) collective-permute-start(bf16[8,1280]{1,0:T(8,128)(2,1)S(1)} %pad_maximum_fusion.2), channel_id=1, source_target_pairs={{0,4},{1,5},{2,6},{3,7},{4,0},{5,1},{6,2},{7,3},{8,12},{9,13},{10,... | collective-permute-start | bytes 61448 | tf_op jit(solution)/shard_map/ppermute | solution.py:256
  91.8 4.2 %collective-permute-start.19 = (bf16[16,1280]{1,0:T(8,128)(2,1)S(1)}, bf16[16,1280]{1,0:T(8,128)(2,1)S(1)}, u32[]{:S(2)}, u32[]{:S(2)}) collective-permute-start(bf16[16,1280]{1,0:T(8,128)(2,1)S(1)} %pad_maximum_fusion.1), channel_id=1, source_target_pairs={{0,2},{1,3},{2,0},{3,1},{4,6},{5,7},{6,4},{7,5},{8,10},{9,11},{10,... | collective-permute-start | bytes 122888 | tf_op jit(solution)/shard_map/ppermute | solution.py:256
  96.0 1.3 %collective-permute-start.20 = (bf16[32,1280]{1,0:T(8,128)(2,1)S(1)}, bf16[32,1280]{1,0:T(8,128)(2,1)S(1)}, u32[]{:S(2)}, u32[]{:S(2)}) collective-permute-start(bf16[32,1280]{1,0:T(8,128)(2,1)S(1)} %pad_maximum_fusion), channel_id=1, source_target_pairs={{0,1},{1,0},{2,3},{3,2},{4,5},{5,4},{6,7},{7,6},{8,9},{9,8},{10,11... | collective-permute-start | bytes 245768 | tf_op jit(solution)/shard_map/ppermute | solution.py:256
